TPU v7x, 32 devices: a whole 2x2x4 slice. The times are simulated.
32 devices in a mesh: dp: 16 (over z, y, x), seq: 2 (over core).
Axes of the slice: x: 2, y: 2, z: 4, core: 2. Of those that a mesh axis runs over, the one named last changes fastest.
Arguments:
- hidden_in: bfloat16 [64, 512, 768], P('dp', 'seq'), may hold values from -6 to 6
- out_grad: bfloat16 [64, 512, 768], P('dp', 'seq')
- seg_lengths: int32 [64, 4], P('dp'), may hold values from 1 to 320, as said below
- attn_master: float32 [4, 768, 768], P(None, 'dp')
- ffn_master: float32 [2, 3072, 768], P(None, 'dp')
- attn_moment: float32 [4, 768, 768], P(None, 'dp')
- ffn_moment: float32 [2, 3072, 768], P(None, 'dp')
- gains: float32 [2, 768], replicated, may hold values from 0.2 to 4
- gain_first: float32 [2, 768], replicated
- gain_second: float32 [2, 768], replicated, as said below
- bias_table: float32 [32, 12], replicated, may hold values from -3 to 3
- bias_first: float32 [32, 12], replicated
- bias_second: float32 [32, 12], replicated, as said below
Outputs:
- hidden_out: bfloat16 [64, 512, 768], P('dp', 'seq')
- hidden_grad: float32 [64, 512, 768], P('dp', 'seq')
- new_attn: float32 [4, 768, 768], P('seq', 'dp')
- new_attn_moment: float32 [4, 768, 768], P(None, 'dp')
- new_ffn: float32 [2, 3072, 768], P('seq', 'dp')
- new_ffn_moment: float32 [2, 3072, 768], P(None, 'dp')
- new_gains: float32 [2, 768], replicated
- new_gain_first: float32 [2, 768], replicated
- new_gain_second: float32 [2, 768], replicated
- new_bias: float32 [32, 12], replicated
- new_bias_first: float32 [32, 12], replicated
- new_bias_second: float32 [32, 12], replicated
Inputs may be any that keep to these rules, and one draw needn't show every extreme that they name: `seg_lengths`: each row has 4 segment lengths of at least 1 whose sum leaves fewer than 64 padding tokens at its end; one segment of each row, at a place drawn from the seed, has exactly 320 tokens. `gain_second`: Positive. `bias_second`: Positive.
All inputs are finite; a program needn't handle non-finite values.
Results may differ from a plain program's by a relative error of at most 0.012.
The roundings to bfloat16 on the way count: a program that leaves them out, or rounds other values in their place, can miss the bound.
Values may be sent and summed in bfloat16 or wider, within the bound.
No kernel may reach another device: no remote copies, remote signals or barrier semaphores. Data moves between devices by JAX's collectives and lax.ppermute only.
A program may use at most 256 MiB of HBM per device.

v0:
```python
import math

import jax
import jax.numpy as jnp
from jax import lax
from jax.sharding import PartitionSpec as P

D = 768
FF = 3072
NS_STEPS = 2
STEP = 10


bucket_edges = (1, 2, 3, 4, 5, 6, 7, 8, 12, 16, 23, 32, 46, 64, 91)
norm_eps = 1e-06
masked_score = -1000000000.0
coeff_a = 3.4445
coeff_b = -4.775
coeff_c = 2.0315
frob_eps = 1e-07
muon_beta = 0.95
muon_rate = 0.6
muon_decay = 0.01
adam_one = 0.9
adam_two = 0.999
adam_rate = 0.3
adam_eps = 1e-08


def exact_dot(left, right, form):
    return jnp.einsum(form, left, right, precision=lax.Precision.HIGHEST)


def bucket_of(query_pos, key_pos):
    offset = key_pos[None, :] - query_pos[:, None]
    distance = jnp.abs(offset)
    bucket = jnp.where(offset > 0, 16, 0).astype(jnp.int32)
    for edge_value in bucket_edges:
        bucket = bucket + (distance >= edge_value).astype(jnp.int32)
    return bucket


def norm_back(scaled_grad, unit, scale):
    return scale * (scaled_grad - unit * jnp.mean(scaled_grad * unit, axis=-1, keepdims=True))


def adamw(param, first_in, second_in, grad):
    first_new = adam_one * first_in + (1.0 - adam_one) * grad
    second_new = adam_two * second_in + (1.0 - adam_two) * grad * grad
    fix_one = 1.0 - adam_one**STEP
    fix_two = 1.0 - adam_two**STEP
    update = first_new / fix_one / (jnp.sqrt(second_new / fix_two) + adam_eps)
    return (param - adam_rate * update, first_new, second_new)


def per_device(
    hidden_in,
    out_grad,
    seg_lengths,
    attn_master,
    ffn_master,
    attn_moment,
    ffn_moment,
    gains,
    gain_first,
    gain_second,
    bias_table,
    bias_first,
    bias_second,
):
    row_len = hidden_in.shape[1] * lax.axis_size("seq")
    heads = bias_table.shape[1]
    seq_index = lax.axis_index("seq")
    attn_w, ffn_w = (
        lax.all_gather(attn_master.astype(jnp.bfloat16), "dp", axis=1, tiled=True),
        lax.all_gather(ffn_master.astype(jnp.bfloat16), "dp", axis=1, tiled=True),
    )
    hidden_rows, cot_rows = (
        lax.all_to_all(hidden_in, "seq", split_axis=0, concat_axis=1, tiled=True),
        lax.all_to_all(out_grad, "seq", split_axis=0, concat_axis=1, tiled=True),
    )
    rows_here = hidden_rows.shape[0]
    seg_rows = lax.dynamic_slice_in_dim(seg_lengths, seq_index * rows_here, rows_here, 0)
    rows_dev, local_len, width = hidden_rows.shape
    head_dim = width // heads
    seg_ends = jnp.cumsum(seg_rows, axis=-1)
    places = jnp.arange(row_len, dtype=jnp.int32)
    seg_full = jnp.sum((places[None, :, None] >= seg_ends[:, None, :]).astype(jnp.int32), axis=-1)
    valid_mask = (seg_full < seg_rows.shape[1]).astype(jnp.float32)
    query_pos = jnp.arange(local_len, dtype=jnp.int32)
    onehot = (
        bucket_of(query_pos, places)[:, :, None] == jnp.arange(bias_table.shape[0], dtype=jnp.int32)
    ).astype(jnp.float32)
    bias_map = exact_dot(onehot, bias_table, "qkb,bh->hqk")
    hidden = hidden_rows.astype(jnp.float32)
    scale_one = lax.rsqrt(jnp.mean(hidden * hidden, axis=-1, keepdims=True) + norm_eps)
    unit_one = hidden * scale_one
    normed = (unit_one * gains[0]).astype(jnp.bfloat16)
    projected = jnp.einsum(
        "rtd,cde->rtce", normed, attn_w[:3], preferred_element_type=jnp.float32
    ).astype(jnp.bfloat16)
    queries = projected[:, :, 0]
    keyval = projected[:, :, 1:]
    block_rows = min(rows_dev, max(1, 512 // local_len))
    blocks = rows_dev // block_rows

    def split_rows(value):
        return value.reshape((blocks, block_rows) + value.shape[1:])

    query_b = split_rows(queries.reshape(rows_dev, local_len, heads, head_dim))
    keyval_b = split_rows(keyval.reshape(rows_dev, row_len, 2, heads, head_dim))
    segq_b = split_rows(seg_full)
    segk_b = split_rows(seg_full)

    def scores_of(query_blk, key_blk, segq, segk):
        raw = (
            jnp.einsum("rqhe,rkhe->rhqk", query_blk, key_blk, preferred_element_type=jnp.float32)
            + bias_map[None]
        )
        same_seg = segq[:, None, :, None] == segk[:, None, None, :]
        return jnp.where(same_seg, raw, masked_score)

    def attend(block_in):
        query_blk, keyval_blk, segq, segk = block_in
        scores = scores_of(query_blk, keyval_blk[:, :, 0], segq, segk)
        row_max = jnp.max(scores, axis=-1, keepdims=True)
        exp_scores = jnp.exp(scores - row_max)
        exp_total = jnp.sum(exp_scores, axis=-1, keepdims=True)
        probs_low = (exp_scores / exp_total).astype(jnp.bfloat16)
        context_blk = jnp.einsum(
            "rhqk,rkhe->rqhe", probs_low, keyval_blk[:, :, 1], preferred_element_type=jnp.float32
        )
        return (context_blk.astype(jnp.bfloat16), (row_max + jnp.log(exp_total))[..., 0])

    context_b, logsum_b = lax.map(attend, (query_b, keyval_b, segq_b, segk_b))
    context = context_b.reshape(rows_dev, local_len, width)
    middle = hidden + jnp.einsum(
        "rtd,de->rte", context, attn_w[3], preferred_element_type=jnp.float32
    )
    scale_two = lax.rsqrt(jnp.mean(middle * middle, axis=-1, keepdims=True) + norm_eps)
    unit_two = middle * scale_two
    normed_two = (unit_two * gains[1]).astype(jnp.bfloat16)
    pre_act = jnp.einsum("rtd,fd->rtf", normed_two, ffn_w[0], preferred_element_type=jnp.float32)
    activation, gelu_back = jax.vjp(jax.nn.gelu, pre_act)
    act_low = activation.astype(jnp.bfloat16)
    output = middle + jnp.einsum(
        "rtf,fd->rtd", act_low, ffn_w[1], preferred_element_type=jnp.float32
    )
    cotangent = cot_rows.astype(jnp.float32) * valid_mask[:, :, None]
    cot_low = cotangent.astype(jnp.bfloat16)
    ffn_down_grad = jnp.einsum("rtf,rtd->fd", act_low, cot_low, preferred_element_type=jnp.float32)
    act_grad = jnp.einsum("rtd,fd->rtf", cot_low, ffn_w[1], preferred_element_type=jnp.float32)
    (pre_grad,) = gelu_back(act_grad)
    pre_low = pre_grad.astype(jnp.bfloat16)
    ffn_up_grad = jnp.einsum("rtf,rtd->fd", pre_low, normed_two, preferred_element_type=jnp.float32)
    normed_two_grad = jnp.einsum(
        "rtf,fd->rtd", pre_low, ffn_w[0], preferred_element_type=jnp.float32
    )
    gain_two_grad = jnp.sum(normed_two_grad * unit_two, axis=(0, 1))
    middle_grad = cotangent + norm_back(normed_two_grad * gains[1], unit_two, scale_two)
    middle_low = middle_grad.astype(jnp.bfloat16)
    out_map_grad = jnp.einsum(
        "rtd,rte->de", context, middle_low, preferred_element_type=jnp.float32
    )
    context_grad = jnp.einsum(
        "rte,de->rtd", middle_low, attn_w[3], preferred_element_type=jnp.float32
    ).astype(jnp.bfloat16)
    context_grad_b = split_rows(context_grad.reshape(rows_dev, local_len, heads, head_dim))

    def attend_back(bias_acc, block_in):
        query_blk, keyval_blk, segq, segk, logsum, grad_blk = block_in
        scores = scores_of(query_blk, keyval_blk[:, :, 0], segq, segk)
        attn_probs = jnp.exp(scores - logsum[..., None])
        probs_grad = jnp.einsum(
            "rqhe,rkhe->rhqk", grad_blk, keyval_blk[:, :, 1], preferred_element_type=jnp.float32
        )
        inner_prod = jnp.sum(attn_probs * probs_grad, axis=-1, keepdims=True)
        score_grad = (attn_probs * (probs_grad - inner_prod)).astype(jnp.bfloat16)
        query_grad = jnp.einsum(
            "rhqk,rkhe->rqhe", score_grad, keyval_blk[:, :, 0], preferred_element_type=jnp.float32
        )
        key_grad = jnp.einsum(
            "rhqk,rqhe->rkhe", score_grad, query_blk, preferred_element_type=jnp.float32
        )
        value_grad = jnp.einsum(
            "rhqk,rqhe->rkhe",
            attn_probs.astype(jnp.bfloat16),
            grad_blk,
            preferred_element_type=jnp.float32,
        )
        bias_acc = bias_acc + jnp.sum(score_grad.astype(jnp.float32), axis=0)
        return (
            bias_acc,
            (query_grad.astype(jnp.bfloat16), jnp.stack([key_grad, value_grad], axis=2)),
        )

    bias_grad_map, (query_grad_b, keyval_grad_b) = lax.scan(
        attend_back,
        jnp.zeros((heads, local_len, row_len), jnp.float32),
        (query_b, keyval_b, segq_b, segk_b, logsum_b, context_grad_b),
    )
    keyval_grad = keyval_grad_b.reshape(rows_dev, row_len, 2, width)
    keyval_local_grad = keyval_grad.astype(jnp.bfloat16)
    query_grad = query_grad_b.reshape(rows_dev, local_len, width)
    proj_grad = jnp.concatenate([query_grad[:, :, None], keyval_local_grad], axis=2)
    qkv_grad = jnp.einsum("rtd,rtce->cde", normed, proj_grad, preferred_element_type=jnp.float32)
    normed_grad = jnp.einsum(
        "rtce,cde->rtd", proj_grad, attn_w[:3], preferred_element_type=jnp.float32
    )
    gain_one_grad = jnp.sum(normed_grad * unit_one, axis=(0, 1))
    hidden_grad = middle_grad + norm_back(normed_grad * gains[0], unit_one, scale_one)
    table_grad = exact_dot(onehot, bias_grad_map, "qkb,hqk->bh")
    out_tokens, grad_tokens = (
        lax.all_to_all(output, "seq", split_axis=1, concat_axis=0, tiled=True),
        lax.all_to_all(hidden_grad, "seq", split_axis=1, concat_axis=0, tiled=True),
    )
    hidden_out = out_tokens.astype(jnp.bfloat16)
    attn_grad = jnp.concatenate([qkv_grad, out_map_grad[None]], axis=0)
    ffn_grad = jnp.stack([ffn_up_grad, ffn_down_grad], axis=0)
    part_attn, part_ffn = (
        lax.psum_scatter(attn_grad, "dp", scatter_dimension=1, tiled=True),
        lax.psum_scatter(ffn_grad, "dp", scatter_dimension=1, tiled=True),
    )
    attn_sum, ffn_sum = lax.psum((part_attn, part_ffn), "seq")
    gain_sum, table_sum = lax.psum(
        (jnp.stack([gain_one_grad, gain_two_grad], axis=0), table_grad), ("dp", "seq")
    )
    attn_mom = muon_beta * attn_moment + attn_sum
    ffn_mom = muon_beta * ffn_moment + ffn_sum
    is_first = seq_index == 0
    pick_attn = jnp.where(is_first, attn_mom[:2], attn_mom[2:])
    pick_ffn = jnp.where(is_first, ffn_mom[0], ffn_mom[1])
    master_attn = jnp.where(is_first, attn_master[:2], attn_master[2:])
    master_ffn = jnp.where(is_first, ffn_master[0], ffn_master[1])

    def gram_sum(ortho_attn, ortho_ffn):
        return lax.psum(
            (
                exact_dot(ortho_attn, ortho_attn, "mrd,mre->mde"),
                exact_dot(ortho_ffn, ortho_ffn, "rd,re->de"),
            ),
            "dp",
        )

    square_attn, square_ffn = lax.psum(
        (jnp.sum(pick_attn * pick_attn, axis=(1, 2)), jnp.sum(pick_ffn * pick_ffn)), "dp"
    )
    ortho_attn = pick_attn / (jnp.sqrt(square_attn) + frob_eps)[:, None, None]
    ortho_ffn = pick_ffn / (jnp.sqrt(square_ffn) + frob_eps)
    gram_attn, gram_ffn = gram_sum(ortho_attn, ortho_ffn)
    for ns_turn in range(NS_STEPS):
        if ns_turn > 0:
            gram_attn, gram_ffn = gram_sum(ortho_attn, ortho_ffn)
        poly_attn = coeff_b * gram_attn + coeff_c * exact_dot(gram_attn, gram_attn, "mde,mef->mdf")
        poly_ffn = coeff_b * gram_ffn + coeff_c * exact_dot(gram_ffn, gram_ffn, "de,ef->df")
        ortho_attn = coeff_a * ortho_attn + exact_dot(ortho_attn, poly_attn, "mrd,mde->mre")
        ortho_ffn = coeff_a * ortho_ffn + exact_dot(ortho_ffn, poly_ffn, "rd,de->re")
    ffn_scale = math.sqrt(max(1.0, FF / D))
    new_attn = master_attn * (1.0 - muon_rate * muon_decay) - muon_rate * ortho_attn
    new_ffn = (master_ffn * (1.0 - muon_rate * muon_decay) - muon_rate * ffn_scale * ortho_ffn)[
        None
    ]
    new_gains, new_gain_first, new_gain_second = adamw(gains, gain_first, gain_second, gain_sum)
    new_bias, new_bias_first, new_bias_second = adamw(
        bias_table, bias_first, bias_second, table_sum
    )
    return (
        hidden_out,
        grad_tokens,
        new_attn,
        attn_mom,
        new_ffn,
        ffn_mom,
        new_gains,
        new_gain_first,
        new_gain_second,
        new_bias,
        new_bias_first,
        new_bias_second,
    )


def solution(mesh):
    in_specs = (
        P("dp", "seq", None),
        P("dp", "seq", None),
        P("dp", None),
        P(None, "dp", None),
        P(None, "dp", None),
        P(None, "dp", None),
        P(None, "dp", None),
        P(),
        P(),
        P(),
        P(),
        P(),
        P(),
    )
    out_specs = (
        P("dp", "seq", None),
        P("dp", "seq", None),
        P("seq", "dp", None),
        P(None, "dp", None),
        P("seq", "dp", None),
        P(None, "dp", None),
        P(),
        P(),
        P(),
        P(),
        P(),
        P(),
    )
    return jax.shard_map(
        per_device, mesh=mesh, in_specs=in_specs, out_specs=out_specs, check_vma=False
    )
```

profile of v0, /device:TPU:0, one launch (start us, length us, event | category | flops | bytes accessed | tf_op | source)
XLA Modules:
  0.0 1560.9 jit_solution(3131559597688292541)
XLA Ops:
  11.3 3.7 all-to-all-start
  29.5 9.7 iota_compare_fusion
  39.2 45.2 %copy.142 = pred[512,512,32]{1,2,0:T(32,128)(4,1)S(1)} copy(pred[512,512,32]{0,2,1:T(32,128)(4,1)} %iota_compare_fusion) | data formatting | bytes 16777216 | tf_op jit(solution)/shard_map/eq | solution.py:92
  84.4 12.2 convolution_bitcast_fusion.1
  96.7 18.1 %copy.146 = f32[12,512,512]{1,2,0:T(8,128)} copy(f32[12,512,512]{2,0,1:T(8,128)} %convolution_bitcast_fusion.1) | data formatting | bytes 25165824 | tf_op jit(solution)/shard_map/while | solution.py:135
  119.7 6.3 convolution_convert_fusion.1
  132.2 24.0 %while.29 = (s32[]{:T(128)}, bf16[2,1,512,12,64]{2,4,3,1,0:T(8,128)(2,1)S(1)}, f32[2,1,12,512]{3,2,1,0:T(8,128)S(1)}, bf16[2,1,512,2,12,64]{2,5,4,3,1,0:T(8,128)...) while((s32[]{:T(128)}, ...), condition=%wide.region_6.7_spmd, body=%wide.region_3.6_spmd.sunk | while | flops 831121408 | bytes 57391216 | solution.py:135
  134.0 5.9 fusion.187
  146.0 6.0 fusion.187
  156.3 5.4 multiply_reduce_fusion.4
  161.7 57.1 %all-gather.5.cloned.1.call-done = bf16[2,3072,768]{2,1,0:T(8,128)(2,1)} async-done(((bf16[2,192,768]{2,1,0:T(8,128)(2,1)}), bf16[2,3072,768]{2,1,0:T(8,128)(2,1)}) %all-gather.5.cloned.1.call-update) | async-done | bytes 9437200 | tf_op jit(solution)/shard_map/all_gather | solution.py:76
  218.9 11.5 fusion.47
  230.3 15.5 fusion.37
  245.8 8.3 multiply_reduce_fusion.1
  265.0 91.7 %while.30 = (s32[]{:T(128)}, f32[12,512,512]{1,2,0:T(8,128)}, bf16[2,1,512,12,64]{2,4,3,1,0:T(8,128)(2,1)}, bf16[2,1,512,2,12,64]{2,5,4,3,1,0:T(8,128)(2,1)}, s3...) while((s32[]{:T(128)}, f32[12,512,512]{1,2,0:T(8,128)}, ...), condition=%wide.region_11.12_spmd.clone, body=%wide.region_9.11_spmd.clone.sunk | while | flops 2054809600 | bytes 200407408 | solution.py:197
  271.0 10.7 multiply_reduce_fusion.9
  281.7 7.7 fusion.198
  289.4 12.8 select_add_fusion.2
  315.3 10.7 multiply_reduce_fusion.9
  326.0 7.7 fusion.198
  333.8 15.6 %select_add_fusion.2 = (f32[12,512,512]{1,2,0:T(8,128)}, bf16[12,512,512]{1,2,0:T(8,128)(2,1)S(1)}) fusion(f32[12,512,512]{1,2,0:T(8,128)} %get-tuple-element.503, pred[]{:T(512)S(6)} %compare.3, f32[12,512,512]{1,2,0:T(8,128)} %get-tuple-element.462, f32[12,512,512]{1,2,0:T(8,128)S(1)} %fusion.196, f32[12,512]{1,0:T(8,128)S(1)} %get-tuple-element.463), kind=kLoop, calls=%fused_computation.17.clone.1 | loop fusion | flops 18874368 | bytes 56647680 | tf_op jit(solution)/shard_map/while/body/eval_jaxpr/add | solution.py:191
  356.7 4.7 copy.159
  362.4 7.1 fusion.55
  369.5 4.3 pad_maximum_fusion.1
  373.8 12.0 copy.164
  387.8 8.0 convolution_bitcast_fusion.3
  395.7 10.5 convolution_bitcast_fusion.2
  406.2 6.6 pad_maximum_fusion
  414.8 250.0 %all-reduce.11.cloned.1.call-done = f32[4,768,768]{2,0,1:T(4,128)} async-done(((f32[4,768,768]{2,0,1:T(4,128)}), f32[4,768,768]{2,0,1:T(4,128)}) %all-reduce.11.cloned.1.call-update) | async-done | bytes 9437200
  666.8 288.2 %reduce-scatter.2.cloned.1.call-done = f32[2,192,768]{2,1,0:T(8,128)} async-done(((f32[2,3072,768]{2,1,0:T(8,128)}), f32[2,192,768]{2,1,0:T(8,128)}) %reduce-scatter.2.cloned.1.call-update) | async-done | bytes 1179664 | tf_op jit(solution)/shard_map/reduce_scatter | solution.py:222
  955.1 22.7 %all-reduce.17.cloned.1.call-done = (f32[4,48,768]{2,1,0:T(8,128)}, f32[2,192,768]{2,1,0:T(8,128)}) async-done(((f32[4,48,768]{2,1,0:T(8,128)}, f32[2,192,768]{2,1,0:T(8,128)}), (f32[4,48,768]{2,1,0:T(8,128)}, f32[2,192,768]{2,1,0:T(8,128)})) %all-reduce.17.cloned.1.call-update) | async-done | bytes 1769488 | tf_op jit(solution)/shard_map/psum | solution.py:224
  982.9 42.6 %all-reduce.2 = (f32[2]{0:T(128)S(1)}, f32[]{:T(128)}) all-reduce(f32[2]{0:T(128)S(1)} %multiply_reduce_fusion.7, f32[]{:T(128)} %get-tuple-element.338), channel_id=1, replica_groups=mesh['dp'=16,'seq'=2] {'dp'}, use_global_device_ids=true, to_apply=%region_16.17 | all-reduce | flops 3 | bytes 24 | tf_op jit(solution)/shard_map/psum | solution.py:245
  1026.2 7.3 fusion.140
  1033.5 4.7 fusion.125
  1038.5 223.2 %all-reduce.15.cloned.1.call-done = (f32[2,768,768]{2,1,0:T(8,128)}, f32[768,768]{1,0:T(8,128)}) async-done(((f32[2,768,768]{2,1,0:T(8,128)}, f32[768,768]{1,0:T(8,128)}), (f32[2,768,768]{2,1,0:T(8,128)}, f32[768,768]{1,0:T(8,128)})) %all-reduce.15.cloned.1.call-update) | async-done | bytes 7077904 | tf_op jit(solution)/shard_map/psum | solution.py:237
  1261.7 8.5 fusion.147
  1277.2 12.5 fusion.144
  1293.1 5.7 fusion.145
  1298.8 11.7 fusion.68
  1312.2 5.4 all_to_all.45
  1319.0 6.5 fusion.50
  1328.7 6.9 all_to_all.46
  1337.7 22.4 %fusion.102 = f32[32,12]{0,1:T(8,128)S(1)} fusion(f32[12,512,512]{1,2,0:T(8,128)S(1)} %bitcast.283, s32[512,512]{0,1:T(8,128)} %convert_add_fusion), kind=kOutput, calls=%fused_computation.138 | convolution fusion | flops 1216348160 | bytes 13633024 | tf_op jit(solution)/shard_map/qkb,hqk->bh/dot_general | solution.py:31
  1360.1 40.3 %all-reduce.1 = (f32[2,768]{1,0:T(2,128)S(1)}, f32[32,12]{0,1:T(8,128)S(1)}) all-reduce(f32[2,768]{1,0:T(2,128)S(1)} %pad_maximum_fusion.7, f32[32,12]{0,1:T(8,128)S(1)} %fusion.102), channel_id=1, replica_groups=mesh['dp'=16,'seq'=2] {'dp','seq'}, use_global_device_ids=true, to_apply=%region_27.28 | all-reduce | flops 1920 | bytes 15360 | tf_op jit(solution)/shard_map/psum | solution.py:225
  1401.7 124.3 %all-reduce.13.cloned.1.call-done = (f32[2,768,768]{2,1,0:T(8,128)}, f32[768,768]{1,0:T(8,128)}) async-done(((f32[2,768,768]{2,1,0:T(8,128)}, f32[768,768]{1,0:T(8,128)}), (f32[2,768,768]{2,1,0:T(8,128)}, f32[768,768]{1,0:T(8,128)})) %all-reduce.13.cloned.1.call-update) | async-done | bytes 7077904 | tf_op jit(solution)/shard_map/psum | solution.py:237
  1525.9 8.5 fusion.149
  1537.5 12.3 fusion.146
  1549.7 4.1 fusion.99
  (244 shorter events, 112.5 us)
Async XLA Ops:
  7.2 7.8 copy-start
  7.2 112.5 %all-gather.3.cloned.1.call-start = ((), (), s32[]{:S(2)}) async-start(), calls=%async_computation.5 | async-start | bytes 5013504 | tf_op jit(solution)/shard_map/all_gather | solution.py:75
  9.1 209.8 %all-gather.5.cloned.1.call-start = ((), (), s32[]{:S(2)}) async-start(), calls=%async_computation.6 | async-start | bytes 10027008 | tf_op jit(solution)/shard_map/all_gather | solution.py:76
  11.3 6.2 all-to-all-start
  17.5 8.3 copy-start.11
  17.5 6.2 all-to-all-start.2
  21.2 643.6 %all-reduce.11.cloned.1.call-start = ((), (), s32[]{:S(2)}) async-start(), calls=%async_computation.8 | async-start | bytes 18874368
  21.6 96.6 %copy-start.39 = (f32[2,2,256]{2,1,0:T(2,128)}, f32[2,2,256]{2,1,0:T(2,128)S(1)}, u32[]{:S(2)}) copy-start(f32[2,2,256]{2,1,0:T(2,128)S(1)} %reshape.374) | copy-start | bytes 12292
  27.5 90.8 %copy-start.7 = (f32[2,2,256,768]{3,2,0,1:T(8,128)}, f32[2,2,256,768]{3,2,0,1:T(8,128)S(1)}, u32[]{:S(2)}) copy-start(f32[2,2,256,768]{3,2,0,1:T(8,128)S(1)} %copy.139) | copy-start | bytes 9437188
  39.2 45.3 %copy-start.43 = (f32[32,12]{0,1:T(8,128)S(1)}, f32[32,12]{0,1:T(8,128)}, u32[]{:S(2)}) copy-start(f32[32,12]{0,1:T(8,128)} %param.27) | copy-start | bytes 4612
  96.7 18.1 %copy-start.45 = (f32[2,768]{1,0:T(2,128)S(1)}, f32[2,768]{1,0:T(2,128)}, u32[]{:S(2)}) copy-start(f32[2,768]{1,0:T(2,128)} %param.24) | copy-start | bytes 18436
  156.3 62.6 %copy-start.47 = (f32[768]{0:T(1024)S(1)}, f32[768]{0:T(1024)}, u32[]{:S(2)}) copy-start(f32[768]{0:T(1024)} %get-tuple-element.284) | copy-start | bytes 9220
  161.7 92.4 %copy-start.49 = (f32[2,512]{1,0:T(2,128)}, f32[2,512]{1,0:T(2,128)S(1)}, u32[]{:S(2)}) copy-start(f32[2,512]{1,0:T(2,128)S(1)} %add_rsqrt_fusion.1) | copy-start | bytes 12292
  218.9 11.5 copy-start.32
  218.9 11.5 copy-start.56
  230.3 15.5 copy-start.16
  245.8 8.3 copy-start.13
  245.8 8.3 copy-start.42
  362.4 7.1 copy-start.30
  362.4 7.1 copy-start.29
  385.9 569.1 %reduce-scatter.2.cloned.1.call-start = ((), (), s32[]{:S(2)}) async-start(), calls=%async_computation.7 | async-start | bytes 20054016 | tf_op jit(solution)/shard_map/reduce_scatter | solution.py:222
  387.7 8.0 copy-start.33
  412.9 564.9 %all-reduce.17.cloned.1.call-start = ((), (), s32[]{:S(2)}) async-start(), calls=%async_computation.11 | async-start | bytes 3538944 | tf_op jit(solution)/shard_map/psum | solution.py:224
  955.1 306.7 %all-reduce.15.cloned.1.call-start = ((), (), s32[]{:S(2)}) async-start(), calls=%async_computation.10 | async-start | bytes 14155776 | tf_op jit(solution)/shard_map/psum | solution.py:237
  1038.3 487.6 %all-reduce.13.cloned.1.call-start = ((), (), s32[]{:S(2)}) async-start(), calls=%async_computation.9 | async-start | bytes 14155776 | tf_op jit(solution)/shard_map/psum | solution.py:237
  1261.7 8.5 copy-start.18
  1261.7 15.4 slice-start.3
  1270.3 6.9 slice-start.4
  1277.2 12.5 copy-start.23
  1310.5 8.4 copy-start.55
  1310.6 8.4 copy-start.31
  1312.2 6.8 copy-start.8
  1312.2 6.8 copy-start.25
  1312.2 6.8 copy-start.38
  1325.5 12.1 slice-start
  1325.5 12.1 slice-start.1
  1328.7 8.9 slice-start.2
  1337.6 62.7 %copy-start.46 = (f32[2,768]{1,0:T(2,128)S(1)}, f32[2,768]{1,0:T(2,128)}, u32[]{:S(2)}) copy-start(f32[2,768]{1,0:T(2,128)} %param.24) | copy-start | bytes 18436
  1337.7 62.7 %copy-start.53 = (f32[2,768]{1,0:T(2,128)S(1)}, f32[2,768]{1,0:T(2,128)}, u32[]{:S(2)}) copy-start(f32[2,768]{1,0:T(2,128)} %param.25) | copy-start | bytes 18436
  1337.7 62.7 %copy-start.54 = (f32[2,768]{1,0:T(2,128)S(1)}, f32[2,768]{1,0:T(2,128)}, u32[]{:S(2)}) copy-start(f32[2,768]{1,0:T(2,128)} %param.26) | copy-start | bytes 18436
  1337.7 63.4 %copy-start.44 = (f32[32,12]{0,1:T(8,128)S(1)}, f32[32,12]{0,1:T(8,128)}, u32[]{:S(2)}) copy-start(f32[32,12]{0,1:T(8,128)} %param.27) | copy-start | bytes 4612
  1337.7 63.4 %copy-start.51 = (f32[32,12]{0,1:T(8,128)S(1)}, f32[32,12]{0,1:T(8,128)}, u32[]{:S(2)}) copy-start(f32[32,12]{0,1:T(8,128)} %param.28) | copy-start | bytes 4612
  1337.7 63.3 %copy-start.52 = (f32[32,12]{0,1:T(8,128)S(1)}, f32[32,12]{0,1:T(8,128)}, u32[]{:S(2)}) copy-start(f32[32,12]{0,1:T(8,128)} %param.29) | copy-start | bytes 4612
  1525.9 8.5 copy-start.10
  1525.9 8.6 copy-start.21
  1525.9 8.6 copy-start.28
  1537.4 12.3 copy-start.34
  1537.5 16.4 %copy-start.1 = (s32[4,4]{1,0:T(4,128)S(1)}, s32[4,4]{1,0:T(4,128)}, u32[]{:S(2)}) copy-start(s32[4,4]{1,0:T(4,128)} %param.19) | copy-start | bytes 196
  (31 other events, 80.0 us)
Sparse Core Ops, SparseCore 0:
  11.3 83.1 all-gather.2
  97.8 121.0 all-gather.4
  386.0 278.7 all-reduce.10
  670.4 284.5 reduce-scatter.1
  957.9 19.8 all-reduce.16
  1038.4 223.2 all-reduce.14
  1298.9 226.9 all-reduce.12
where the time goes:
time: 1570 us; the launch traced here: 1560 us
  waiting for transfers between devices  970 us (62%)
  matrix products  276 us (18%)
  local copies, waits for them, and re-layouts  123 us (8%)
  blocking collectives  95.2 us (6%)
  other arithmetic  72.3 us (5%)
  between operations  16.5 us (1%)
    psum x2, waiting for transfers between devices, gram_sum(): lax.psum((exact_dot(ortho_attn, ortho_attn, 'mrd,mre->mde'), exact_dot(or...  347 us
    reduce_scatter x1, waiting for transfers between devices, per_device(): lax.psum_scatter(ffn_grad, 'dp', scatter_dimension=1, tiled=True)  288 us
    unnamed x8, waiting for transfers between devices  250 us
    dot_general x14, matrix products, exact_dot(): return jnp.einsum(form, left, right, precision=lax.Precision.HIGHEST)  111 us
    all_gather x1, waiting for transfers between devices, per_device(): lax.all_gather(ffn_master.astype(jnp.bfloat16), 'dp', axis=1, tiled=True)  57.1 us
    eq x1, local copies, waits for them, and re-layouts, per_device(): bucket_of(query_pos, places)[:, :, None]  45.2 us
    psum x1, blocking collectives, per_device(): lax.psum((jnp.sum(pick_attn * pick_attn, axis=(1, 2)), jnp.sum(pick_ffn *...  42.6 us
    psum x1, blocking collectives, per_device(): lax.psum((jnp.stack([gain_one_grad, gain_two_grad], axis=0), table_grad),...  40.3 us
  transfers between devices with their start and end apart: 9, of which 8 were waited for; matrix products, arithmetic and copies ran while one was open for 14% of the time, Pallas kernels for 0%

commit v1 on v0

v1 whole, which is shorter than its diff:
```python
import functools
import math

import jax
import jax.numpy as jnp
import numpy as np
from jax import lax
from jax.experimental import pallas as pl
from jax.experimental.pallas import tpu as pltpu
from jax.sharding import PartitionSpec as P

D = 768
FF = 3072
NS_STEPS = 2
STEP = 10
TILE = 128

bucket_edges = (1, 2, 3, 4, 5, 6, 7, 8, 12, 16, 23, 32, 46, 64, 91)
norm_eps = 1e-06
masked_score = -1000000000.0
coeff_a = 3.4445
coeff_b = -4.775
coeff_c = 2.0315
frob_eps = 1e-07
muon_beta = 0.95
muon_rate = 0.6
muon_decay = 0.01
adam_one = 0.9
adam_two = 0.999
adam_rate = 0.3
adam_eps = 1e-08

BF = jnp.bfloat16
F32 = jnp.float32
NT = (((1,), (1,)), ((), ()))
NN = (((1,), (0,)), ((), ()))
TN = (((0,), (0,)), ((), ()))
SMALL = pl.CostEstimate(flops=1000, bytes_accessed=1000, transcendentals=0)


def mm(left, right, dims):
    return lax.dot_general(left, right, dims, preferred_element_type=F32)


def hbm(*values):
    return tuple(pltpu.with_memory_space_constraint(v, pltpu.HBM) for v in values)


def exact_dot(left, right, form):
    return jnp.einsum(form, left, right, precision=lax.Precision.HIGHEST)


def offset_onehot(buckets):
    offset = np.arange(4 * TILE) - (2 * TILE - 1)
    bucket = np.where(offset > 0, 16, 0)
    for edge_value in bucket_edges:
        bucket = bucket + (np.abs(offset) >= edge_value)
    hot = (bucket[:, None] == np.arange(buckets)).astype(np.float32)
    hot[-1] = 0.0
    return hot


def norm_back(scaled_grad, unit, scale):
    return scale * (scaled_grad - unit * jnp.mean(scaled_grad * unit, axis=-1, keepdims=True))


def adamw(param, first_in, second_in, grad):
    first_new = adam_one * first_in + (1.0 - adam_one) * grad
    second_new = adam_two * second_in + (1.0 - adam_two) * grad * grad
    fix_one = 1.0 - adam_one**STEP
    fix_two = 1.0 - adam_two**STEP
    update = first_new / fix_one / (jnp.sqrt(second_new / fix_two) + adam_eps)
    return (param - adam_rate * update, first_new, second_new)


def skew_tile(vector):
    width = vector.shape[1]
    base = pltpu.roll(jnp.broadcast_to(vector, (8, width)), width - (TILE - 1), axis=1)
    row = lax.broadcasted_iota(jnp.int32, (8, width), 0)
    head = base
    for i in range(1, 8):
        head = jnp.where(row == i, pltpu.roll(base, i, axis=1), head)
    pieces = [head] + [pltpu.roll(head, 8 * g, axis=1) for g in range(1, TILE // 8)]
    return jnp.concatenate(pieces, axis=0)


def unskew_sum(tile):
    width = tile.shape[1]
    rows = tile.shape[0]
    while rows > 8:
        half = rows // 2
        tile = tile[:half] + pltpu.roll(tile[half:], width - half, axis=1)
        rows = half
    row = lax.broadcasted_iota(jnp.int32, (8, width), 0)
    total = jnp.where(row == 0, tile, 0.0)
    for i in range(1, 8):
        total = total + jnp.where(row == i, pltpu.roll(tile, width - i, axis=1), 0.0)
    return pltpu.roll(jnp.broadcast_to(jnp.sum(total, axis=0, keepdims=True), (8, width)), TILE - 1, axis=1)[
        0:1
    ]


def bias_column(bias_ref, far, a, first_block, count, blocks):
    columns = []
    for qb in range(first_block, first_block + count):
        pieces = []
        for kb in range(blocks):
            diff = qb - kb
            if diff <= -2:
                pieces.append(far[a][0])
            elif diff >= 2:
                pieces.append(far[a][1])
            else:
                pieces.append(bias_ref[a, :, (diff + 1) * TILE : (diff + 2) * TILE])
        columns.append(jnp.concatenate(pieces, axis=0))
    return jnp.concatenate(columns, axis=1)


def bias_setup(trev_ref, bias_ref):
    far = []
    for a in range(2):
        vector = trev_ref[0, a : a + 1, :]
        bias_ref[a] = skew_tile(vector)
        far.append(
            (
                jnp.broadcast_to(vector[:, 0:1], (TILE, TILE)),
                jnp.broadcast_to(vector[:, 4 * TILE - 2 : 4 * TILE - 1], (TILE, TILE)),
            )
        )
    return far


def attend_kernel(
    rows, length, wide, extra, trev_ref, segk_ref, segq_ref, q_ref, k_ref, v_ref, *refs
):
    ctx_ref, lse_ref, bias_ref = refs[extra:]
    blocks = length // TILE
    lane = lax.broadcasted_iota(jnp.int32, (wide, TILE), 1)
    low_half = lane < TILE // 2
    far = bias_setup(trev_ref, bias_ref)
    for r in range(rows):
        span = slice(r * length, (r + 1) * length)
        keys = k_ref[0, span, :]
        values = v_ref[0, span, :]
        seg_k = segk_ref[r]
        for qt in range(length // wide):
            at = slice(r * length + qt * wide, r * length + (qt + 1) * wide)
            query = q_ref[0, at, :]
            same = seg_k == segq_ref[r, :, qt * wide : (qt + 1) * wide]
            outs = []
            for a in range(2):
                mine = low_half if a == 0 else jnp.logical_not(low_half)
                raw = mm(keys, jnp.where(mine, query, jnp.zeros_like(query)), NT)
                step = wide // TILE
                raw = raw + bias_column(bias_ref, far, a, qt * step, step, blocks)
                scores = jnp.where(same, raw, masked_score)
                row_max = jnp.max(scores, axis=0, keepdims=True)
                exp_scores = jnp.exp(scores - row_max)
                total = jnp.sum(exp_scores, axis=0, keepdims=True)
                probs = (exp_scores * (1.0 / total)).astype(BF)
                outs.append(mm(probs, values, TN))
                lse_ref[0, a : a + 1, at] = row_max + jnp.log(total)
            ctx_ref[at, :] = jnp.where(low_half, outs[0], outs[1]).astype(BF)


def attend(proj, trev, seg_col, seg_row, rows, length, first_pair, after=()):
    tokens = proj.shape[1]
    pairs = proj.shape[2] // TILE
    whole = lambda shape: pl.BlockSpec(shape, lambda p: (0,) * len(shape))
    part = lambda c: pl.BlockSpec((1, tokens, TILE), lambda p: (c, 0, p))
    return pl.pallas_call(
        functools.partial(attend_kernel, rows, length, 2 * TILE, len(after)),
        grid=(pairs,),
        in_specs=[
            pl.BlockSpec((1, 2, 4 * TILE), lambda p: (p + first_pair, 0, 0)),
            whole((rows, length, 1)),
            whole((rows, 1, length)),
            part(0),
            part(1),
            part(2),
        ]
        + [pl.BlockSpec(memory_space=pl.ANY)] * len(after),
        out_specs=[
            pl.BlockSpec((tokens, TILE), lambda p: (0, p)),
            pl.BlockSpec((1, 2, tokens), lambda p: (p, 0, 0)),
        ],
        out_shape=[
            jax.ShapeDtypeStruct((tokens, pairs * TILE), BF),
            jax.ShapeDtypeStruct((pairs, 2, tokens), F32),
        ],
        scratch_shapes=[pltpu.VMEM((2, TILE, 4 * TILE), F32)],
        compiler_params=pltpu.CompilerParams(vmem_limit_bytes=40 << 20),
        cost_estimate=SMALL,
        name="attend",
    )(trev, seg_col, seg_row, proj, proj, proj, *after)


def attend_back_kernel(
    rows,
    length,
    wide,
    extra,
    trev_ref,
    segk_ref,
    segq_ref,
    lse_ref,
    q_ref,
    k_ref,
    v_ref,
    do_ref,
    *refs,
):
    grad_ref, diag_ref, bias_ref, acc_ref = refs[extra:]
    blocks = length // TILE
    lane = lax.broadcasted_iota(jnp.int32, (wide, TILE), 1)
    low_half = lane < TILE // 2
    lane_row = lax.broadcasted_iota(jnp.int32, (1, 4 * TILE), 1)
    far = bias_setup(trev_ref, bias_ref)
    sums = [[jnp.zeros((8, TILE), F32) for _ in range(2)] for _ in range(2)]
    acc_ref[...] = jnp.zeros_like(acc_ref)
    step = wide // TILE
    for r in range(rows):
        span = slice(r * length, (r + 1) * length)
        keys = k_ref[0, span, :]
        values = v_ref[0, span, :]
        seg_k = segk_ref[r]
        key_grad = jnp.zeros((length, TILE), F32)
        value_grad = jnp.zeros((length, TILE), F32)
        for qt in range(length // wide):
            at = slice(r * length + qt * wide, r * length + (qt + 1) * wide)
            query = q_ref[0, at, :]
            do = do_ref[at, :]
            same = seg_k == segq_ref[r, :, qt * wide : (qt + 1) * wide]
            query_grads = []
            for a in range(2):
                mine = low_half if a == 0 else jnp.logical_not(low_half)
                query_a = jnp.where(mine, query, jnp.zeros_like(query))
                do_a = jnp.where(mine, do, jnp.zeros_like(do))
                raw = mm(keys, query_a, NT)
                raw = raw + bias_column(bias_ref, far, a, qt * step, step, blocks)
                scores = jnp.where(same, raw, masked_score)
                probs = jnp.exp(scores - lse_ref[0, a : a + 1, at])
                probs_grad = mm(values, do_a, NT)
                weighted = probs * probs_grad
                inner = jnp.sum(weighted, axis=0, keepdims=True)
                score_grad = (weighted - probs * inner).astype(BF)
                value_grad = value_grad + mm(probs.astype(BF), do_a, NN)
                key_grad = key_grad + mm(score_grad, query_a, NN)
                query_grads.append(mm(score_grad, keys, TN))
                for qs in range(step):
                    for kb in range(blocks):
                        diff = qt * step + qs - kb
                        piece = score_grad[
                            kb * TILE : (kb + 1) * TILE, qs * TILE : (qs + 1) * TILE
                        ].astype(F32)
                        if abs(diff) >= 2:
                            side = 0 if diff < 0 else 1
                            sums[a][side] = sums[a][side] + jnp.sum(
                                piece.reshape(TILE // 8, 8, TILE), axis=0
                            )
                        else:
                            acc_ref[a, :, (diff + 1) * TILE : (diff + 2) * TILE] += piece
            grad_ref[0, at, :] = jnp.where(low_half, query_grads[0], query_grads[1]).astype(BF)
        grad_ref[1, span, :] = key_grad.astype(BF)
        grad_ref[2, span, :] = value_grad.astype(BF)
    for a in range(2):
        near = unskew_sum(acc_ref[a])
        ends = [
            jnp.sum(jnp.sum(sums[a][side], axis=1, keepdims=True), axis=0, keepdims=True)
            for side in range(2)
        ]
        diag_ref[0, a : a + 1, :] = (
            near
            + jnp.where(lane_row == 0, ends[0], 0.0)
            + jnp.where(lane_row == 4 * TILE - 2, ends[1], 0.0)
        )


def attend_back(
    proj, trev, seg_col, seg_row, lse_rows, do, rows, length, pair, member, count, pairs, carried
):
    tokens = proj.shape[1]
    lanes = pairs * TILE
    whole = lambda shape: pl.BlockSpec(shape, lambda p: (0,) * len(shape))
    part = lambda c: pl.BlockSpec((1, tokens, TILE), lambda p: (c, 0, pair + p))
    one = lambda size, which: pl.BlockSpec((1, 2, size), lambda p: (which + p, 0, 0))
    extras = () if carried is None else (carried,)
    return pl.pallas_call(
        functools.partial(attend_back_kernel, rows, length, 2 * TILE, len(extras)),
        grid=(count,),
        in_specs=[
            one(4 * TILE, pair),
            whole((rows, length, 1)),
            whole((rows, 1, length)),
            one(tokens, pair),
            part(0),
            part(1),
            part(2),
            pl.BlockSpec((tokens, TILE), lambda p: (0, pair + p)),
        ]
        + [pl.BlockSpec(memory_space=pl.ANY)] * len(extras),
        out_specs=[
            pl.BlockSpec((3, tokens, TILE), lambda p: (0, 0, member + p)),
            one(4 * TILE, 0),
        ],
        out_shape=[
            jax.ShapeDtypeStruct((3, tokens, lanes), BF),
            jax.ShapeDtypeStruct((count, 2, 4 * TILE), F32),
        ],
        scratch_shapes=[
            pltpu.VMEM((2, TILE, 4 * TILE), F32),
            pltpu.VMEM((2, TILE, 4 * TILE), F32),
        ],
        input_output_aliases={} if carried is None else {8: 0},
        compiler_params=pltpu.CompilerParams(vmem_limit_bytes=48 << 20),
        cost_estimate=SMALL,
        name="attend_back",
    )(trev, seg_col, seg_row, lse_rows, *hbm(proj, proj, proj, do), *extras)


def ffn_kernel(extra, first_ref, normed_ref, cot_ref, w_ref, *refs):
    y_ref, dn_ref, keep_ref, send_ref = refs[extra:]
    step = pl.program_id(0)
    width = normed_ref.shape[1]

    @pl.when(step == 0)
    def _():
        y_ref[...] = jnp.zeros_like(y_ref)
        dn_ref[...] = jnp.zeros_like(dn_ref)

    w_in = w_ref[0].reshape(-1, width)
    w_out = w_ref[1].reshape(-1, width)
    normed = normed_ref[...]
    cot = cot_ref[...]
    pre = mm(w_in, normed, NT)
    act_grad = mm(w_out, cot, NT)
    square = pre * pre
    root = math.sqrt(2.0 / math.pi)
    tanh = jnp.tanh(pre * (root + (root * 0.044715) * square))
    half = 0.5 * (1.0 + tanh)
    act = (pre * half).astype(BF)
    slope = half + (0.5 * pre) * (1.0 - tanh * tanh) * (root + (3.0 * root * 0.044715) * square)
    pre_low = (act_grad * slope).astype(BF)
    y_ref[...] += mm(act, w_out, TN)
    dn_ref[...] += mm(pre_low, w_in, TN)
    down = mm(act, cot, NN)
    up = mm(pre_low, normed, NN)

    @pl.when(first_ref[0] == 1)
    def _():
        keep_ref[...] = up
        send_ref[...] = down.astype(BF)

    @pl.when(first_ref[0] == 0)
    def _():
        keep_ref[...] = down
        send_ref[...] = up.astype(BF)


def ffn(first, normed, cot, weights, places, part, after=()):
    tokens, width = normed.shape
    units = weights.shape[1] // 2
    half = units // places
    view = weights.reshape(2, places, 2, half, width)
    if half % 16 == 0:
        blocks = 384 // half
        chunk = blocks * half
        w_spec = pl.BlockSpec((2, blocks, None, half, width), lambda s: (0, s, part, 0, 0))
    else:
        chunk = 512
        view = view[:, :, part].reshape(2, units, width)
        w_spec = pl.BlockSpec((2, chunk, width), lambda s: (0, s, 0))
    whole = lambda shape, mode=None: pl.BlockSpec(
        shape, lambda s: (0,) * len(shape), pipeline_mode=mode
    )
    block = pl.BlockSpec((chunk, width), lambda s: (s, 0))
    once = pl.Buffered(1)
    return pl.pallas_call(
        functools.partial(ffn_kernel, len(after)),
        grid=(units // chunk,),
        in_specs=[
            pl.BlockSpec(memory_space=pltpu.SMEM),
            whole((tokens, width), once),
            whole((tokens, width), once),
            w_spec,
        ]
        + [pl.BlockSpec(memory_space=pl.ANY)] * len(after),
        out_specs=[whole((tokens, width)), whole((tokens, width)), block, block],
        out_shape=[
            jax.ShapeDtypeStruct((tokens, width), F32),
            jax.ShapeDtypeStruct((tokens, width), F32),
            jax.ShapeDtypeStruct((units, width), F32),
            jax.ShapeDtypeStruct((units, width), BF),
        ],
        compiler_params=pltpu.CompilerParams(vmem_limit_bytes=52 << 20),
        cost_estimate=SMALL,
        name="ffn",
    )(first, normed, cot, view, *after)


def token_maps(length):
    block = lambda r, far, core: 2 * r + jnp.bitwise_xor(core[0], far)
    return lambda r, far, core: (block(r, far, core), 0), lambda r, far, core: (r, 0, 0)


def middle_kernel(core_ref, middle_ref, cot_ref, gain_ref, out_w_ref, y0_ref, y1_ref, dn0_ref, dn1_ref, *refs):
    ctx_ref, own_ref, send_ref, grad_ref, ctx_grad_ref, map_grad_ref, gain_grad_ref = refs
    y_refs, dn_refs, ctx_refs = (y0_ref, y1_ref), (dn0_ref, dn1_ref), (ctx_ref,)
    middle = middle_ref[...]
    out = (middle + (y_refs[0][...] + y_refs[1][...])).astype(BF)

    @pl.when(pl.program_id(1) == 0)
    def _():
        own_ref[0] = out

    @pl.when(pl.program_id(1) == 1)
    def _():
        send_ref[0] = out

    dn = dn_refs[0][...] + dn_refs[1][...]
    scale = lax.rsqrt(jnp.mean(middle * middle, axis=1, keepdims=True) + norm_eps)
    unit = middle * scale
    scaled = dn * gain_ref[...]
    inner = jnp.mean(scaled * unit, axis=1, keepdims=True)
    grad = cot_ref[...].astype(F32) + scale * (scaled - unit * inner)
    grad_ref[...] = grad
    low = grad.astype(BF)
    ctx_grad_ref[...] = mm(low, out_w_ref[...], NT).astype(BF)
    map_grad = mm(ctx_refs[0][...], low, TN)
    gain_grad = jnp.sum((dn * unit).reshape(-1, 8, dn.shape[1]), axis=0)
    fresh = pl.program_id(0) + pl.program_id(1) == 0

    @pl.when(fresh)
    def _():
        map_grad_ref[...] = map_grad
        gain_grad_ref[...] = gain_grad

    @pl.when(jnp.logical_not(fresh))
    def _():
        map_grad_ref[...] += map_grad
        gain_grad_ref[...] += gain_grad


def middle_back(core, middle, cot, gain, out_w, y_parts, dn_parts, context, rows):
    tokens, width = middle.shape
    chunk = tokens // rows // 2
    here, row = token_maps(chunk)
    block = pl.BlockSpec((chunk, width), here)
    whole = lambda shape: pl.BlockSpec(shape, lambda r, far, core: (0,) * len(shape))
    half = pl.BlockSpec((1, chunk, width), row)
    return pl.pallas_call(
        middle_kernel,
        grid_spec=pltpu.PrefetchScalarGridSpec(
            num_scalar_prefetch=1,
            grid=(rows, 2),
            in_specs=[block, block, whole((1, width)), whole((width, width))] + [block] * 5,
            out_specs=[half, half, block, block, whole((width, width)), whole((8, width))],
        ),
        out_shape=[
            jax.ShapeDtypeStruct((rows, chunk, width), BF),
            jax.ShapeDtypeStruct((rows, chunk, width), BF),
            jax.ShapeDtypeStruct((tokens, width), F32),
            jax.ShapeDtypeStruct((tokens, width), BF),
            jax.ShapeDtypeStruct((width, width), F32),
            jax.ShapeDtypeStruct((8, width), F32),
        ],
        compiler_params=pltpu.CompilerParams(vmem_limit_bytes=40 << 20),
        cost_estimate=SMALL,
        name="middle_back",
    )(core, *hbm(middle, cot), gain, *hbm(out_w, *y_parts, *dn_parts, context))


def project_kernel(core_ref, normed_ref, own_ref, other_ref, out_ref):
    def each(w_ref):
        for c in range(3):
            out_ref[c] = mm(normed_ref[...], w_ref[c], NN).astype(BF)

    @pl.when(pl.program_id(0) == 0)
    def _():
        each(own_ref)

    @pl.when(pl.program_id(0) == 1)
    def _():
        each(other_ref)


def project(core, normed, own, other):
    tokens, width = normed.shape
    strip = own.shape[2]
    half = pl.BlockSpec((3, width, strip), lambda far, core: (0, 0, 0))
    return pl.pallas_call(
        project_kernel,
        grid_spec=pltpu.PrefetchScalarGridSpec(
            num_scalar_prefetch=1,
            grid=(2,),
            in_specs=[pl.BlockSpec((tokens, width), lambda far, core: (0, 0)), half, half],
            out_specs=pl.BlockSpec(
                (3, tokens, strip), lambda far, core: (0, 0, jnp.bitwise_xor(core[0], far))
            ),
        ),
        out_shape=jax.ShapeDtypeStruct((3, tokens, 2 * strip), BF),
        compiler_params=pltpu.CompilerParams(vmem_limit_bytes=40 << 20),
        cost_estimate=SMALL,
        name="project",
    )(core, normed, own, other)


def entry_kernel(core_ref, hidden_ref, grad_ref, gain_ref, w_own_ref, w_other_ref, *refs):
    grad_refs, (own_ref, send_ref, gain_grad_ref) = refs[:-3], refs[-3:]
    strip = w_own_ref.shape[2]

    def back(low, high):
        total = 0.0
        for c in range(3):
            grads = jnp.concatenate([ref[c] for ref in grad_refs], axis=1)
            total = total + mm(grads[:, :strip], low[c], NT) + mm(grads[:, strip:], high[c], NT)
        hidden = hidden_ref[...].astype(F32)
        scale = lax.rsqrt(jnp.mean(hidden * hidden, axis=1, keepdims=True) + norm_eps)
        unit = hidden * scale
        scaled = total * gain_ref[...]
        inner = jnp.mean(scaled * unit, axis=1, keepdims=True)
        result = grad_ref[...] + scale * (scaled - unit * inner)
        gain_grad = jnp.sum((total * unit).reshape(-1, 8, total.shape[1]), axis=0)
        far = pl.program_id(1)
        fresh = pl.program_id(0) + far == 0

        @pl.when(far == 0)
        def _():
            own_ref[0] = result

        @pl.when(far == 1)
        def _():
            send_ref[0] = result

        @pl.when(fresh)
        def _():
            gain_grad_ref[...] = gain_grad

        @pl.when(jnp.logical_not(fresh))
        def _():
            gain_grad_ref[...] += gain_grad

    @pl.when(core_ref[0] == 0)
    def _():
        back(w_own_ref, w_other_ref)

    @pl.when(core_ref[0] == 1)
    def _():
        back(w_other_ref, w_own_ref)


def entry_back(core, hidden, middle_grad, gain, own, other, grads, rows):
    tokens, width = hidden.shape
    chunk = tokens // rows // 2
    here, row = token_maps(chunk)
    block = pl.BlockSpec((chunk, width), here)
    whole = lambda shape: pl.BlockSpec(shape, lambda r, far, core: (0,) * len(shape))
    half = pl.BlockSpec((1, chunk, width), row)
    part = lambda lanes: pl.BlockSpec((3, chunk, lanes), lambda r, far, core: (0,) + here(r, far, core))
    return pl.pallas_call(
        entry_kernel,
        grid_spec=pltpu.PrefetchScalarGridSpec(
            num_scalar_prefetch=1,
            grid=(rows, 2),
            in_specs=[block, block, whole((1, width))]
            + [whole((3,) + own.shape[1:])] * 2
            + [part(v.shape[2]) for v in grads],
            out_specs=[half, half, whole((8, width))],
        ),
        out_shape=[
            jax.ShapeDtypeStruct((rows, chunk, width), F32),
            jax.ShapeDtypeStruct((rows, chunk, width), F32),
            jax.ShapeDtypeStruct((8, width), F32),
        ],
        compiler_params=pltpu.CompilerParams(vmem_limit_bytes=40 << 20),
        cost_estimate=SMALL,
        name="entry_back",
    )(core, *hbm(hidden, middle_grad), gain, *hbm(own, other, *grads))


def maps_kernel(first_ref, normed_ref, grads_ref, map_ref, *refs):
    keep_ref, send_ref = refs[-2:]
    normed = normed_ref[...]
    one, two, three = (mm(normed, grads_ref[c], TN) for c in range(3))
    four = map_ref[...]

    @pl.when(first_ref[0] == 1)
    def _():
        keep_ref[0], keep_ref[1] = one, two
        send_ref[0], send_ref[1] = three.astype(BF), four.astype(BF)

    @pl.when(first_ref[0] == 0)
    def _():
        keep_ref[0], keep_ref[1] = three, four
        send_ref[0], send_ref[1] = one.astype(BF), two.astype(BF)


def maps_grad(first, normed, grads, map_grad, start, after=()):
    tokens, width = normed.shape
    lanes = grads.shape[2]
    chunk = width // 3
    out = pl.BlockSpec((2, chunk, lanes), lambda s: (0, s, 0))
    return pl.pallas_call(
        maps_kernel,
        grid=(width // chunk,),
        in_specs=[
            pl.BlockSpec(memory_space=pltpu.SMEM),
            pl.BlockSpec((tokens, chunk), lambda s: (0, s)),
            pl.BlockSpec((3, tokens, lanes), lambda s: (0, 0, 0)),
            pl.BlockSpec((chunk, lanes), lambda s: (s, start // lanes)),
        ]
        + [pl.BlockSpec(memory_space=pl.ANY)] * len(after),
        out_specs=[out, out],
        out_shape=[
            jax.ShapeDtypeStruct((2, width, lanes), F32),
            jax.ShapeDtypeStruct((2, width, lanes), BF),
        ],
        compiler_params=pltpu.CompilerParams(vmem_limit_bytes=32 << 20),
        cost_estimate=SMALL,
        name="maps_grad",
    )(first, normed, grads, map_grad, *after)


FOLD = 2


def fold_kernel(order_ref, *refs):
    keep_out, send_out = refs[-2:]
    for j in range(FOLD):
        keep_ref, send_ref, got_keep_ref, got_send_ref = refs[4 * j : 4 * j + 4]
        keep_out[:, j : j + 1] = keep_ref[...] + got_keep_ref[...].astype(F32)
        send_out[:, j : j + 1] = (send_ref[...] + got_send_ref[...].astype(F32)).astype(BF)


def fold(value, got, order):
    many, count, rows, width = value.shape

    def at(which, j):
        return pl.BlockSpec(
            (many, 1, rows, width), lambda s, order: (0, order[which, FOLD * s + j], 0, 0)
        )

    out = pl.BlockSpec((many, FOLD, rows, width), lambda s, order: (0, s, 0, 0))
    shape = (many, count // 2, rows, width)
    return pl.pallas_call(
        fold_kernel,
        grid_spec=pltpu.PrefetchScalarGridSpec(
            num_scalar_prefetch=1,
            grid=(count // 2 // FOLD,),
            in_specs=[at(which, j) for j in range(FOLD) for which in (0, 1, 0, 1)],
            out_specs=[out, out],
        ),
        out_shape=[jax.ShapeDtypeStruct(shape, F32), jax.ShapeDtypeStruct(shape, BF)],
        compiler_params=pltpu.CompilerParams(vmem_limit_bytes=24 << 20),
        cost_estimate=SMALL,
        name="fold",
    )(order, *([value, value, got, got] * FOLD))


class Links:
    def __init__(self, clock):
        self.clock = clock
        self.size = lax.axis_size("dp")
        self.bits = self.size.bit_length() - 1
        self.place = lax.axis_index("dp")
        self.core = lax.axis_index("seq")
        self.first = self.core == 0

    def bit(self, number):
        return lax.rem(lax.div(self.place, 1 << number), 2)

    def turn_bit(self, turn):
        if turn > 1:
            return self.bit(turn)
        return jnp.where(self.first, self.bit(turn), self.bit(1 - turn))

    def swap_seq(self, value):
        return lax.ppermute(value, "seq", [(0, 1), (1, 0)])

    def swap_dp(self, value, turn):
        numbers = (turn, 1 - turn if turn <= 1 else turn)
        pairs = [
            (2 * i + c, 2 * (i ^ (1 << numbers[c])) + c) for i in range(self.size) for c in range(2)
        ]
        return lax.ppermute(value, ("dp", "seq"), pairs)

    def half_places(self):
        quads = np.arange(self.size // 4, dtype=np.int32)[:, None] * 4
        near = np.arange(2, dtype=np.int32)[None, :]
        bit = self.turn_bit(0)

        def places(wanted):
            return jnp.where(
                self.first, quads + near * 2 + wanted, quads + near + wanted * 2
            ).reshape(-1)

        return jnp.stack([places(bit), places(1 - bit)])


    def scatter_first(self, value, got):
        buf, send = fold(value, got, self.clock.after(self.places))
        came = yield send, functools.partial(self.swap_dp, turn=0)
        return buf + came.astype(F32)

    def scatter_rest(self, buf):
        many, _, rows, width = buf.shape
        for turn in range(1, self.bits):
            bit = self.turn_bit(turn)
            view = buf.reshape(many, -1, 2, rows, width)
            cut = lambda b: lax.dynamic_index_in_dim(view, b, 2, keepdims=False)
            send, buf = cut(1 - bit).astype(BF), cut(bit)
            came = yield send, functools.partial(self.swap_dp, turn=turn)
            buf = buf + came.astype(F32)
        return buf

    def scatter(self, value, got):
        buf = yield from self.scatter_first(value, got)
        return (yield from self.scatter_rest(buf))

    def sum_far(self, value):
        for turn in range(2, self.bits):
            low = value.astype(BF)
            came = yield low, functools.partial(self.swap_dp, turn=turn)
            value = low.astype(F32) + came.astype(F32)
        return value

    def order(self, bit, same, other, axis):
        return jnp.where(
            bit == 0, jnp.stack([same, other], axis=axis), jnp.stack([other, same], axis=axis)
        )

    def gather_near(self, buf, at):
        came = yield buf, functools.partial(self.swap_dp, turn=1)
        buf = self.order(self.turn_bit(1), buf, came, at)
        came = yield buf, functools.partial(self.swap_dp, turn=0)
        return jnp.where(
            self.first,
            self.order(self.bit(0), buf, came, at + 1),
            self.order(self.bit(1), buf, came, at),
        )

    def gather(self, value, axis):
        buf, at = value, axis
        for turn in range(self.bits - 1, 1, -1):
            came = yield buf, functools.partial(self.swap_dp, turn=turn)
            buf = self.order(self.bit(turn), buf, came, at)
            at += 1
        buf = yield from self.gather_near(buf, at)
        shape = value.shape
        return buf.reshape(shape[:axis] + (shape[axis] * self.size,) + shape[axis + 1 :])

    def sum_blocks(self, value):
        rows, width = value.shape
        view = value.reshape(2, 2, rows // 4, width)
        cut = lambda b: jnp.where(
            self.first,
            lax.dynamic_index_in_dim(view, b, 1, keepdims=False),
            lax.dynamic_index_in_dim(view, b, 0, keepdims=False),
        )
        bit = self.turn_bit(0)
        came = yield cut(1 - bit).astype(BF), functools.partial(self.swap_dp, turn=0)
        buf = cut(bit) + came.astype(F32)
        bit = self.turn_bit(1)
        half = lambda b: lax.dynamic_index_in_dim(buf, b, 0, keepdims=False)
        came = yield half(1 - bit).astype(BF), functools.partial(self.swap_dp, turn=1)
        buf = yield from self.sum_far(half(bit) + came.astype(F32))
        buf = yield from self.gather_near(buf.astype(BF), 0)
        return buf.reshape(rows, width)

    def all_sum(self, value):
        for turn in range(self.bits):
            came = yield value, functools.partial(self.swap_dp, turn=turn)
            value = value + came
        came = yield value, self.swap_seq
        return value + came

    def by_core(self, own, other, axis):
        return jnp.where(
            self.first,
            jnp.concatenate([own, other], axis=axis),
            jnp.concatenate([other, own], axis=axis),
        )


def tie(value, others):
    return lax.optimization_barrier((value, *others))[0]


class Order:
    def __init__(self):
        self.last = ()

    def after(self, value):
        return tie(value, self.last) if self.last else value

    def done(self, *values):
        self.last = values


class Chain:
    def __init__(self, order, steps):
        self.clock, self.steps, self.result = order, steps, None
        self.launch(*next(steps))

    def launch(self, send, how, free=False):
        self.flight, self.free = how(send), free
        self.clock.done(send)

    def step(self, count=1):
        for _ in range(count):
            if self.steps is None:
                return
            try:
                came = self.flight if self.free else self.clock.after(self.flight)
                self.launch(*self.steps.send(came))
            except StopIteration as end:
                self.result, self.steps = end.value, None
                self.clock.done(*jax.tree.leaves(self.result))

    def finish(self):
        while self.steps is not None:
            self.step()
        return self.result


def pack_gram(gram):
    count = gram.shape[0] // TILE
    row = lambda i: gram[i * TILE : (i + 1) * TILE, i * TILE :]
    return jnp.concatenate(
        [jnp.concatenate([row(i), row(count - 1 - i)], axis=1) for i in range(count // 2)], axis=0
    )


def unpack_gram(packed):
    count = 2 * packed.shape[0] // TILE
    blocks = {}
    for i in range(count // 2):
        strip = packed[i * TILE : (i + 1) * TILE]
        for j in range(i, count):
            blocks[i, j] = strip[:, (j - i) * TILE : (j - i + 1) * TILE]
        low = count - 1 - i
        for j in range(low, count):
            blocks[low, j] = strip[:, (count - i + j - low) * TILE : (count - i + j - low + 1) * TILE]
    rows = []
    for i in range(count):
        rows.append(
            jnp.concatenate([blocks[i, j] if j >= i else blocks[j, i].T for j in range(count)], axis=1)
        )
    return jnp.concatenate(rows, axis=0)


def muon_kernel(parts, gathered, scaling, *refs):
    sources, (mom_ref, master_ref, out_ref) = refs[:parts], refs[parts:]
    whole = jnp.concatenate([ref[0] for ref in sources], axis=1) if parts > 1 else sources[0][0]
    gram = mm(whole, whole, TN) if gathered else unpack_gram(whole.astype(F32))
    width = gram.shape[1]
    row = lax.broadcasted_iota(jnp.int32, (width, width), 0)
    column = lax.broadcasted_iota(jnp.int32, (width, width), 1)
    trace = jnp.sum(
        jnp.sum(jnp.where(row == column, gram, 0.0), axis=0, keepdims=True), axis=1, keepdims=True
    )
    scale = 1.0 / (jnp.sqrt(trace) + frob_eps)
    unit = gram * (scale * scale)
    unit_low = unit.astype(BF)
    rest_one = (coeff_b * unit + coeff_c * mm(unit_low, unit_low, NN)).astype(BF)
    cross = mm(rest_one, unit_low, NN)
    second = (
        (coeff_a * coeff_a) * unit
        + (2.0 * coeff_a) * cross
        + mm(rest_one, cross.astype(BF), NN)
    )
    second_low = second.astype(BF)
    rest_two = (coeff_b * second + coeff_c * mm(second_low, second_low, NN)).astype(BF)
    ortho = mom_ref[0] * scale
    ortho = coeff_a * ortho + mm(ortho.astype(BF), rest_one, NN)
    ortho = coeff_a * ortho + mm(ortho.astype(BF), rest_two, NN)
    out_ref[0] = master_ref[0] * (1.0 - muon_rate * muon_decay) - (muon_rate * scaling) * ortho


def gram_kernel(mom_ref, out_ref):
    low = mom_ref[...].astype(BF)
    out_ref[...] = pack_gram(mm(low, low, TN))


def packed_gram(mom):
    width = mom.shape[1]
    return pl.pallas_call(
        gram_kernel,
        out_shape=jax.ShapeDtypeStruct((width // 2, width + TILE), F32),
        compiler_params=pltpu.CompilerParams(vmem_limit_bytes=24 << 20),
        cost_estimate=SMALL,
        name="gram",
    )(mom)


def muon(sources, gathered, mom, master, scaling):
    count, rows, width = mom.shape
    one = lambda shape: pl.BlockSpec((1,) + shape, lambda m: (m, 0, 0))
    return pl.pallas_call(
        functools.partial(muon_kernel, len(sources), gathered, scaling),
        grid=(count,),
        in_specs=[one(v.shape[1:]) for v in sources] + [one((rows, width)), one((rows, width))],
        out_specs=one((rows, width)),
        out_shape=jax.ShapeDtypeStruct(mom.shape, F32),
        compiler_params=pltpu.CompilerParams(vmem_limit_bytes=48 << 20),
        cost_estimate=SMALL,
        name="muon",
    )(*sources, mom, master)


def per_device(
    hidden_in,
    out_grad,
    seg_lengths,
    attn_master,
    ffn_master,
    attn_moment,
    ffn_moment,
    gains,
    gain_first,
    gain_second,
    bias_table,
    bias_first,
    bias_second,
):
    clock = Order()
    links = Links(clock)
    row_len = hidden_in.shape[1] * lax.axis_size("seq")
    heads = bias_table.shape[1]
    core = links.core
    first = links.first
    flag = first.astype(jnp.int32).reshape(1)
    core_at = core.astype(jnp.int32).reshape(1)
    width = attn_master.shape[2]
    pairs = heads // 2
    strip = width // 2
    half = ffn_master.shape[1] // 2
    size = links.size

    def pick(value, count):
        return lax.dynamic_slice_in_dim(value, core * count, count, 0)

    ffn_own = lax.dynamic_slice_in_dim(ffn_master, core * half, half, axis=1).astype(BF)
    ffn_w = lax.all_gather(ffn_own, ("dp", "seq"), axis=1, tiled=True)

    def attn_weights(shard):
        own = yield from links.gather(shard, 1)
        other = yield own, links.swap_seq
        return own, other

    weights = Chain(
        clock,
        attn_weights(
            lax.dynamic_slice_in_dim(attn_master, core * strip, strip, axis=2).astype(BF)
        ),
    )

    def row_halves(value):
        view = value.reshape((2, value.shape[0] // 2) + value.shape[1:])
        own, send = (lax.dynamic_index_in_dim(view, c, 0, keepdims=False) for c in (core, 1 - core))
        return own, send

    hidden_own, hidden_send = row_halves(hidden_in)
    cot_own, cot_send = row_halves(out_grad)
    hidden_other = links.swap_seq(hidden_send)
    cot_other = links.swap_seq(cot_send)
    clock.done(hidden_send, cot_send)
    weights.step()

    rows = hidden_own.shape[0]
    tokens = rows * row_len
    hidden_low = links.by_core(hidden_own, clock.after(hidden_other), 1).reshape(tokens, width)
    hidden = hidden_low.astype(F32)
    scale_one = lax.rsqrt(jnp.mean(hidden * hidden, axis=-1, keepdims=True) + norm_eps)
    normed = (hidden * scale_one * gains[0]).astype(BF)
    clock.done(normed)
    weights.step()

    seg_rows = lax.dynamic_slice_in_dim(seg_lengths, core * rows, rows, 0)
    seg_ends = jnp.cumsum(seg_rows, axis=-1)
    places = jnp.arange(row_len, dtype=jnp.int32)
    seg_full = jnp.sum((places[None, :, None] >= seg_ends[:, None, :]).astype(jnp.int32), axis=-1)
    valid = (seg_full < seg_rows.shape[1]).reshape(tokens, 1)
    seg_col = seg_full.reshape(rows, row_len, 1)
    seg_row = seg_full.reshape(rows, 1, row_len)
    cot_rows = links.by_core(cot_own, clock.after(cot_other), 1).reshape(tokens, width)
    cotangent = jnp.where(valid, cot_rows, jnp.zeros((), BF))
    onehot = offset_onehot(bias_table.shape[0])
    onehot_rev = np.concatenate([onehot[-2::-1], onehot[-1:]], axis=0)
    trev = exact_dot(onehot_rev, bias_table, "mb,bh->hm").reshape(heads // 2, 2, 4 * TILE)
    links.places = links.half_places()
    clock.done(cotangent, seg_col, seg_row, trev, links.places)
    weights.step()

    moment_attn = pick(attn_moment, 2)
    w_own, w_other = weights.finish()
    proj = project(core_at, normed, w_own, w_other)
    out_w = links.by_core(w_own[3], w_other[3], 1)
    context, lse = attend(proj, trev, seg_col, seg_row, rows, row_len, 0)

    middle = hidden + mm(context, out_w, NN)
    scale_two = lax.rsqrt(jnp.mean(middle * middle, axis=-1, keepdims=True) + norm_eps)
    normed_two = (middle * scale_two * gains[1]).astype(BF)

    def ffn_first(keep, send):
        view = (1, size, half, width)
        came = yield send, links.swap_seq, True
        return (yield from links.scatter_first(keep.reshape(view), came.reshape(view)))

    def ffn_rest(first_part, second_part):
        buf = jnp.concatenate([first_part, second_part], axis=2)
        total = yield from links.scatter_rest(buf)
        return total.reshape(1, 2 * half, width)

    y_parts, dn_parts, sums = [], [], []
    clock.done(normed_two)
    for p in range(2):
        y, dn, keep, send = ffn(clock.after(flag), normed_two, cotangent, ffn_w, size, p)
        y_parts.append(y)
        dn_parts.append(dn)
        sums.append(Chain(clock, ffn_first(keep, send)))
    one, two = sums
    one.step()
    out_own, out_send, middle_grad, context_grad, out_map_grad, gain_two_part = middle_back(
        clock.after(core_at), middle, cotangent, gains[1:2], out_w, y_parts, dn_parts, context, rows
    )
    clock.done(gain_two_part)

    done_grads, diag = [], []
    near = [0, 0]
    sizes = (pairs - pairs // 3, pairs // 3)

    def back(group, grads, count=2):
        start, member = sum(sizes[:group]), near[group]
        near[group] += count
        grads, diag_m = attend_back(
            proj,
            trev,
            seg_col,
            clock.after(seg_row),
            lse,
            context_grad,
            rows,
            row_len,
            start + member,
            member,
            count,
            sizes[group],
            grads,
        )
        diag.append(diag_m)
        clock.done(diag_m)
        return grads

    def maps(group, grads):
        done_grads.append(grads)
        keep, send = maps_grad(
            clock.after(flag), normed, grads, out_map_grad, sum(sizes[:group]) * TILE
        )
        clock.done(send)
        return keep, send

    def attn_first(group, keep, send):
        view = (2, size, width // size, sizes[group] * TILE)
        came = yield send, links.swap_seq, True
        return (yield from links.scatter_first(keep.reshape(view), came.reshape(view)))

    def attn_rest(first_group, second_group):
        buf = jnp.concatenate([first_group, second_group], axis=3)
        total = yield from links.scatter_rest(buf)
        grad = total.reshape(2, width // size, width)
        mom = muon_beta * moment_attn + grad
        whole = yield from links.gather(mom.astype(BF), 1)
        return grad, mom, whole

    two.step()
    grads = back(0, None)
    grads = back(0, grads)
    first_part, second_part = one.finish(), two.finish()
    units = Chain(clock, ffn_rest(first_part, second_part))
    three = Chain(clock, attn_first(0, *maps(0, grads)))
    grads = back(1, None)
    three.step()
    four = Chain(clock, attn_first(1, *maps(1, grads)))
    units.step()
    four.step()
    grad_own, grad_send, gain_one_part = entry_back(
        clock.after(core_at), hidden_low, middle_grad, gains[0:1], w_own, w_other, done_grads, rows
    )
    clock.done(gain_one_part)
    first_group, second_group = three.finish(), four.finish()
    maps_sum = Chain(clock, attn_rest(first_group, second_group))
    units.step()
    out_other = links.swap_seq(clock.after(out_send))
    diag = jnp.concatenate(diag, axis=0).reshape(heads, 4 * TILE)
    table_grad = exact_dot(onehot_rev, diag, "mb,hm->bh")
    small = jnp.concatenate(
        [
            jnp.sum(gain_one_part, axis=0),
            jnp.sum(gain_two_part, axis=0),
            table_grad.reshape(-1),
        ]
    )
    small = Chain(clock, links.all_sum(small))
    maps_sum.step()
    ffn_grad = units.finish()
    mom_ffn = muon_beta * pick(ffn_moment, 1) + ffn_grad
    gram = Chain(clock, links.sum_blocks(packed_gram(mom_ffn[0])))
    hidden_out = links.by_core(out_own, clock.after(out_other), 0)
    clock.done(hidden_out)
    maps_sum.step()
    gram.step()
    small.step()
    grad_other = links.swap_seq(clock.after(grad_send))
    maps_sum.step()
    gram.step()
    small.step()
    grad_tokens = links.by_core(grad_own, clock.after(grad_other), 0)
    clock.done(grad_tokens)
    gram.step()
    maps_sum.step()
    ffn_other = links.swap_seq(clock.after(ffn_grad))
    small.step()
    gram.step()
    ffn_mom = muon_beta * ffn_moment + links.by_core(ffn_grad, clock.after(ffn_other), 0)
    clock.done(ffn_mom)
    maps_sum.step()
    gram.step()
    small.step()
    maps_sum.step()
    if links.bits > 4:
        maps_sum.step(2 * links.bits - 8)
    gram_ffn, small = gram.finish(), small.finish()
    gain_sum = small[: 2 * width].reshape(2, width)
    table_sum = small[2 * width :].reshape(table_grad.shape)
    new_ffn = muon(
        [gram_ffn[None]],
        False,
        clock.after(mom_ffn),
        pick(ffn_master, 1),
        math.sqrt(max(1.0, FF / D)),
    )
    clock.done(new_ffn)
    attn_grad, mom_attn, attn_whole = maps_sum.finish()
    attn_other = links.swap_seq(attn_grad)
    new_attn = muon([attn_whole], True, mom_attn, pick(attn_master, 2), 1.0)
    attn_mom = muon_beta * attn_moment + links.by_core(attn_grad, attn_other, 0)
    new_gains, new_gain_first, new_gain_second = adamw(gains, gain_first, gain_second, gain_sum)
    new_bias, new_bias_first, new_bias_second = adamw(
        bias_table, bias_first, bias_second, table_sum
    )
    return (
        hidden_out,
        grad_tokens,
        new_attn,
        attn_mom,
        new_ffn,
        ffn_mom,
        new_gains,
        new_gain_first,
        new_gain_second,
        new_bias,
        new_bias_first,
        new_bias_second,
    )


def solution(mesh):
    in_specs = (
        P("dp", "seq", None),
        P("dp", "seq", None),
        P("dp", None),
        P(None, "dp", None),
        P(None, "dp", None),
        P(None, "dp", None),
        P(None, "dp", None),
        P(),
        P(),
        P(),
        P(),
        P(),
        P(),
    )
    out_specs = (
        P("dp", "seq", None),
        P("dp", "seq", None),
        P("seq", "dp", None),
        P(None, "dp", None),
        P("seq", "dp", None),
        P(None, "dp", None),
        P(),
        P(),
        P(),
        P(),
        P(),
        P(),
    )
    return jax.shard_map(
        per_device, mesh=mesh, in_specs=in_specs, out_specs=out_specs, check_vma=False
    )
```

time: 1570 us -> 402 us (0.26)
  waiting for transfers between devices: 970 us -> 95.6 us
  matrix products: 276 us -> 2.41 us
  Pallas kernels: 0 us -> 164 us
  blocking collectives: 95.2 us -> 0 us
  local copies, waits for them, and re-layouts: 123 us -> 32.3 us
  starting transfers between devices: 8.23 us -> 40.1 us
  other arithmetic: 72.3 us -> 47.7 us
    psum x3 -> x0, waiting for transfers between devices: 370 us -> none  [the longest x2 347 us: gram_sum(): lax.psum((exact_dot(ortho_attn, ortho_attn, 'mrd,mre->mde'), exact_dot(or...]
    reduce_scatter x1 -> x0, waiting for transfers between devices: 288 us -> none  [per_device(): lax.psum_scatter(ffn_grad, 'dp', scatter_dimension=1, tiled=True)]
    unnamed x8 -> x1, waiting for transfers between devices: 250 us -> 0.02 us
    pallas_call x0 -> x18, Pallas kernels: none -> 164 us  [the longest x2 48.8 us: ffn(): pl.pallas_call(functools.partial(ffn_kernel, len(after)), grid=(units //...]
    dot_general x26 -> x1, matrix products: 164 us -> 1.5 us  [mm(): return lax.dot_general(left, right, dims, preferred_element_type=F32)]
    dot_general x14 -> x2, matrix products: 111 us -> 0.91 us  [exact_dot(): return jnp.einsum(form, left, right, precision=lax.Precision.HIGHEST)]
    ppermute x0 -> x40, waiting for transfers between devices: none -> 95.6 us  [the longest x28 91 us: swap_dp(): return lax.ppermute(value, ('dp', 'seq'), pairs)]
    psum x2 -> x0, blocking collectives: 82.9 us -> none  [the longest x1 42.6 us: per_device(): lax.psum((jnp.sum(pick_attn * pick_attn, axis=(1, 2)), jnp.sum(pick_ffn *...]
  transfers between devices with their start and end apart: 9 -> 41, of which waited for: 8 -> 16; matrix products, arithmetic and copies ran while one was open for 14% -> 14% of each run, Pallas kernels for 0% -> 31%
where the time goes in v1:
time: 402 us; the launch traced here: 398 us
  Pallas kernels  164 us (41%)
  waiting for transfers between devices  95.6 us (24%)
  other arithmetic  47.7 us (12%)
  starting transfers between devices  40.1 us (10%)
  local copies, waits for them, and re-layouts  32.3 us (8%)
  between operations  15.7 us (4%)
    ppermute x28, waiting for transfers between devices, swap_dp(): return lax.ppermute(value, ('dp', 'seq'), pairs)  91 us
    pallas_call x2, Pallas kernels, ffn(): pl.pallas_call(functools.partial(ffn_kernel, len(after)), grid=(units //...  48.8 us
    ppermute x28, starting transfers between devices, swap_dp(): return lax.ppermute(value, ('dp', 'seq'), pairs)  38.5 us
    pallas_call x3, Pallas kernels, attend_back(): pl.pallas_call(functools.partial(attend_back_kernel, rows, length, 2 * TI...  33.3 us
    pallas_call x2, Pallas kernels, muon(): pl.pallas_call(functools.partial(muon_kernel, len(sources), gathered, sca...  18.8 us
    pallas_call x1, Pallas kernels, attend(): pl.pallas_call(functools.partial(attend_kernel, rows, length, 2 * TILE, l...  17.2 us
    unnamed x151, local copies, waits for them, and re-layouts  16.4 us
    pallas_call x1, Pallas kernels, middle_back(): pl.pallas_call(middle_kernel, grid_spec=pltpu.PrefetchScalarGridSpec(num_...  10.6 us
  transfers between devices with their start and end apart: 41, of which 16 were waited for; matrix products, arithmetic and copies ran while one was open for 14% of the time, Pallas kernels for 31%

profile of v1, /device:TPU:0, one launch (start us, length us, event | category | flops | bytes accessed | tf_op | source)
XLA Modules:
  0.0 397.7 jit_solution(2496361429197297775)
XLA Ops:
  10.9 4.0 %collective-permute-start.1 = (bf16[4,48,384]{2,1,0:T(8,128)(2,1)}, bf16[4,48,384]{2,1,0:T(8,128)(2,1)S(1)}, u32[]{:S(2)}, u32[]{:S(2)}) collective-permute-start(bf16[4,48,384]{2,1,0:T(8,128)(2,1)} %dynamic-slice_convert_fusion.4), channel_id=1, source_target_pairs={{0,16},{1,17},{2,18},{3,19},{4,20},{5,21},{6,22},{7,23},{8,24},{9,... | collective-permute-start | bytes 442376 | tf_op jit(solution)/shard_map/ppermute | solution.py:685
  14.9 2.5 dynamic-slice_bitcast_fusion.2
  20.3 1.8 collective-permute-done.1
  23.2 2.1 multiply_reduce_fusion.1
  26.5 8.9 %collective-permute-done.2 = bf16[4,2,48,384]{3,2,0,1:T(8,128)(2,1)S(1)} collective-permute-done((bf16[4,2,48,384]{3,2,0,1:T(8,128)(2,1)S(1)}, bf16[4,2,48,384]{3,2,0,1:T(8,128)(2,1)S(1)}, u32[]{:S(2)}, u32[]{:S(2)}) %collective-permute-start.2) | collective-permute-done | bytes 294944 | tf_op jit(solution)/shard_map/ppermute | solution.py:685
  35.6 1.8 collective-permute-start.3
  37.6 1.9 maximum_select_fusion.6
  40.9 6.1 %collective-permute-done.3 = bf16[4,2,2,48,384]{4,3,0,2,1:T(8,128)(2,1)S(1)} collective-permute-done((bf16[4,2,2,48,384]{4,3,0,2,1:T(8,128)(2,1)S(1)}, bf16[4,2,2,48,384]{4,3,0,2,1:T(8,128)(2,1)S(1)}, u32[]{:S(2)}, u32[]{:S(2)}) %collective-permute-start.3) | collective-permute-done | bytes 589856 | tf_op jit(solution)/shard_map/ppermute | solution.py:685
  51.7 15.3 %collective-permute-done.5 = bf16[4,2,2,2,48,384]{5,4,0,2,1,3:T(8,128)(2,1)} collective-permute-done((bf16[4,2,2,2,48,384]{5,4,0,2,1,3:T(8,128)(2,1)}, bf16[4,2,2,2,48,384]{5,4,0,2,1,3:T(8,128)(2,1)}, u32[]{:S(2)}, u32[]{:S(2)}) %collective-permute-start.5) | collective-permute-done | bytes 1179680 | tf_op jit(solution)/shard_map/ppermute | solution.py:685
  67.1 4.3 %fusion.2 = bf16[4,2,2,2,2,48,384]{6,5,0,2,1,4,3:T(8,128)(2,1)S(1)} fusion(bf16[4,2,2,2,1,48,384]{6,5,0,2,1,4,3:T(8,128)(2,1)} %bitcast.24, bf16[4,2,2,2,1,48,384]{6,5,0,2,1,4,3:T(8,128)(2,1)S(1)} %maximum_select_fusion.8, bf16[4,2,2,1,2,48,384]{6,5,0,2,1,4,3:T(8,128)(2,1)} %bitcast.25, bf16[4,2,2,1,2,48,384]{6,5,0,2,1,4,3:T(8,128)(2,1)S(1)} %maximum_select_fusion.10, ...), kind=kLoop, calls=%fused_computation.10 | loop fusion | flops 8257536 | bytes 7077891 | tf_op jit(solution)/shard_map/jit(_where)/select_n | solution.py:736
  71.3 2.0 copy.122
  73.8 4.6 %collective-permute-done.6.other_ref.w_other_ref = bf16[4,768,384]{2,1,0:T(8,128)(2,1)} collective-permute-done((bf16[4,768,384]{2,1,0:T(8,128)(2,1)}, bf16[4,768,384]{2,1,0:T(8,128)(2,1)}, u32[]{:S(2)}, u32[]{:S(2)}) %collective-permute-start.6) | collective-permute-done | bytes 2359328 | tf_op jit(solution)/shard_map/ppermute | solution.py:678
  78.4 7.8 %project.1.q_ref.k_ref.v_ref = bf16[3,1024,768]{2,1,0:T(8,128)(2,1)S(1)} custom-call(s32[1]{0:T(128)} %bitcast.core_ref, bf16[1024,768]{1,0:T(8,128)(2,1)S(1)} %fusion.1.normed_ref, bf16[4,768,384]{2,1,0:T(8,128)(2,1)} %bitcast.26.own_ref.w_own_ref, bf16[4,768,384]{2,1,0:T(8,128)(2,1)} %collective-permute-done.6.other_ref.w_other_ref), custom_call_target="tpu_custom_call" | custom-call | flops 1000 | bytes 1000 | tf_op jit(solution)/shard_map/project/pallas_call | solution.py:491
  86.3 17.2 %attend.1 = (bf16[1024,768]{1,0:T(8,128)(2,1)S(1)}, f32[6,2,1024]{2,1,0:T(2,128)S(1)}) custom-call(f32[6,2,512]{2,1,0:T(2,128)S(1)} %reshape.1167.trev_ref, s32[2,512,1]{2,1,0:T(8,128)S(1)} %copy.123.segk_ref, s32[2,1,512]{2,1,0:T(1,128)S(1)} %reshape.1169.segq_ref, bf16[3,1024,768]{2,1,0:T(8,128)(2,1)S(1)} %project.1.q_ref.k_ref.v_ref, ...), custom_call_target="tpu_custom_call" | custom-call | flops 1000 | bytes 1000 | tf_op jit(solution)/shard_map/attend/pallas_call | solution.py:171
  108.9 24.7 %ffn.2 = (f32[1024,768]{1,0:T(8,128)}, f32[1024,768]{1,0:T(8,128)}, f32[1536,768]{1,0:T(8,128)}, bf16[1536,768]{1,0:T(8,128)(2,1)}) custom-call(s32[1]{0:T(128)} %bitcast.1.first_ref, bf16[1024,768]{1,0:T(8,128)(2,1)S(1)} %multiply_convert_fusion.normed_ref, bf16[1024,768]{1,0:T(8,128)(2,1)} %bitcast_select_fusion.cot_ref, bf16[2,16,2,96,768]{4,3,2,1,0:T(8,128)(2,1)} %bitcast.191), custom_call_target="tpu_custom_call" | custom-call | flops 1000 | bytes 1000 | tf_op jit(solution)/shard_map/ffn/pallas_call | solution.py:378
  135.6 24.1 %ffn.3 = (f32[1024,768]{1,0:T(8,128)}, f32[1024,768]{1,0:T(8,128)}, f32[1536,768]{1,0:T(8,128)}, bf16[1536,768]{1,0:T(8,128)(2,1)}) custom-call(s32[1]{0:T(128)} %bitcast.1.first_ref, bf16[1024,768]{1,0:T(8,128)(2,1)S(1)} %copy-done.7, bf16[1024,768]{1,0:T(8,128)(2,1)} %bitcast_select_fusion.cot_ref, bf16[2,16,2,96,768]{4,3,2,1,0:T(8,128)(2,1)} %bitcast.192), custom_call_target="tpu_custom_call" | custom-call | flops 1000 | bytes 1000 | tf_op jit(solution)/shard_map/ffn/pallas_call | solution.py:378
  162.5 10.6 %middle_back.1 = (bf16[2,256,768]{2,1,0:T(8,128)(2,1)S(1)}, bf16[2,256,768]{2,1,0:T(8,128)(2,1)S(1)}, f32[1024,768]{1,0:T(8,128)S(1)}, bf16[1024,768]{1,0:T(8,12...) custom-call(s32[1]{0:T(128)} %bitcast.core_ref, f32[1024,768]{1,0:T(8,128)} %copy-done.41, ...), custom_call_target="tpu_custom_call" | custom-call | flops 1000 | bytes 1000 | tf_op jit(solution)/shard_map/middle_back/pallas_call | solution.py:451
  174.7 3.5 fold.5
  179.6 2.0 collective-permute-start.10
  181.6 11.2 %attend_back.3 = (bf16[3,1024,512]{2,1,0:T(8,128)(2,1)S(1)}, f32[2,2,512]{2,1,0:T(2,128)S(1)}) custom-call(f32[6,2,512]{2,1,0:T(2,128)S(1)} %copy-done.27, s32[2,512,1]{2,1,0:T(8,128)S(1)} %copy-done.9, s32[2,1,512]{2,1,0:T(1,128)S(1)} %reshape.1169.segq_ref, f32[6,2,1024]{2,1,0:T(2,128)S(1)} %copy-done.29, bf16[3,1024,768]{2,1,0:T(8,128)(2,1)} %copy-done.1, ...), custom_call_target="tpu_custom_call" | custom-call | flops 1000 | bytes 1000 | tf_op jit(solution)/shard_map/attend_back/pallas_call | solution.py:288
  192.9 11.0 %attend_back.4 = (bf16[3,1024,512]{2,1,0:T(8,128)(2,1)S(1)}, f32[2,2,512]{2,1,0:T(2,128)S(1)}) custom-call(f32[6,2,512]{2,1,0:T(2,128)S(1)} %copy-done.27, s32[2,512,1]{2,1,0:T(8,128)S(1)} %copy-done.9, s32[2,1,512]{2,1,0:T(1,128)S(1)} %reshape.1169.segq_ref, f32[6,2,1024]{2,1,0:T(2,128)S(1)} %copy-done.29, ...), custom_call_target="tpu_custom_call", output_to_operand_aliasing={{0}: (8, {})} | custom-call | flops 1000 | bytes 1000 | tf_op jit(solution)/shard_map/attend_back/pallas_call | solution.py:288
  204.0 2.6 convert_add_fusion.2
  208.7 2.6 pad_maximum_fusion
  211.3 2.9 fusion.4
  214.2 4.1 %maps_grad.2 = (f32[2,768,512]{2,1,0:T(8,128)S(1)}, bf16[2,768,512]{2,1,0:T(8,128)(2,1)S(1)}) custom-call(s32[1]{0:T(128)} %bitcast.1.first_ref, bf16[1024,768]{1,0:T(8,128)(2,1)S(1)} %copy-done.4, bf16[3,1024,512]{2,1,0:T(8,128)(2,1)S(1)} %get-tuple-element.138.grads_ref.refs_0_, f32[768,768]{1,0:T(8,128)S(1)} %copy-done.11), custom_call_target="tpu_custom_call" | custom-call | flops 1000 | bytes 1000 | tf_op jit(solution)/shard_map/maps_grad/pallas_call | solution.py:603
  219.6 11.0 %attend_back.5 = (bf16[3,1024,256]{2,1,0:T(8,128)(2,1)S(1)}, f32[2,2,512]{2,1,0:T(2,128)S(1)}) custom-call(f32[6,2,512]{2,1,0:T(2,128)S(1)} %copy-done.27, s32[2,512,1]{2,1,0:T(8,128)S(1)} %copy-done.9, s32[2,1,512]{2,1,0:T(1,128)S(1)} %reshape.1169.segq_ref, f32[6,2,1024]{2,1,0:T(2,128)S(1)} %copy-done.29, bf16[3,1024,768]{2,1,0:T(8,128)(2,1)} %copy-done.1, ...), custom_call_target="tpu_custom_call" | custom-call | flops 1000 | bytes 1000 | tf_op jit(solution)/shard_map/attend_back/pallas_call | solution.py:288
  231.2 2.8 fold.6
  234.1 3.1 maps_grad.3
  239.5 2.3 bitcast_add_fusion
  243.4 2.5 fold.7
  247.8 3.1 collective-permute-start.13
  250.9 9.9 %entry_back.1 = (f32[2,256,768]{2,1,0:T(8,128)S(1)}, f32[2,256,768]{2,1,0:T(8,128)S(1)}, f32[8,768]{1,0:T(8,128)S(1)}) custom-call(s32[1]{0:T(128)} %bitcast.core_ref, bf16[1024,768]{1,0:T(8,128)(2,1)} %bitcast.193, f32[1024,768]{1,0:T(8,128)} %copy-done.13, f32[1,768]{1,0:T(1,128)S(1)} %get-tuple-element.243.gain_ref, ...), custom_call_target="tpu_custom_call" | custom-call | flops 1000 | bytes 1000 | tf_op jit(solution)/shard_map/entry_back/pallas_call | solution.py:560
  271.0 4.8 %collective-permute-start.18 = (bf16[1,1,192,768]{3,2,1,0:T(8,128)(2,1)S(1)}, bf16[1,1,192,768]{3,2,1,0:T(8,128)(2,1)S(1)}, u32[]{:S(2)}, u32[]{:S(2)}) collective-permute-start(bf16[1,1,192,768]{3,2,1,0:T(8,128)(2,1)S(1)} %dynamic-slice_convert_fusion), channel_id=1, source_target_pairs={{0,16},{1,17},{2,18},{3,19},{4,20},{5,21},{6,22},{7,23},{8,24},{9,... | collective-permute-start | bytes 884744 | tf_op jit(solution)/shard_map/ppermute | solution.py:685
  277.8 11.8 %collective-permute-done.18 = bf16[1,1,192,768]{3,2,1,0:T(8,128)(2,1)S(1)} collective-permute-done((bf16[1,1,192,768]{3,2,1,0:T(8,128)(2,1)S(1)}, bf16[1,1,192,768]{3,2,1,0:T(8,128)(2,1)S(1)}, u32[]{:S(2)}, u32[]{:S(2)}) %collective-permute-start.18) | collective-permute-done | bytes 294944 | tf_op jit(solution)/shard_map/ppermute | solution.py:685
  293.4 4.2 %collective-permute-done.21 = bf16[2,96,896]{2,1,0:T(8,128)(2,1)S(1)} collective-permute-done((bf16[2,96,896]{2,1,0:T(8,128)(2,1)S(1)}, bf16[2,96,896]{2,1,0:T(8,128)(2,1)S(1)}, u32[]{:S(2)}, u32[]{:S(2)}) %collective-permute-start.21) | collective-permute-done | bytes 344096 | tf_op jit(solution)/shard_map/ppermute | solution.py:685
  300.1 8.2 %collective-permute-done.26 = bf16[2,1,48,768]{3,2,0,1:T(8,128)(2,1)S(1)} collective-permute-done((bf16[2,1,48,768]{3,2,0,1:T(8,128)(2,1)S(1)}, bf16[2,1,48,768]{3,2,0,1:T(8,128)(2,1)S(1)}, u32[]{:S(2)}, u32[]{:S(2)}) %collective-permute-start.26) | collective-permute-done | bytes 147488 | tf_op jit(solution)/shard_map/ppermute | solution.py:685
  309.1 1.8 collective-permute-start.28
  310.9 2.0 maximum_select_fusion
  312.8 5.6 %collective-permute-done.28 = bf16[96,896]{1,0:T(8,128)(2,1)S(1)} collective-permute-done((bf16[96,896]{1,0:T(8,128)(2,1)S(1)}, bf16[96,896]{1,0:T(8,128)(2,1)S(1)}, u32[]{:S(2)}, u32[]{:S(2)}) %collective-permute-start.28) | collective-permute-done | bytes 172064 | tf_op jit(solution)/shard_map/ppermute | solution.py:685
  318.9 2.7 collective-permute-start.31
  322.4 7.8 %collective-permute-done.31 = bf16[96,896]{1,0:T(8,128)(2,1)S(1)} collective-permute-done((bf16[96,896]{1,0:T(8,128)(2,1)S(1)}, bf16[96,896]{1,0:T(8,128)(2,1)S(1)}, u32[]{:S(2)}, u32[]{:S(2)}) %collective-permute-start.31) | collective-permute-done | bytes 172064 | tf_op jit(solution)/shard_map/ppermute | solution.py:685
  338.1 2.9 collective-permute-done.34
  341.0 2.7 collective-permute-done.33
  351.0 14.2 %collective-permute-done.37 = bf16[2,96,896]{2,1,0:T(8,128)(2,1)} collective-permute-done((bf16[2,96,896]{2,1,0:T(8,128)(2,1)}, bf16[2,96,896]{2,1,0:T(8,128)(2,1)}, u32[]{:S(2)}, u32[]{:S(2)}) %collective-permute-start.37) | collective-permute-done | bytes 344096 | tf_op jit(solution)/shard_map/ppermute | solution.py:685
  365.2 2.2 fusion.6
  367.4 5.6 %muon.2 = f32[1,192,768]{2,1,0:T(8,128)} custom-call(bf16[1,384,896]{2,1,0:T(8,128)(2,1)S(1)} %bitcast.190, f32[1,192,768]{2,1,0:T(8,128)S(1)} %get-tuple-element.186.refs_1_, f32[1,192,768]{2,1,0:T(8,128)S(1)} %constant_dynamic-slice_fusion.1.refs_2_), custom_call_target="tpu_custom_call" | custom-call | flops 1000 | bytes 1000 | tf_op jit(solution)/shard_map/muon/pallas_call | solution.py:899
  373.5 3.0 fusion.3
  377.4 13.1 %muon.3 = f32[2,48,768]{2,1,0:T(8,128)} custom-call(bf16[2,768,768]{2,1,0:T(8,128)(2,1)S(1)} %bitcast.186, f32[2,48,768]{2,1,0:T(8,128)S(1)} %copy-done.21, f32[2,48,768]{2,1,0:T(8,128)S(1)} %constant_dynamic-slice_fusion.refs_2_), custom_call_target="tpu_custom_call" | custom-call | flops 1000 | bytes 1000 | tf_op jit(solution)/shard_map/muon/pallas_call | solution.py:899
  (314 shorter events, 75.1 us)
Async XLA Ops:
  7.2 101.7 %all-gather.2.cloned.1.call-start = ((), (), s32[]{:S(2)}) async-start(), calls=%async_computation | async-start | bytes 9732096 | tf_op jit(solution)/shard_map/all_gather | solution.py:944
  10.9 11.3 %collective-permute-start.1 = (bf16[4,48,384]{2,1,0:T(8,128)(2,1)}, bf16[4,48,384]{2,1,0:T(8,128)(2,1)S(1)}, u32[]{:S(2)}, u32[]{:S(2)}) collective-permute-start(bf16[4,48,384]{2,1,0:T(8,128)(2,1)} %dynamic-slice_convert_fusion.4), channel_id=1, source_target_pairs={{0,16},{1,17},{2,18},{3,19},{4,20},{5,21},{6,22},{7,23},{8,24},{9,... | collective-permute-start | bytes 442376 | tf_op jit(solution)/shard_map/ppermute | solution.py:685
  17.4 5.9 %collective-permute-start = (bf16[2,256,768]{2,1,0:T(8,128)(2,1)}, bf16[2,256,768]{2,1,0:T(8,128)(2,1)}, u32[]{:S(2)}, u32[]{:S(2)}) collective-permute-start(bf16[2,256,768]{2,1,0:T(8,128)(2,1)} %get-tuple-element.241), channel_id=1, source_target_pairs={{0,1},{1,0},{2,3},{3,2},{4,5},{5,4},{6,7},{7,6},{8,9},{9,8},{10,11... | collective-permute-start | bytes 2359304 | tf_op jit(solution)/shard_map/ppermute | solution.py:678
  18.7 18.7 %collective-permute-start.4 = (bf16[2,256,768]{2,1,0:T(8,128)(2,1)}, bf16[2,256,768]{2,1,0:T(8,128)(2,1)}, u32[]{:S(2)}, u32[]{:S(2)}) collective-permute-start(bf16[2,256,768]{2,1,0:T(8,128)(2,1)} %get-tuple-element.240), channel_id=1, source_target_pairs={{0,1},{1,0},{2,3},{3,2},{4,5},{5,4},{6,7},{7,6},{8,9},{9,8},{10,11... | collective-permute-start | bytes 2359304 | tf_op jit(solution)/shard_map/ppermute | solution.py:678
  20.2 66.1 %copy-start.26 = (f32[6,2,512]{2,1,0:T(2,128)}, f32[6,2,512]{2,1,0:T(2,128)S(1)}, u32[]{:S(2)}) copy-start(f32[6,2,512]{2,1,0:T(2,128)S(1)} %reshape.1167.trev_ref) | copy-start | bytes 73732
  22.2 13.3 %collective-permute-start.2 = (bf16[4,2,48,384]{3,2,0,1:T(8,128)(2,1)S(1)}, bf16[4,2,48,384]{3,2,0,1:T(8,128)(2,1)S(1)}, u32[]{:S(2)}, u32[]{:S(2)}) collective-permute-start(bf16[4,2,48,384]{3,2,0,1:T(8,128)(2,1)S(1)} %maximum_select_fusion.25), channel_id=1, source_target_pairs={{0,8},{1,9},{2,10},{3,11},{4,12},{5,13},{6,14},{7,15},{8,0},{9,1},... | collective-permute-start | bytes 884744 | tf_op jit(solution)/shard_map/ppermute | solution.py:685
  26.5 51.9 %copy-start.3 = (bf16[1024,768]{1,0:T(8,128)(2,1)}, bf16[1024,768]{1,0:T(8,128)(2,1)S(1)}, u32[]{:S(2)}) copy-start(bf16[1024,768]{1,0:T(8,128)(2,1)S(1)} %fusion.1.normed_ref) | copy-start | bytes 4718596
  35.6 11.4 %collective-permute-start.3 = (bf16[4,2,2,48,384]{4,3,0,2,1:T(8,128)(2,1)S(1)}, bf16[4,2,2,48,384]{4,3,0,2,1:T(8,128)(2,1)S(1)}, u32[]{:S(2)}, u32[]{:S(2)}) collective-permute-start(bf16[4,2,2,48,384]{4,3,0,2,1:T(8,128)(2,1)S(1)} %maximum_select_fusion.19), channel_id=1, source_target_pairs={{0,4},{1,3},{2,6},{3,1},{4,0},{5,7},{6,2},{7,5},{8,12},{9,11},{10,... | collective-permute-start | bytes 1769480 | tf_op jit(solution)/shard_map/ppermute | solution.py:685
  49.0 18.0 %collective-permute-start.5 = (bf16[4,2,2,2,48,384]{5,4,0,2,1,3:T(8,128)(2,1)}, bf16[4,2,2,2,48,384]{5,4,0,2,1,3:T(8,128)(2,1)}, u32[]{:S(2)}, u32[]{:S(2)}) collective-permute-start(bf16[4,2,2,2,48,384]{5,4,0,2,1,3:T(8,128)(2,1)} %maximum_select_fusion.9), channel_id=1, source_target_pairs={{0,2},{1,5},{2,0},{3,7},{4,6},{5,1},{6,4},{7,3},{8,10},{9,13},{10,... | collective-permute-start | bytes 3538952 | tf_op jit(solution)/shard_map/ppermute | solution.py:685
  73.5 4.9 %collective-permute-start.6 = (bf16[4,768,384]{2,1,0:T(8,128)(2,1)}, bf16[4,768,384]{2,1,0:T(8,128)(2,1)}, u32[]{:S(2)}, u32[]{:S(2)}) collective-permute-start(bf16[4,768,384]{2,1,0:T(8,128)(2,1)} %bitcast.26.own_ref.w_own_ref), channel_id=1, source_target_pairs={{0,1},{1,0},{2,3},{3,2},{4,5},{5,4},{6,7},{7,6},{8,9},{9,8},{10,11... | collective-permute-start | bytes 7077896 | tf_op jit(solution)/shard_map/ppermute | solution.py:678
  86.2 17.3 %copy-start.1 = (bf16[3,1024,768]{2,1,0:T(8,128)(2,1)}, bf16[3,1024,768]{2,1,0:T(8,128)(2,1)S(1)}, u32[]{:S(2)}) copy-start(bf16[3,1024,768]{2,1,0:T(8,128)(2,1)S(1)} %project.1.q_ref.k_ref.v_ref) | copy-start | bytes 14155780
  108.9 24.7 %copy-start.6 = (bf16[1024,768]{1,0:T(8,128)(2,1)}, bf16[1024,768]{1,0:T(8,128)(2,1)S(1)}, u32[]{:S(2)}) copy-start(bf16[1024,768]{1,0:T(8,128)(2,1)S(1)} %multiply_convert_fusion.normed_ref) | copy-start | bytes 4718596
  133.7 26.4 %slice-start.2 = ((s8[4718592]{0:T(1024)(128)(4,1)}), s8[4194304]{0:T(1024)(128)(4,1)S(1)}, s32[]{:S(2)}) async-start(s8[4718592]{0:T(1024)(128)(4,1)} %bitcast.156), calls=%async_computation.3 | async-start | bytes 8388608
  133.7 26.4 %slice-start.3 = ((s8[4718592]{0:T(1024)(128)(4,1)}), s8[524288]{0:T(1024)(128)(4,1)S(1)}, s32[]{:S(2)}) async-start(s8[4718592]{0:T(1024)(128)(4,1)} %bitcast.156), calls=%async_computation.4 | async-start | bytes 1048576
  133.7 26.4 %collective-permute-start.7 = (bf16[1536,768]{1,0:T(8,128)(2,1)}, bf16[1536,768]{1,0:T(8,128)(2,1)S(1)}, u32[]{:S(2)}, u32[]{:S(2)}) collective-permute-start(bf16[1536,768]{1,0:T(8,128)(2,1)} %get-tuple-element.109), channel_id=1, source_target_pairs={{0,1},{1,0},{2,3},{3,2},{4,5},{5,4},{6,7},{7,6},{8,9},{9,8},{10,11... | collective-permute-start | bytes 7077896 | tf_op jit(solution)/shard_map/ppermute | solution.py:678
  159.7 15.0 %collective-permute-start.9 = (bf16[1536,768]{1,0:T(8,128)(2,1)}, bf16[1536,768]{1,0:T(8,128)(2,1)S(1)}, u32[]{:S(2)}, u32[]{:S(2)}) collective-permute-start(bf16[1536,768]{1,0:T(8,128)(2,1)} %get-tuple-element.111), channel_id=1, source_target_pairs={{0,1},{1,0},{2,3},{3,2},{4,5},{5,4},{6,7},{7,6},{8,9},{9,8},{10,11... | collective-permute-start | bytes 7077896 | tf_op jit(solution)/shard_map/ppermute | solution.py:678
  162.5 41.5 %collective-permute-start.8 = (bf16[1,8,96,768]{3,2,1,0:T(8,128)(2,1)S(1)}, bf16[1,8,96,768]{3,2,1,0:T(8,128)(2,1)}, u32[]{:S(2)}, u32[]{:S(2)}) collective-permute-start(bf16[1,8,96,768]{3,2,1,0:T(8,128)(2,1)S(1)} %get-tuple-element.114), channel_id=1, source_target_pairs={{0,2},{1,5},{2,0},{3,7},{4,6},{5,1},{6,4},{7,3},{8,10},{9,13},{10,... | collective-permute-start | bytes 3538952 | tf_op jit(solution)/shard_map/ppermute | solution.py:685
  179.6 26.9 %collective-permute-start.10 = (bf16[1,8,96,768]{3,2,1,0:T(8,128)(2,1)}, bf16[1,8,96,768]{3,2,1,0:T(8,128)(2,1)}, u32[]{:S(2)}, u32[]{:S(2)}) collective-permute-start(bf16[1,8,96,768]{3,2,1,0:T(8,128)(2,1)} %get-tuple-element.126), channel_id=1, source_target_pairs={{0,2},{1,5},{2,0},{3,7},{4,6},{5,1},{6,4},{7,3},{8,10},{9,13},{10,... | collective-permute-start | bytes 3538952 | tf_op jit(solution)/shard_map/ppermute | solution.py:685
  218.3 13.0 %collective-permute-start.12 = (bf16[2,768,512]{2,1,0:T(8,128)(2,1)S(1)}, bf16[2,768,512]{2,1,0:T(8,128)(2,1)S(1)}, u32[]{:S(2)}, u32[]{:S(2)}) collective-permute-start(bf16[2,768,512]{2,1,0:T(8,128)(2,1)S(1)} %get-tuple-element.140), channel_id=1, source_target_pairs={{0,1},{1,0},{2,3},{3,2},{4,5},{5,4},{6,7},{7,6},{8,9},{9,8},{10,11... | collective-permute-start | bytes 4718600 | tf_op jit(solution)/shard_map/ppermute | solution.py:678
  218.4 21.1 %collective-permute-start.11 = (bf16[1,4,192,768]{3,2,1,0:T(8,128)(2,1)}, bf16[1,4,192,768]{3,2,1,0:T(8,128)(2,1)}, u32[]{:S(2)}, u32[]{:S(2)}) collective-permute-start(bf16[1,4,192,768]{3,2,1,0:T(8,128)(2,1)} %fusion.4), channel_id=1, source_target_pairs={{0,4},{1,3},{2,6},{3,1},{4,0},{5,7},{6,2},{7,5},{8,12},{9,11},{10,... | collective-permute-start | bytes 3538952 | tf_op jit(solution)/shard_map/ppermute | solution.py:685
  237.2 5.6 %collective-permute-start.15 = (bf16[2,768,256]{2,1,0:T(8,128)(2,1)}, bf16[2,768,256]{2,1,0:T(8,128)(2,1)S(1)}, u32[]{:S(2)}, u32[]{:S(2)}) collective-permute-start(bf16[2,768,256]{2,1,0:T(8,128)(2,1)} %get-tuple-element.148), channel_id=1, source_target_pairs={{0,1},{1,0},{2,3},{3,2},{4,5},{5,4},{6,7},{7,6},{8,9},{9,8},{10,11... | collective-permute-start | bytes 2359304 | tf_op jit(solution)/shard_map/ppermute | solution.py:678
  237.2 24.8 %collective-permute-start.14 = (bf16[2,8,48,512]{3,2,1,0:T(8,128)(2,1)}, bf16[2,8,48,512]{3,2,1,0:T(8,128)(2,1)}, u32[]{:S(2)}, u32[]{:S(2)}) collective-permute-start(bf16[2,8,48,512]{3,2,1,0:T(8,128)(2,1)} %get-tuple-element.145), channel_id=1, source_target_pairs={{0,2},{1,5},{2,0},{3,7},{4,6},{5,1},{6,4},{7,3},{8,10},{9,13},{10,... | collective-permute-start | bytes 2359304 | tf_op jit(solution)/shard_map/ppermute | solution.py:685
  246.7 16.8 %collective-permute-start.16 = (bf16[2,8,48,256]{3,2,1,0:T(8,128)(2,1)}, bf16[2,8,48,256]{3,2,1,0:T(8,128)(2,1)S(1)}, u32[]{:S(2)}, u32[]{:S(2)}) collective-permute-start(bf16[2,8,48,256]{3,2,1,0:T(8,128)(2,1)} %get-tuple-element.153), channel_id=1, source_target_pairs={{0,2},{1,5},{2,0},{3,7},{4,6},{5,1},{6,4},{7,3},{8,10},{9,13},{10,... | collective-permute-start | bytes 1179656 | tf_op jit(solution)/shard_map/ppermute | solution.py:685
  247.8 20.6 %collective-permute-start.13 = (bf16[1,2,192,768]{3,2,1,0:T(8,128)(2,1)}, bf16[1,2,192,768]{3,2,1,0:T(8,128)(2,1)}, u32[]{:S(2)}, u32[]{:S(2)}) collective-permute-start(bf16[1,2,192,768]{3,2,1,0:T(8,128)(2,1)} %fusion.9), channel_id=1, source_target_pairs={{0,8},{1,9},{2,10},{3,11},{4,12},{5,13},{6,14},{7,15},{8,0},{9,1},... | collective-permute-start | bytes 1769480 | tf_op jit(solution)/shard_map/ppermute | solution.py:685
  266.1 10.3 %collective-permute-start.19 = (bf16[2,4,48,768]{3,2,1,0:T(8,128)(2,1)}, bf16[2,4,48,768]{3,2,1,0:T(8,128)(2,1)}, u32[]{:S(2)}, u32[]{:S(2)}) collective-permute-start(bf16[2,4,48,768]{3,2,1,0:T(8,128)(2,1)} %fusion.10), channel_id=1, source_target_pairs={{0,4},{1,3},{2,6},{3,1},{4,0},{5,7},{6,2},{7,5},{8,12},{9,11},{10,... | collective-permute-start | bytes 1769480 | tf_op jit(solution)/shard_map/ppermute | solution.py:685
  270.2 21.7 %collective-permute-start.17 = (bf16[2,256,768]{2,1,0:T(8,128)(2,1)S(1)}, bf16[2,256,768]{2,1,0:T(8,128)(2,1)S(1)}, u32[]{:S(2)}, u32[]{:S(2)}) collective-permute-start(bf16[2,256,768]{2,1,0:T(8,128)(2,1)S(1)} %copy-done.38), channel_id=1, source_target_pairs={{0,1},{1,0},{2,3},{3,2},{4,5},{5,4},{6,7},{7,6},{8,9},{9,8},{10,11... | collective-permute-start | bytes 2359304 | tf_op jit(solution)/shard_map/ppermute | solution.py:678
  270.3 19.3 %copy-start.51 = (f32[2,192,768]{2,1,0:T(8,128)S(1)}, f32[2,192,768]{2,1,0:T(8,128)}, u32[]{:S(2)}) copy-start(f32[2,192,768]{2,1,0:T(8,128)} %param.25) | copy-start | bytes 3538948
  270.4 27.5 %collective-permute-start.20 = (f32[1920]{0:T(1024)S(1)}, f32[1920]{0:T(1024)S(1)}, u32[]{:S(2)}, u32[]{:S(2)}) collective-permute-start(f32[1920]{0:T(1024)S(1)} %pad_maximum_fusion.4), channel_id=1, source_target_pairs={{0,2},{1,5},{2,0},{3,7},{4,6},{5,1},{6,4},{7,3},{8,10},{9,13},{10,... | collective-permute-start | bytes 23048 | tf_op jit(solution)/shard_map/ppermute | solution.py:685
  271.0 18.6 %collective-permute-start.18 = (bf16[1,1,192,768]{3,2,1,0:T(8,128)(2,1)S(1)}, bf16[1,1,192,768]{3,2,1,0:T(8,128)(2,1)S(1)}, u32[]{:S(2)}, u32[]{:S(2)}) collective-permute-start(bf16[1,1,192,768]{3,2,1,0:T(8,128)(2,1)S(1)} %dynamic-slice_convert_fusion), channel_id=1, source_target_pairs={{0,16},{1,17},{2,18},{3,19},{4,20},{5,21},{6,22},{7,23},{8,24},{9,... | collective-permute-start | bytes 884744 | tf_op jit(solution)/shard_map/ppermute | solution.py:685
  277.6 15.7 %collective-permute-start.22 = (bf16[2,2,48,768]{3,2,0,1:T(8,128)(2,1)S(1)}, bf16[2,2,48,768]{3,2,0,1:T(8,128)(2,1)S(1)}, u32[]{:S(2)}, u32[]{:S(2)}) collective-permute-start(bf16[2,2,48,768]{3,2,0,1:T(8,128)(2,1)S(1)} %fusion.14), channel_id=1, source_target_pairs={{0,8},{1,9},{2,10},{3,11},{4,12},{5,13},{6,14},{7,15},{8,0},{9,1},... | collective-permute-start | bytes 884744 | tf_op jit(solution)/shard_map/ppermute | solution.py:685
  290.4 7.3 %collective-permute-start.21 = (bf16[2,96,896]{2,1,0:T(8,128)(2,1)S(1)}, bf16[2,96,896]{2,1,0:T(8,128)(2,1)S(1)}, u32[]{:S(2)}, u32[]{:S(2)}) collective-permute-start(bf16[2,96,896]{2,1,0:T(8,128)(2,1)S(1)} %fusion.8), channel_id=1, source_target_pairs={{0,2},{1,5},{2,0},{3,7},{4,6},{5,1},{6,4},{7,3},{8,10},{9,13},{10,... | collective-permute-start | bytes 1032200 | tf_op jit(solution)/shard_map/ppermute | solution.py:685
  297.8 13.0 %collective-permute-start.23 = (f32[2,256,768]{2,1,0:T(8,128)S(1)}, f32[2,256,768]{2,1,0:T(8,128)S(1)}, u32[]{:S(2)}, u32[]{:S(2)}) collective-permute-start(f32[2,256,768]{2,1,0:T(8,128)S(1)} %copy-done.36), channel_id=1, source_target_pairs={{0,1},{1,0},{2,3},{3,2},{4,5},{5,4},{6,7},{7,6},{8,9},{9,8},{10,11... | collective-permute-start | bytes 4718600 | tf_op jit(solution)/shard_map/ppermute | solution.py:678
  297.9 10.3 %collective-permute-start.26 = (bf16[2,1,48,768]{3,2,0,1:T(8,128)(2,1)S(1)}, bf16[2,1,48,768]{3,2,0,1:T(8,128)(2,1)S(1)}, u32[]{:S(2)}, u32[]{:S(2)}) collective-permute-start(bf16[2,1,48,768]{3,2,0,1:T(8,128)(2,1)S(1)} %dynamic-slice_convert_fusion.3), channel_id=1, source_target_pairs={{0,16},{1,17},{2,18},{3,19},{4,20},{5,21},{6,22},{7,23},{8,24},{9,... | collective-permute-start | bytes 442376 | tf_op jit(solution)/shard_map/ppermute | solution.py:685
  298.0 11.0 %collective-permute-start.25 = (bf16[96,896]{1,0:T(8,128)(2,1)S(1)}, bf16[96,896]{1,0:T(8,128)(2,1)S(1)}, u32[]{:S(2)}, u32[]{:S(2)}) collective-permute-start(bf16[96,896]{1,0:T(8,128)(2,1)S(1)} %fusion.15), channel_id=1, source_target_pairs={{0,4},{1,3},{2,6},{3,1},{4,0},{5,7},{6,2},{7,5},{8,12},{9,11},{10,... | collective-permute-start | bytes 516104 | tf_op jit(solution)/shard_map/ppermute | solution.py:685
  299.7 11.1 %collective-permute-start.24 = (f32[1920]{0:T(1024)S(1)}, f32[1920]{0:T(1024)S(1)}, u32[]{:S(2)}, u32[]{:S(2)}) collective-permute-start(f32[1920]{0:T(1024)S(1)} %fusion.30), channel_id=1, source_target_pairs={{0,4},{1,3},{2,6},{3,1},{4,0},{5,7},{6,2},{7,5},{8,12},{9,11},{10,... | collective-permute-start | bytes 23048 | tf_op jit(solution)/shard_map/ppermute | solution.py:685
  309.0 9.4 %collective-permute-start.27 = (bf16[2,48,768]{2,1,0:T(8,128)(2,1)S(1)}, bf16[2,48,768]{2,1,0:T(8,128)(2,1)S(1)}, u32[]{:S(2)}, u32[]{:S(2)}) collective-permute-start(bf16[2,48,768]{2,1,0:T(8,128)(2,1)S(1)} %get-tuple-element.232), channel_id=1, source_target_pairs={{0,16},{1,17},{2,18},{3,19},{4,20},{5,21},{6,22},{7,23},{8,24},{9,... | collective-permute-start | bytes 442376 | tf_op jit(solution)/shard_map/ppermute | solution.py:685
  309.1 9.3 %collective-permute-start.28 = (bf16[96,896]{1,0:T(8,128)(2,1)S(1)}, bf16[96,896]{1,0:T(8,128)(2,1)S(1)}, u32[]{:S(2)}, u32[]{:S(2)}) collective-permute-start(bf16[96,896]{1,0:T(8,128)(2,1)S(1)} %fusion.13), channel_id=1, source_target_pairs={{0,8},{1,9},{2,10},{3,11},{4,12},{5,13},{6,14},{7,15},{8,0},{9,1},... | collective-permute-start | bytes 516104 | tf_op jit(solution)/shard_map/ppermute | solution.py:685
  318.5 13.5 %collective-permute-start.30 = (f32[1,192,768]{2,1,0:T(8,128)S(1)}, f32[1,192,768]{2,1,0:T(8,128)S(1)}, u32[]{:S(2)}, u32[]{:S(2)}) collective-permute-start(f32[1,192,768]{2,1,0:T(8,128)S(1)} %get-tuple-element.177), channel_id=1, source_target_pairs={{0,1},{1,0},{2,3},{3,2},{4,5},{5,4},{6,7},{7,6},{8,9},{9,8},{10,11... | collective-permute-start | bytes 1769480 | tf_op jit(solution)/shard_map/ppermute | solution.py:678
  318.6 3.7 collective-permute-start.32
  318.9 11.3 %collective-permute-start.31 = (bf16[96,896]{1,0:T(8,128)(2,1)S(1)}, bf16[96,896]{1,0:T(8,128)(2,1)S(1)}, u32[]{:S(2)}, u32[]{:S(2)}) collective-permute-start(bf16[96,896]{1,0:T(8,128)(2,1)S(1)} %add_convert_fusion.1), channel_id=1, source_target_pairs={{0,16},{1,17},{2,18},{3,19},{4,20},{5,21},{6,22},{7,23},{8,24},{9,... | collective-permute-start | bytes 516104 | tf_op jit(solution)/shard_map/ppermute | solution.py:685
  321.6 13.8 %collective-permute-start.39 = (f32[2,48,768]{2,1,0:T(8,128)S(1)}, f32[2,48,768]{2,1,0:T(8,128)S(1)}, u32[]{:S(2)}, u32[]{:S(2)}) collective-permute-start(f32[2,48,768]{2,1,0:T(8,128)S(1)} %get-tuple-element.234), channel_id=1, source_target_pairs={{0,1},{1,0},{2,3},{3,2},{4,5},{5,4},{6,7},{7,6},{8,9},{9,8},{10,11... | collective-permute-start | bytes 884744 | tf_op jit(solution)/shard_map/ppermute | solution.py:678
  321.7 11.9 %collective-permute-start.29 = (bf16[2,2,48,768]{3,2,0,1:T(8,128)(2,1)S(1)}, bf16[2,2,48,768]{3,2,0,1:T(8,128)(2,1)S(1)}, u32[]{:S(2)}, u32[]{:S(2)}) collective-permute-start(bf16[2,2,48,768]{3,2,0,1:T(8,128)(2,1)S(1)} %maximum_select_fusion.28), channel_id=1, source_target_pairs={{0,8},{1,9},{2,10},{3,11},{4,12},{5,13},{6,14},{7,15},{8,0},{9,1},... | collective-permute-start | bytes 884744 | tf_op jit(solution)/shard_map/ppermute | solution.py:685
  330.3 7.0 %collective-permute-start.35 = (bf16[96,896]{1,0:T(8,128)(2,1)S(1)}, bf16[96,896]{1,0:T(8,128)(2,1)S(1)}, u32[]{:S(2)}, u32[]{:S(2)}) collective-permute-start(bf16[96,896]{1,0:T(8,128)(2,1)S(1)} %add_convert_fusion), channel_id=1, source_target_pairs={{0,4},{1,3},{2,6},{3,1},{4,0},{5,7},{6,2},{7,5},{8,12},{9,11},{10,... | collective-permute-start | bytes 516104 | tf_op jit(solution)/shard_map/ppermute | solution.py:685
  333.7 9.9 %collective-permute-start.33 = (bf16[2,2,2,48,768]{4,3,0,1,2:T(8,128)(2,1)S(1)}, bf16[2,2,2,48,768]{4,3,0,1,2:T(8,128)(2,1)S(1)}, u32[]{:S(2)}, u32[]{:S(2)}) collective-permute-start(bf16[2,2,2,48,768]{4,3,0,1,2:T(8,128)(2,1)S(1)} %maximum_select_fusion.21), channel_id=1, source_target_pairs={{0,4},{1,3},{2,6},{3,1},{4,0},{5,7},{6,2},{7,5},{8,12},{9,11},{10,... | collective-permute-start | bytes 1769480 | tf_op jit(solution)/shard_map/ppermute | solution.py:685
  336.4 4.5 %collective-permute-start.34 = (f32[1920]{0:T(1024)S(1)}, f32[1920]{0:T(1024)S(1)}, u32[]{:S(2)}, u32[]{:S(2)}) collective-permute-start(f32[1920]{0:T(1024)S(1)} %add.248), channel_id=1, source_target_pairs={{0,16},{1,17},{2,18},{3,19},{4,20},{5,21},{6,22},{7,23},{8,24},{9,... | collective-permute-start | bytes 23048 | tf_op jit(solution)/shard_map/ppermute | solution.py:685
  340.9 8.6 %collective-permute-start.38 = (f32[1920]{0:T(1024)S(1)}, f32[1920]{0:T(1024)S(1)}, u32[]{:S(2)}, u32[]{:S(2)}) collective-permute-start(f32[1920]{0:T(1024)S(1)} %add.251), channel_id=1, source_target_pairs={{0,1},{1,0},{2,3},{3,2},{4,5},{5,4},{6,7},{7,6},{8,9},{9,8},{10,11... | collective-permute-start | bytes 23048 | tf_op jit(solution)/shard_map/ppermute | solution.py:678
  344.9 28.5 %collective-permute-start.36 = (bf16[2,2,2,2,48,768]{5,4,0,1,2,3:T(8,128)(2,1)}, bf16[2,2,2,2,48,768]{5,4,0,1,2,3:T(8,128)(2,1)}, u32[]{:S(2)}, u32[]{:S(2)}) collective-permute-start(bf16[2,2,2,2,48,768]{5,4,0,1,2,3:T(8,128)(2,1)} %maximum_select_fusion.14), channel_id=1, source_target_pairs={{0,2},{1,5},{2,0},{3,7},{4,6},{5,1},{6,4},{7,3},{8,10},{9,13},{10,... | collective-permute-start | bytes 3538952 | tf_op jit(solution)/shard_map/ppermute | solution.py:685
  349.0 16.2 %collective-permute-start.37 = (bf16[2,96,896]{2,1,0:T(8,128)(2,1)}, bf16[2,96,896]{2,1,0:T(8,128)(2,1)}, u32[]{:S(2)}, u32[]{:S(2)}) collective-permute-start(bf16[2,96,896]{2,1,0:T(8,128)(2,1)} %maximum_select_fusion.23), channel_id=1, source_target_pairs={{0,2},{1,5},{2,0},{3,7},{4,6},{5,1},{6,4},{7,3},{8,10},{9,13},{10,... | collective-permute-start | bytes 1032200 | tf_op jit(solution)/shard_map/ppermute | solution.py:685
  (69 other events, 297.2 us)
Sparse Core Ops, SparseCore 0:
  11.5 89.2 all-gather.1

commit v2 on v1

--- a/solution.py
+++ b/solution.py
@@ -749,6 +749,14 @@
         shape = value.shape
         return buf.reshape(shape[:axis] + (shape[axis] * self.size,) + shape[axis + 1 :])
 
+    def gather_rows(self, buf, last):
+        for turn in range(self.bits - 1, 0, -1):
+            came = yield buf, functools.partial(self.swap_dp, turn=turn)
+            buf = jnp.concatenate([buf, came], axis=1)
+        buf = held(buf, last())
+        came = yield buf, functools.partial(self.swap_dp, turn=0)
+        return buf, came
+
     def sum_blocks(self, value):
         rows, width = value.shape
         view = value.reshape(2, 2, rows // 4, width)
@@ -782,6 +790,19 @@
         )
 
 
+def held(value, other):
+    where = pl.BlockSpec(memory_space=pl.ANY)
+    return pl.pallas_call(
+        lambda *refs: None,
+        in_specs=[where, where],
+        out_specs=where,
+        out_shape=jax.ShapeDtypeStruct(value.shape, value.dtype),
+        input_output_aliases={0: 0},
+        cost_estimate=SMALL,
+        name="held",
+    )(value, other)
+
+
 def tie(value, others):
     return lax.optimization_barrier((value, *others))[0]
 
@@ -851,8 +872,10 @@
 
 def muon_kernel(parts, gathered, scaling, *refs):
     sources, (mom_ref, master_ref, out_ref) = refs[:parts], refs[parts:]
-    whole = jnp.concatenate([ref[0] for ref in sources], axis=1) if parts > 1 else sources[0][0]
-    gram = mm(whole, whole, TN) if gathered else unpack_gram(whole.astype(F32))
+    if gathered:
+        gram = sum(mm(ref[0], ref[0], TN) for ref in sources)
+    else:
+        gram = unpack_gram(sources[0][0].astype(F32))
     width = gram.shape[1]
     row = lax.broadcasted_iota(jnp.int32, (width, width), 0)
     column = lax.broadcasted_iota(jnp.int32, (width, width), 1)
@@ -1070,7 +1093,7 @@
         total = yield from links.scatter_rest(buf)
         grad = total.reshape(2, width // size, width)
         mom = muon_beta * moment_attn + grad
-        whole = yield from links.gather(mom.astype(BF), 1)
+        whole = yield from links.gather_rows(mom.astype(BF), lambda: gram.result)
         return grad, mom, whole
 
     two.step()
@@ -1103,30 +1126,31 @@
     )
     small = Chain(clock, links.all_sum(small))
     maps_sum.step()
+    hidden_out = links.by_core(out_own, clock.after(out_other), 0)
+    clock.done(hidden_out)
+    maps_sum.step()
     ffn_grad = units.finish()
     mom_ffn = muon_beta * pick(ffn_moment, 1) + ffn_grad
     gram = Chain(clock, links.sum_blocks(packed_gram(mom_ffn[0])))
-    hidden_out = links.by_core(out_own, clock.after(out_other), 0)
-    clock.done(hidden_out)
-    maps_sum.step()
-    gram.step()
     small.step()
     grad_other = links.swap_seq(clock.after(grad_send))
     maps_sum.step()
     gram.step()
     small.step()
+    gram.step()
     grad_tokens = links.by_core(grad_own, clock.after(grad_other), 0)
     clock.done(grad_tokens)
+    maps_sum.step()
+    small.step()
     gram.step()
+    ffn_other = links.swap_seq(clock.after(ffn_grad))
     maps_sum.step()
-    ffn_other = links.swap_seq(clock.after(ffn_grad))
-    small.step()
     gram.step()
     ffn_mom = muon_beta * ffn_moment + links.by_core(ffn_grad, clock.after(ffn_other), 0)
     clock.done(ffn_mom)
-    maps_sum.step()
     gram.step()
     small.step()
+    gram.finish()
     maps_sum.step()
     if links.bits > 4:
         maps_sum.step(2 * links.bits - 8)
@@ -1143,7 +1167,7 @@
     clock.done(new_ffn)
     attn_grad, mom_attn, attn_whole = maps_sum.finish()
     attn_other = links.swap_seq(attn_grad)
-    new_attn = muon([attn_whole], True, mom_attn, pick(attn_master, 2), 1.0)
+    new_attn = muon(attn_whole, True, mom_attn, pick(attn_master, 2), 1.0)
     attn_mom = muon_beta * attn_moment + links.by_core(attn_grad, attn_other, 0)
     new_gains, new_gain_first, new_gain_second = adamw(gains, gain_first, gain_second, gain_sum)
     new_bias, new_bias_first, new_bias_second = adamw(

time: 402 us -> 401 us (level)
  starting transfers between devices: 40.1 us -> 34.4 us
    ppermute x28, starting transfers between devices: 38.5 us -> 32.5 us  [swap_dp(): return lax.ppermute(value, ('dp', 'seq'), pairs)]
    select_n x3 -> x2, other arithmetic: 9.46 us -> 5.36 us  [gather_near(): jnp.where(self.first, self.order(self.bit(0), buf, came, at + 1), self.or...]
    select_n x18 -> x11, other arithmetic: 6.25 us -> 2.19 us  [order(): jnp.where(bit == 0, jnp.stack([same, other], axis=axis), jnp.stack([other...]
    unnamed x151 -> x163, local copies, waits for them, and re-layouts: 16.4 us -> 18 us
  transfers between devices with their start and end apart: 41 -> 41, of which waited for: 16 -> 18; matrix products, arithmetic and copies ran while one was open for 14% -> 15% of each run, Pallas kernels for 31% -> 31%
where the time goes in v2:
time: 401 us; the launch traced here: 397 us
  Pallas kernels  166 us (41%)
  waiting for transfers between devices  96.1 us (24%)
  other arithmetic  46.3 us (12%)
  local copies, waits for them, and re-layouts  35.9 us (9%)
  starting transfers between devices  34.4 us (9%)
  between operations  15.6 us (4%)
    ppermute x28, waiting for transfers between devices, swap_dp(): return lax.ppermute(value, ('dp', 'seq'), pairs)  91.2 us
    pallas_call x2, Pallas kernels, ffn(): pl.pallas_call(functools.partial(ffn_kernel, len(after)), grid=(units //...  48.6 us
    pallas_call x3, Pallas kernels, attend_back(): pl.pallas_call(functools.partial(attend_back_kernel, rows, length, 2 * TI...  33.2 us
    ppermute x28, starting transfers between devices, swap_dp(): return lax.ppermute(value, ('dp', 'seq'), pairs)  32.5 us
    pallas_call x2, Pallas kernels, muon(): pl.pallas_call(functools.partial(muon_kernel, len(sources), gathered, sca...  21.1 us
    unnamed x163, local copies, waits for them, and re-layouts  18 us
    pallas_call x1, Pallas kernels, attend(): pl.pallas_call(functools.partial(attend_kernel, rows, length, 2 * TILE, l...  17.2 us
    pallas_call x1, Pallas kernels, entry_back(): pl.pallas_call(entry_kernel, grid_spec=pltpu.PrefetchScalarGridSpec(num_s...  10.9 us
  transfers between devices with their start and end apart: 41, of which 18 were waited for; matrix products, arithmetic and copies ran while one was open for 15% of the time, Pallas kernels for 31%

profile of v2, /device:TPU:0, one launch (start us, length us, event | category | flops | bytes accessed | tf_op | source)
XLA Modules:
  0.0 396.7 jit_solution(6596448650584926509)
XLA Ops:
  10.9 4.0 %collective-permute-start.1 = (bf16[4,48,384]{2,1,0:T(8,128)(2,1)}, bf16[4,48,384]{2,1,0:T(8,128)(2,1)S(1)}, u32[]{:S(2)}, u32[]{:S(2)}) collective-permute-start(bf16[4,48,384]{2,1,0:T(8,128)(2,1)} %dynamic-slice_convert_fusion.4), channel_id=1, source_target_pairs={{0,16},{1,17},{2,18},{3,19},{4,20},{5,21},{6,22},{7,23},{8,24},{9,... | collective-permute-start | bytes 442376 | tf_op jit(solution)/shard_map/ppermute | solution.py:685
  14.9 2.5 dynamic-slice_bitcast_fusion.2
  23.2 2.1 multiply_reduce_fusion.1
  26.5 8.9 %collective-permute-done.2 = bf16[4,2,48,384]{3,2,0,1:T(8,128)(2,1)S(1)} collective-permute-done((bf16[4,2,48,384]{3,2,0,1:T(8,128)(2,1)S(1)}, bf16[4,2,48,384]{3,2,0,1:T(8,128)(2,1)S(1)}, u32[]{:S(2)}, u32[]{:S(2)}) %collective-permute-start.2) | collective-permute-done | bytes 294944 | tf_op jit(solution)/shard_map/ppermute | solution.py:685
  40.9 6.1 %collective-permute-done.3 = bf16[4,2,2,48,384]{4,3,0,2,1:T(8,128)(2,1)S(1)} collective-permute-done((bf16[4,2,2,48,384]{4,3,0,2,1:T(8,128)(2,1)S(1)}, bf16[4,2,2,48,384]{4,3,0,2,1:T(8,128)(2,1)S(1)}, u32[]{:S(2)}, u32[]{:S(2)}) %collective-permute-start.3) | collective-permute-done | bytes 589856 | tf_op jit(solution)/shard_map/ppermute | solution.py:685
  51.7 15.3 %collective-permute-done.5 = bf16[4,2,2,2,48,384]{5,4,0,2,1,3:T(8,128)(2,1)} collective-permute-done((bf16[4,2,2,2,48,384]{5,4,0,2,1,3:T(8,128)(2,1)}, bf16[4,2,2,2,48,384]{5,4,0,2,1,3:T(8,128)(2,1)}, u32[]{:S(2)}, u32[]{:S(2)}) %collective-permute-start.5) | collective-permute-done | bytes 1179680 | tf_op jit(solution)/shard_map/ppermute | solution.py:685
  67.1 4.3 %fusion.2 = bf16[4,2,2,2,2,48,384]{6,5,0,2,1,4,3:T(8,128)(2,1)S(1)} fusion(bf16[4,2,2,2,1,48,384]{6,5,0,2,1,4,3:T(8,128)(2,1)} %bitcast.24, bf16[4,2,2,2,1,48,384]{6,5,0,2,1,4,3:T(8,128)(2,1)S(1)} %maximum_select_fusion.6, bf16[4,2,2,1,2,48,384]{6,5,0,2,1,4,3:T(8,128)(2,1)} %bitcast.25, bf16[4,2,2,1,2,48,384]{6,5,0,2,1,4,3:T(8,128)(2,1)S(1)} %maximum_select_fusion.8, ...), kind=kLoop, calls=%fused_computation.10 | loop fusion | flops 8257536 | bytes 7077891 | tf_op jit(solution)/shard_map/jit(_where)/select_n | solution.py:736
  71.3 2.0 copy.120
  73.8 4.6 %collective-permute-done.6.other_ref.w_other_ref = bf16[4,768,384]{2,1,0:T(8,128)(2,1)} collective-permute-done((bf16[4,768,384]{2,1,0:T(8,128)(2,1)}, bf16[4,768,384]{2,1,0:T(8,128)(2,1)}, u32[]{:S(2)}, u32[]{:S(2)}) %collective-permute-start.6) | collective-permute-done | bytes 2359328 | tf_op jit(solution)/shard_map/ppermute | solution.py:678
  78.4 7.8 %project.1.q_ref.k_ref.v_ref = bf16[3,1024,768]{2,1,0:T(8,128)(2,1)S(1)} custom-call(s32[1]{0:T(128)} %bitcast.core_ref, bf16[1024,768]{1,0:T(8,128)(2,1)S(1)} %fusion.1.normed_ref, bf16[4,768,384]{2,1,0:T(8,128)(2,1)} %bitcast.26.own_ref.w_own_ref, bf16[4,768,384]{2,1,0:T(8,128)(2,1)} %collective-permute-done.6.other_ref.w_other_ref), custom_call_target="tpu_custom_call" | custom-call | flops 1000 | bytes 1000 | tf_op jit(solution)/shard_map/project/pallas_call | solution.py:491
  86.3 17.2 %attend.1 = (bf16[1024,768]{1,0:T(8,128)(2,1)S(1)}, f32[6,2,1024]{2,1,0:T(2,128)S(1)}) custom-call(f32[6,2,512]{2,1,0:T(2,128)S(1)} %reshape.780.trev_ref, s32[2,512,1]{2,1,0:T(8,128)S(1)} %copy.121.segk_ref, s32[2,1,512]{2,1,0:T(1,128)S(1)} %reshape.782.segq_ref, bf16[3,1024,768]{2,1,0:T(8,128)(2,1)S(1)} %project.1.q_ref.k_ref.v_ref, ...), custom_call_target="tpu_custom_call" | custom-call | flops 1000 | bytes 1000 | tf_op jit(solution)/shard_map/attend/pallas_call | solution.py:171
  108.9 24.5 %ffn.2 = (f32[1024,768]{1,0:T(8,128)}, f32[1024,768]{1,0:T(8,128)}, f32[1536,768]{1,0:T(8,128)}, bf16[1536,768]{1,0:T(8,128)(2,1)}) custom-call(s32[1]{0:T(128)} %bitcast.1.first_ref, bf16[1024,768]{1,0:T(8,128)(2,1)S(1)} %multiply_convert_fusion.normed_ref, bf16[1024,768]{1,0:T(8,128)(2,1)} %bitcast_select_fusion.cot_ref, bf16[2,16,2,96,768]{4,3,2,1,0:T(8,128)(2,1)} %bitcast.177), custom_call_target="tpu_custom_call" | custom-call | flops 1000 | bytes 1000 | tf_op jit(solution)/shard_map/ffn/pallas_call | solution.py:378
  135.4 24.1 %ffn.3 = (f32[1024,768]{1,0:T(8,128)}, f32[1024,768]{1,0:T(8,128)}, f32[1536,768]{1,0:T(8,128)}, bf16[1536,768]{1,0:T(8,128)(2,1)}) custom-call(s32[1]{0:T(128)} %bitcast.1.first_ref, bf16[1024,768]{1,0:T(8,128)(2,1)S(1)} %copy-done.7, bf16[1024,768]{1,0:T(8,128)(2,1)} %bitcast_select_fusion.cot_ref, bf16[2,16,2,96,768]{4,3,2,1,0:T(8,128)(2,1)} %bitcast.178), custom_call_target="tpu_custom_call" | custom-call | flops 1000 | bytes 1000 | tf_op jit(solution)/shard_map/ffn/pallas_call | solution.py:378
  162.4 10.6 %middle_back.1 = (bf16[2,256,768]{2,1,0:T(8,128)(2,1)S(1)}, bf16[2,256,768]{2,1,0:T(8,128)(2,1)S(1)}, f32[1024,768]{1,0:T(8,128)S(1)}, bf16[1024,768]{1,0:T(8,12...) custom-call(s32[1]{0:T(128)} %bitcast.core_ref, f32[1024,768]{1,0:T(8,128)} %copy-done.40, ...), custom_call_target="tpu_custom_call" | custom-call | flops 1000 | bytes 1000 | tf_op jit(solution)/shard_map/middle_back/pallas_call | solution.py:451
  176.2 2.6 fold.5
  180.2 2.0 collective-permute-start.10
  182.2 11.2 %attend_back.3 = (bf16[3,1024,512]{2,1,0:T(8,128)(2,1)S(1)}, f32[2,2,512]{2,1,0:T(2,128)S(1)}) custom-call(f32[6,2,512]{2,1,0:T(2,128)S(1)} %reshape.780.trev_ref, s32[2,512,1]{2,1,0:T(8,128)S(1)} %copy-done.9, s32[2,1,512]{2,1,0:T(1,128)S(1)} %reshape.782.segq_ref, f32[6,2,1024]{2,1,0:T(2,128)S(1)} %get-tuple-element.129.lse_ref, ...), custom_call_target="tpu_custom_call" | custom-call | flops 1000 | bytes 1000 | tf_op jit(solution)/shard_map/attend_back/pallas_call | solution.py:288
  193.4 11.0 %attend_back.4 = (bf16[3,1024,512]{2,1,0:T(8,128)(2,1)S(1)}, f32[2,2,512]{2,1,0:T(2,128)S(1)}) custom-call(f32[6,2,512]{2,1,0:T(2,128)S(1)} %reshape.780.trev_ref, s32[2,512,1]{2,1,0:T(8,128)S(1)} %copy-done.9, s32[2,1,512]{2,1,0:T(1,128)S(1)} %reshape.782.segq_ref, f32[6,2,1024]{2,1,0:T(2,128)S(1)} %get-tuple-element.129.lse_ref, ...), custom_call_target="tpu_custom_call", output_to_operand_aliasing={{0}: (8, {})} | custom-call | flops 1000 | bytes 1000 | tf_op jit(solution)/shard_map/attend_back/pallas_call | solution.py:288
  204.5 2.6 convert_add_fusion.2
  209.2 2.5 pad_maximum_fusion
  211.6 2.9 fusion.3
  214.5 4.1 %maps_grad.2 = (f32[2,768,512]{2,1,0:T(8,128)S(1)}, bf16[2,768,512]{2,1,0:T(8,128)(2,1)S(1)}) custom-call(s32[1]{0:T(128)} %bitcast.1.first_ref, bf16[1024,768]{1,0:T(8,128)(2,1)S(1)} %copy-done.4, bf16[3,1024,512]{2,1,0:T(8,128)(2,1)S(1)} %get-tuple-element.139.grads_ref.refs_0_, f32[768,768]{1,0:T(8,128)S(1)} %copy-done.12), custom_call_target="tpu_custom_call" | custom-call | flops 1000 | bytes 1000 | tf_op jit(solution)/shard_map/maps_grad/pallas_call | solution.py:603
  220.0 11.0 %attend_back.5 = (bf16[3,1024,256]{2,1,0:T(8,128)(2,1)S(1)}, f32[2,2,512]{2,1,0:T(2,128)S(1)}) custom-call(f32[6,2,512]{2,1,0:T(2,128)S(1)} %reshape.780.trev_ref, s32[2,512,1]{2,1,0:T(8,128)S(1)} %copy-done.9, s32[2,1,512]{2,1,0:T(1,128)S(1)} %reshape.782.segq_ref, f32[6,2,1024]{2,1,0:T(2,128)S(1)} %get-tuple-element.129.lse_ref, ...), custom_call_target="tpu_custom_call" | custom-call | flops 1000 | bytes 1000 | tf_op jit(solution)/shard_map/attend_back/pallas_call | solution.py:288
  231.0 2.8 fold.6
  233.8 3.1 maps_grad.3
  239.3 2.3 bitcast_add_fusion
  243.2 2.5 fold.7
  247.7 3.3 collective-permute-start.13
  250.9 10.9 %entry_back.1 = (f32[2,256,768]{2,1,0:T(8,128)S(1)}, f32[2,256,768]{2,1,0:T(8,128)}, f32[8,768]{1,0:T(8,128)S(1)}) custom-call(s32[1]{0:T(128)} %bitcast.core_ref, bf16[1024,768]{1,0:T(8,128)(2,1)} %bitcast.179, f32[1024,768]{1,0:T(8,128)} %copy-done.16, f32[1,768]{1,0:T(1,128)S(1)} %get-tuple-element.245.gain_ref, ...), custom_call_target="tpu_custom_call" | custom-call | flops 1000 | bytes 1000 | tf_op jit(solution)/shard_map/entry_back/pallas_call | solution.py:560
  261.8 1.9 convert_add_fusion.3
  269.3 6.0 %collective-permute-done.18 = bf16[2,4,48,768]{3,2,1,0:T(8,128)(2,1)} collective-permute-done((bf16[2,4,48,768]{3,2,1,0:T(8,128)(2,1)}, bf16[2,4,48,768]{3,2,1,0:T(8,128)(2,1)}, u32[]{:S(2)}, u32[]{:S(2)}) %collective-permute-start.18) | collective-permute-done | bytes 589856 | tf_op jit(solution)/shard_map/ppermute | solution.py:685
  280.1 5.7 %collective-permute-start.20 = (bf16[1,1,192,768]{3,2,1,0:T(8,128)(2,1)}, bf16[1,1,192,768]{3,2,1,0:T(8,128)(2,1)S(1)}, u32[]{:S(2)}, u32[]{:S(2)}) collective-permute-start(bf16[1,1,192,768]{3,2,1,0:T(8,128)(2,1)} %dynamic-slice_convert_fusion), channel_id=1, source_target_pairs={{0,16},{1,17},{2,18},{3,19},{4,20},{5,21},{6,22},{7,23},{8,24},{9,... | collective-permute-start | bytes 884744 | tf_op jit(solution)/shard_map/ppermute | solution.py:685
  287.3 4.7 %collective-permute-done.21 = bf16[2,2,48,768]{3,2,0,1:T(8,128)(2,1)} collective-permute-done((bf16[2,2,48,768]{3,2,0,1:T(8,128)(2,1)}, bf16[2,2,48,768]{3,2,0,1:T(8,128)(2,1)}, u32[]{:S(2)}, u32[]{:S(2)}) %collective-permute-start.21) | collective-permute-done | bytes 294944 | tf_op jit(solution)/shard_map/ppermute | solution.py:685
  293.9 3.6 collective-permute-done.20
  300.0 10.3 %collective-permute-done.24 = bf16[2,1,48,768]{3,2,0,1:T(8,128)(2,1)} collective-permute-done((bf16[2,1,48,768]{3,2,0,1:T(8,128)(2,1)S(1)}, bf16[2,1,48,768]{3,2,0,1:T(8,128)(2,1)}, u32[]{:S(2)}, u32[]{:S(2)}) %collective-permute-start.24) | collective-permute-done | bytes 147488 | tf_op jit(solution)/shard_map/ppermute | solution.py:685
  313.5 2.0 collective-permute-start.26
  315.5 3.5 collective-permute-done.26
  319.0 2.1 collective-permute-start.29
  321.1 4.0 %maximum_select_fusion = f32[4,256,768]{2,1,0:T(8,128)} fusion(f32[2,256,768]{2,1,0:T(8,128)} %collective-permute-done.22, f32[2,256,768]{2,1,0:T(8,128)S(1)} %copy-done.23, pred[]{:T(512)S(6)} %eq.21), kind=kLoop, calls=%fused_computation.5 | loop fusion | flops 2359296 | bytes 6291457 | tf_op jit(solution)/shard_map/jit(_where)/select_n | solution.py:786
  325.2 2.1 collective-permute-done.29
  327.7 7.4 %collective-permute-done.28 = bf16[2,96,768]{2,1,0:T(8,128)(2,1)S(1)} collective-permute-done((bf16[2,96,768]{2,1,0:T(8,128)(2,1)S(1)}, bf16[2,96,768]{2,1,0:T(8,128)(2,1)S(1)}, u32[]{:S(2)}, u32[]{:S(2)}) %collective-permute-start.28) | collective-permute-done | bytes 294944 | tf_op jit(solution)/shard_map/ppermute | solution.py:685
  335.9 2.9 collective-permute-done.32
  340.8 6.1 %collective-permute-done.33 = bf16[96,896]{1,0:T(8,128)(2,1)S(1)} collective-permute-done((bf16[96,896]{1,0:T(8,128)(2,1)S(1)}, bf16[96,896]{1,0:T(8,128)(2,1)S(1)}, u32[]{:S(2)}, u32[]{:S(2)}) %collective-permute-start.33) | collective-permute-done | bytes 172064 | tf_op jit(solution)/shard_map/ppermute | solution.py:685
  347.7 4.4 %collective-permute-done.36 = f32[1920]{0:T(1024)S(1)} collective-permute-done((f32[1920]{0:T(1024)S(1)}, f32[1920]{0:T(1024)S(1)}, u32[]{:S(2)}, u32[]{:S(2)}) %collective-permute-start.36) | collective-permute-done | bytes 7712 | tf_op jit(solution)/shard_map/ppermute | solution.py:685
  352.2 2.2 collective-permute-done.35
  360.1 5.6 %muon.2 = f32[1,192,768]{2,1,0:T(8,128)} custom-call(bf16[1,384,896]{2,1,0:T(8,128)(2,1)S(1)} %bitcast.175, f32[1,192,768]{2,1,0:T(8,128)S(1)} %get-tuple-element.188.refs_1_, f32[1,192,768]{2,1,0:T(8,128)S(1)} %constant_dynamic-slice_fusion.1.refs_2_), custom_call_target="tpu_custom_call" | custom-call | flops 1000 | bytes 1000 | tf_op jit(solution)/shard_map/muon/pallas_call | solution.py:922
  367.2 5.9 %collective-permute-done.37.refs_1_ = bf16[2,384,768]{2,1,0:T(8,128)(2,1)} collective-permute-done((bf16[2,384,768]{2,1,0:T(8,128)(2,1)}, bf16[2,384,768]{2,1,0:T(8,128)(2,1)}, u32[]{:S(2)}, u32[]{:S(2)}) %collective-permute-start.37) | collective-permute-done | bytes 1179680 | tf_op jit(solution)/shard_map/ppermute | solution.py:685
  374.1 15.5 %muon.3 = f32[2,48,768]{2,1,0:T(8,128)} custom-call(bf16[2,384,768]{2,1,0:T(8,128)(2,1)S(1)} %copy-done.10, bf16[2,384,768]{2,1,0:T(8,128)(2,1)} %collective-permute-done.37.refs_1_, f32[2,48,768]{2,1,0:T(8,128)S(1)} %get-tuple-element.235.refs_2_, f32[2,48,768]{2,1,0:T(8,128)S(1)} %copy-done.26), custom_call_target="tpu_custom_call" | custom-call | flops 1000 | bytes 1000 | tf_op jit(solution)/shard_map/muon/pallas_call | solution.py:922
  (319 shorter events, 76.5 us)
Async XLA Ops:
  7.2 101.7 %all-gather.2.cloned.1.call-start = ((), (), s32[]{:S(2)}) async-start(), calls=%async_computation | async-start | bytes 9732096 | tf_op jit(solution)/shard_map/all_gather | solution.py:967
  10.9 11.3 %collective-permute-start.1 = (bf16[4,48,384]{2,1,0:T(8,128)(2,1)}, bf16[4,48,384]{2,1,0:T(8,128)(2,1)S(1)}, u32[]{:S(2)}, u32[]{:S(2)}) collective-permute-start(bf16[4,48,384]{2,1,0:T(8,128)(2,1)} %dynamic-slice_convert_fusion.4), channel_id=1, source_target_pairs={{0,16},{1,17},{2,18},{3,19},{4,20},{5,21},{6,22},{7,23},{8,24},{9,... | collective-permute-start | bytes 442376 | tf_op jit(solution)/shard_map/ppermute | solution.py:685
  17.4 5.9 %collective-permute-start = (bf16[2,256,768]{2,1,0:T(8,128)(2,1)}, bf16[2,256,768]{2,1,0:T(8,128)(2,1)}, u32[]{:S(2)}, u32[]{:S(2)}) collective-permute-start(bf16[2,256,768]{2,1,0:T(8,128)(2,1)} %get-tuple-element.243), channel_id=1, source_target_pairs={{0,1},{1,0},{2,3},{3,2},{4,5},{5,4},{6,7},{7,6},{8,9},{9,8},{10,11... | collective-permute-start | bytes 2359304 | tf_op jit(solution)/shard_map/ppermute | solution.py:678
  18.7 18.7 %collective-permute-start.4 = (bf16[2,256,768]{2,1,0:T(8,128)(2,1)}, bf16[2,256,768]{2,1,0:T(8,128)(2,1)}, u32[]{:S(2)}, u32[]{:S(2)}) collective-permute-start(bf16[2,256,768]{2,1,0:T(8,128)(2,1)} %get-tuple-element.242), channel_id=1, source_target_pairs={{0,1},{1,0},{2,3},{3,2},{4,5},{5,4},{6,7},{7,6},{8,9},{9,8},{10,11... | collective-permute-start | bytes 2359304 | tf_op jit(solution)/shard_map/ppermute | solution.py:678
  22.2 13.3 %collective-permute-start.2 = (bf16[4,2,48,384]{3,2,0,1:T(8,128)(2,1)S(1)}, bf16[4,2,48,384]{3,2,0,1:T(8,128)(2,1)S(1)}, u32[]{:S(2)}, u32[]{:S(2)}) collective-permute-start(bf16[4,2,48,384]{3,2,0,1:T(8,128)(2,1)S(1)} %maximum_select_fusion.18), channel_id=1, source_target_pairs={{0,8},{1,9},{2,10},{3,11},{4,12},{5,13},{6,14},{7,15},{8,0},{9,1},... | collective-permute-start | bytes 884744 | tf_op jit(solution)/shard_map/ppermute | solution.py:685
  26.5 51.9 %copy-start.3 = (bf16[1024,768]{1,0:T(8,128)(2,1)}, bf16[1024,768]{1,0:T(8,128)(2,1)S(1)}, u32[]{:S(2)}) copy-start(bf16[1024,768]{1,0:T(8,128)(2,1)S(1)} %fusion.1.normed_ref) | copy-start | bytes 4718596
  35.6 11.4 %collective-permute-start.3 = (bf16[4,2,2,48,384]{4,3,0,2,1:T(8,128)(2,1)S(1)}, bf16[4,2,2,48,384]{4,3,0,2,1:T(8,128)(2,1)S(1)}, u32[]{:S(2)}, u32[]{:S(2)}) collective-permute-start(bf16[4,2,2,48,384]{4,3,0,2,1:T(8,128)(2,1)S(1)} %maximum_select_fusion.14), channel_id=1, source_target_pairs={{0,4},{1,3},{2,6},{3,1},{4,0},{5,7},{6,2},{7,5},{8,12},{9,11},{10,... | collective-permute-start | bytes 1769480 | tf_op jit(solution)/shard_map/ppermute | solution.py:685
  49.0 18.0 %collective-permute-start.5 = (bf16[4,2,2,2,48,384]{5,4,0,2,1,3:T(8,128)(2,1)}, bf16[4,2,2,2,48,384]{5,4,0,2,1,3:T(8,128)(2,1)}, u32[]{:S(2)}, u32[]{:S(2)}) collective-permute-start(bf16[4,2,2,2,48,384]{5,4,0,2,1,3:T(8,128)(2,1)} %maximum_select_fusion.7), channel_id=1, source_target_pairs={{0,2},{1,5},{2,0},{3,7},{4,6},{5,1},{6,4},{7,3},{8,10},{9,13},{10,... | collective-permute-start | bytes 3538952 | tf_op jit(solution)/shard_map/ppermute | solution.py:685
  73.5 4.9 %collective-permute-start.6 = (bf16[4,768,384]{2,1,0:T(8,128)(2,1)}, bf16[4,768,384]{2,1,0:T(8,128)(2,1)}, u32[]{:S(2)}, u32[]{:S(2)}) collective-permute-start(bf16[4,768,384]{2,1,0:T(8,128)(2,1)} %bitcast.26.own_ref.w_own_ref), channel_id=1, source_target_pairs={{0,1},{1,0},{2,3},{3,2},{4,5},{5,4},{6,7},{7,6},{8,9},{9,8},{10,11... | collective-permute-start | bytes 7077896 | tf_op jit(solution)/shard_map/ppermute | solution.py:678
  86.2 17.3 %copy-start.1 = (bf16[3,1024,768]{2,1,0:T(8,128)(2,1)}, bf16[3,1024,768]{2,1,0:T(8,128)(2,1)S(1)}, u32[]{:S(2)}) copy-start(bf16[3,1024,768]{2,1,0:T(8,128)(2,1)S(1)} %project.1.q_ref.k_ref.v_ref) | copy-start | bytes 14155780
  108.9 24.5 %copy-start.6 = (bf16[1024,768]{1,0:T(8,128)(2,1)}, bf16[1024,768]{1,0:T(8,128)(2,1)S(1)}, u32[]{:S(2)}) copy-start(bf16[1024,768]{1,0:T(8,128)(2,1)S(1)} %multiply_convert_fusion.normed_ref) | copy-start | bytes 4718596
  133.4 26.4 %slice-start.2 = ((s8[4718592]{0:T(1024)(128)(4,1)}), s8[4194304]{0:T(1024)(128)(4,1)S(1)}, s32[]{:S(2)}) async-start(s8[4718592]{0:T(1024)(128)(4,1)} %bitcast.142), calls=%async_computation.3 | async-start | bytes 8388608
  133.5 26.4 %slice-start.3 = ((s8[4718592]{0:T(1024)(128)(4,1)}), s8[524288]{0:T(1024)(128)(4,1)S(1)}, s32[]{:S(2)}) async-start(s8[4718592]{0:T(1024)(128)(4,1)} %bitcast.142), calls=%async_computation.4 | async-start | bytes 1048576
  133.5 26.4 %collective-permute-start.7 = (bf16[1536,768]{1,0:T(8,128)(2,1)}, bf16[1536,768]{1,0:T(8,128)(2,1)S(1)}, u32[]{:S(2)}, u32[]{:S(2)}) collective-permute-start(bf16[1536,768]{1,0:T(8,128)(2,1)} %get-tuple-element.110), channel_id=1, source_target_pairs={{0,1},{1,0},{2,3},{3,2},{4,5},{5,4},{6,7},{7,6},{8,9},{9,8},{10,11... | collective-permute-start | bytes 7077896 | tf_op jit(solution)/shard_map/ppermute | solution.py:678
  159.5 16.7 %collective-permute-start.9 = (bf16[1536,768]{1,0:T(8,128)(2,1)}, bf16[1536,768]{1,0:T(8,128)(2,1)S(1)}, u32[]{:S(2)}, u32[]{:S(2)}) collective-permute-start(bf16[1536,768]{1,0:T(8,128)(2,1)} %get-tuple-element.112), channel_id=1, source_target_pairs={{0,1},{1,0},{2,3},{3,2},{4,5},{5,4},{6,7},{7,6},{8,9},{9,8},{10,11... | collective-permute-start | bytes 7077896 | tf_op jit(solution)/shard_map/ppermute | solution.py:678
  162.4 42.1 %collective-permute-start.8 = (bf16[1,8,96,768]{3,2,1,0:T(8,128)(2,1)S(1)}, bf16[1,8,96,768]{3,2,1,0:T(8,128)(2,1)}, u32[]{:S(2)}, u32[]{:S(2)}) collective-permute-start(bf16[1,8,96,768]{3,2,1,0:T(8,128)(2,1)S(1)} %get-tuple-element.115), channel_id=1, source_target_pairs={{0,2},{1,5},{2,0},{3,7},{4,6},{5,1},{6,4},{7,3},{8,10},{9,13},{10,... | collective-permute-start | bytes 3538952 | tf_op jit(solution)/shard_map/ppermute | solution.py:685
  180.2 26.9 %collective-permute-start.10 = (bf16[1,8,96,768]{3,2,1,0:T(8,128)(2,1)}, bf16[1,8,96,768]{3,2,1,0:T(8,128)(2,1)}, u32[]{:S(2)}, u32[]{:S(2)}) collective-permute-start(bf16[1,8,96,768]{3,2,1,0:T(8,128)(2,1)} %get-tuple-element.127), channel_id=1, source_target_pairs={{0,2},{1,5},{2,0},{3,7},{4,6},{5,1},{6,4},{7,3},{8,10},{9,13},{10,... | collective-permute-start | bytes 3538952 | tf_op jit(solution)/shard_map/ppermute | solution.py:685
  218.6 12.4 %collective-permute-start.12 = (bf16[2,768,512]{2,1,0:T(8,128)(2,1)S(1)}, bf16[2,768,512]{2,1,0:T(8,128)(2,1)S(1)}, u32[]{:S(2)}, u32[]{:S(2)}) collective-permute-start(bf16[2,768,512]{2,1,0:T(8,128)(2,1)S(1)} %get-tuple-element.141), channel_id=1, source_target_pairs={{0,1},{1,0},{2,3},{3,2},{4,5},{5,4},{6,7},{7,6},{8,9},{9,8},{10,11... | collective-permute-start | bytes 4718600 | tf_op jit(solution)/shard_map/ppermute | solution.py:678
  218.7 20.6 %collective-permute-start.11 = (bf16[1,4,192,768]{3,2,1,0:T(8,128)(2,1)}, bf16[1,4,192,768]{3,2,1,0:T(8,128)(2,1)}, u32[]{:S(2)}, u32[]{:S(2)}) collective-permute-start(bf16[1,4,192,768]{3,2,1,0:T(8,128)(2,1)} %fusion.3), channel_id=1, source_target_pairs={{0,4},{1,3},{2,6},{3,1},{4,0},{5,7},{6,2},{7,5},{8,12},{9,11},{10,... | collective-permute-start | bytes 3538952 | tf_op jit(solution)/shard_map/ppermute | solution.py:685
  237.0 5.6 %collective-permute-start.15 = (bf16[2,768,256]{2,1,0:T(8,128)(2,1)}, bf16[2,768,256]{2,1,0:T(8,128)(2,1)S(1)}, u32[]{:S(2)}, u32[]{:S(2)}) collective-permute-start(bf16[2,768,256]{2,1,0:T(8,128)(2,1)} %get-tuple-element.149), channel_id=1, source_target_pairs={{0,1},{1,0},{2,3},{3,2},{4,5},{5,4},{6,7},{7,6},{8,9},{9,8},{10,11... | collective-permute-start | bytes 2359304 | tf_op jit(solution)/shard_map/ppermute | solution.py:678
  237.0 24.8 %collective-permute-start.14 = (bf16[2,8,48,512]{3,2,1,0:T(8,128)(2,1)}, bf16[2,8,48,512]{3,2,1,0:T(8,128)(2,1)}, u32[]{:S(2)}, u32[]{:S(2)}) collective-permute-start(bf16[2,8,48,512]{3,2,1,0:T(8,128)(2,1)} %get-tuple-element.146), channel_id=1, source_target_pairs={{0,2},{1,5},{2,0},{3,7},{4,6},{5,1},{6,4},{7,3},{8,10},{9,13},{10,... | collective-permute-start | bytes 2359304 | tf_op jit(solution)/shard_map/ppermute | solution.py:685
  246.6 17.3 %collective-permute-start.16 = (bf16[2,8,48,256]{3,2,1,0:T(8,128)(2,1)}, bf16[2,8,48,256]{3,2,1,0:T(8,128)(2,1)S(1)}, u32[]{:S(2)}, u32[]{:S(2)}) collective-permute-start(bf16[2,8,48,256]{3,2,1,0:T(8,128)(2,1)} %get-tuple-element.154), channel_id=1, source_target_pairs={{0,2},{1,5},{2,0},{3,7},{4,6},{5,1},{6,4},{7,3},{8,10},{9,13},{10,... | collective-permute-start | bytes 1179656 | tf_op jit(solution)/shard_map/ppermute | solution.py:685
  247.7 19.0 %collective-permute-start.13 = (bf16[1,2,192,768]{3,2,1,0:T(8,128)(2,1)}, bf16[1,2,192,768]{3,2,1,0:T(8,128)(2,1)S(1)}, u32[]{:S(2)}, u32[]{:S(2)}) collective-permute-start(bf16[1,2,192,768]{3,2,1,0:T(8,128)(2,1)} %fusion.8), channel_id=1, source_target_pairs={{0,8},{1,9},{2,10},{3,11},{4,12},{5,13},{6,14},{7,15},{8,0},{9,1},... | collective-permute-start | bytes 1769480 | tf_op jit(solution)/shard_map/ppermute | solution.py:685
  265.0 10.2 %collective-permute-start.18 = (bf16[2,4,48,768]{3,2,1,0:T(8,128)(2,1)}, bf16[2,4,48,768]{3,2,1,0:T(8,128)(2,1)}, u32[]{:S(2)}, u32[]{:S(2)}) collective-permute-start(bf16[2,4,48,768]{3,2,1,0:T(8,128)(2,1)} %fusion.9), channel_id=1, source_target_pairs={{0,4},{1,3},{2,6},{3,1},{4,0},{5,7},{6,2},{7,5},{8,12},{9,11},{10,... | collective-permute-start | bytes 1769480 | tf_op jit(solution)/shard_map/ppermute | solution.py:685
  267.7 18.2 %collective-permute-start.17 = (bf16[2,256,768]{2,1,0:T(8,128)(2,1)S(1)}, bf16[2,256,768]{2,1,0:T(8,128)(2,1)S(1)}, u32[]{:S(2)}, u32[]{:S(2)}) collective-permute-start(bf16[2,256,768]{2,1,0:T(8,128)(2,1)S(1)} %copy-done.37), channel_id=1, source_target_pairs={{0,1},{1,0},{2,3},{3,2},{4,5},{5,4},{6,7},{7,6},{8,9},{9,8},{10,11... | collective-permute-start | bytes 2359304 | tf_op jit(solution)/shard_map/ppermute | solution.py:678
  269.3 16.6 %copy-start.30 = (bf16[2,256,768]{2,1,0:T(8,128)(2,1)S(1)}, bf16[2,256,768]{2,1,0:T(8,128)(2,1)}, u32[]{:S(2)}) copy-start(bf16[2,256,768]{2,1,0:T(8,128)(2,1)} %copy-done.29) | copy-start | bytes 2359300
  278.6 13.4 %collective-permute-start.21 = (bf16[2,2,48,768]{3,2,0,1:T(8,128)(2,1)}, bf16[2,2,48,768]{3,2,0,1:T(8,128)(2,1)}, u32[]{:S(2)}, u32[]{:S(2)}) collective-permute-start(bf16[2,2,48,768]{3,2,0,1:T(8,128)(2,1)} %fusion.13), channel_id=1, source_target_pairs={{0,8},{1,9},{2,10},{3,11},{4,12},{5,13},{6,14},{7,15},{8,0},{9,1},... | collective-permute-start | bytes 884744 | tf_op jit(solution)/shard_map/ppermute | solution.py:685
  278.6 21.1 %collective-permute-start.19 = (f32[1920]{0:T(1024)}, f32[1920]{0:T(1024)S(1)}, u32[]{:S(2)}, u32[]{:S(2)}) collective-permute-start(f32[1920]{0:T(1024)} %pad_maximum_fusion.7), channel_id=1, source_target_pairs={{0,2},{1,5},{2,0},{3,7},{4,6},{5,1},{6,4},{7,3},{8,10},{9,13},{10,... | collective-permute-start | bytes 23048 | tf_op jit(solution)/shard_map/ppermute | solution.py:685
  280.1 17.4 %collective-permute-start.20 = (bf16[1,1,192,768]{3,2,1,0:T(8,128)(2,1)}, bf16[1,1,192,768]{3,2,1,0:T(8,128)(2,1)S(1)}, u32[]{:S(2)}, u32[]{:S(2)}) collective-permute-start(bf16[1,1,192,768]{3,2,1,0:T(8,128)(2,1)} %dynamic-slice_convert_fusion), channel_id=1, source_target_pairs={{0,16},{1,17},{2,18},{3,19},{4,20},{5,21},{6,22},{7,23},{8,24},{9,... | collective-permute-start | bytes 884744 | tf_op jit(solution)/shard_map/ppermute | solution.py:685
  299.8 21.3 %collective-permute-start.22 = (f32[2,256,768]{2,1,0:T(8,128)}, f32[2,256,768]{2,1,0:T(8,128)}, u32[]{:S(2)}, u32[]{:S(2)}) collective-permute-start(f32[2,256,768]{2,1,0:T(8,128)} %get-tuple-element.170), channel_id=1, source_target_pairs={{0,1},{1,0},{2,3},{3,2},{4,5},{5,4},{6,7},{7,6},{8,9},{9,8},{10,11... | collective-permute-start | bytes 4718600 | tf_op jit(solution)/shard_map/ppermute | solution.py:678
  299.8 10.4 %collective-permute-start.24 = (bf16[2,1,48,768]{3,2,0,1:T(8,128)(2,1)S(1)}, bf16[2,1,48,768]{3,2,0,1:T(8,128)(2,1)}, u32[]{:S(2)}, u32[]{:S(2)}) collective-permute-start(bf16[2,1,48,768]{3,2,0,1:T(8,128)(2,1)S(1)} %dynamic-slice_convert_fusion.3), channel_id=1, source_target_pairs={{0,16},{1,17},{2,18},{3,19},{4,20},{5,21},{6,22},{7,23},{8,24},{9,... | collective-permute-start | bytes 442376 | tf_op jit(solution)/shard_map/ppermute | solution.py:685
  299.9 12.2 %collective-permute-start.23 = (bf16[2,96,896]{2,1,0:T(8,128)(2,1)}, bf16[2,96,896]{2,1,0:T(8,128)(2,1)}, u32[]{:S(2)}, u32[]{:S(2)}) collective-permute-start(bf16[2,96,896]{2,1,0:T(8,128)(2,1)} %fusion.7), channel_id=1, source_target_pairs={{0,2},{1,5},{2,0},{3,7},{4,6},{5,1},{6,4},{7,3},{8,10},{9,13},{10,... | collective-permute-start | bytes 1032200 | tf_op jit(solution)/shard_map/ppermute | solution.py:685
  313.4 5.6 %collective-permute-start.25 = (bf16[96,896]{1,0:T(8,128)(2,1)S(1)}, bf16[96,896]{1,0:T(8,128)(2,1)S(1)}, u32[]{:S(2)}, u32[]{:S(2)}) collective-permute-start(bf16[96,896]{1,0:T(8,128)(2,1)S(1)} %fusion.14), channel_id=1, source_target_pairs={{0,4},{1,3},{2,6},{3,1},{4,0},{5,7},{6,2},{7,5},{8,12},{9,11},{10,... | collective-permute-start | bytes 516104 | tf_op jit(solution)/shard_map/ppermute | solution.py:685
  313.5 5.5 %collective-permute-start.26 = (f32[1920]{0:T(1024)S(1)}, f32[1920]{0:T(1024)S(1)}, u32[]{:S(2)}, u32[]{:S(2)}) collective-permute-start(f32[1920]{0:T(1024)S(1)} %fusion.27), channel_id=1, source_target_pairs={{0,4},{1,3},{2,6},{3,1},{4,0},{5,7},{6,2},{7,5},{8,12},{9,11},{10,... | collective-permute-start | bytes 23048 | tf_op jit(solution)/shard_map/ppermute | solution.py:685
  315.5 9.6 %collective-permute-start.27 = (bf16[2,48,768]{2,1,0:T(8,128)(2,1)S(1)}, bf16[2,48,768]{2,1,0:T(8,128)(2,1)S(1)}, u32[]{:S(2)}, u32[]{:S(2)}) collective-permute-start(bf16[2,48,768]{2,1,0:T(8,128)(2,1)S(1)} %get-tuple-element.234), channel_id=1, source_target_pairs={{0,16},{1,17},{2,18},{3,19},{4,20},{5,21},{6,22},{7,23},{8,24},{9,... | collective-permute-start | bytes 442376 | tf_op jit(solution)/shard_map/ppermute | solution.py:685
  318.9 6.2 %collective-permute-start.30 = (f32[1920]{0:T(1024)S(1)}, f32[1920]{0:T(1024)S(1)}, u32[]{:S(2)}, u32[]{:S(2)}) collective-permute-start(f32[1920]{0:T(1024)S(1)} %add.245), channel_id=1, source_target_pairs={{0,8},{1,9},{2,10},{3,11},{4,12},{5,13},{6,14},{7,15},{8,0},{9,1},... | collective-permute-start | bytes 23048 | tf_op jit(solution)/shard_map/ppermute | solution.py:685
  319.0 8.3 %collective-permute-start.29 = (bf16[96,896]{1,0:T(8,128)(2,1)S(1)}, bf16[96,896]{1,0:T(8,128)(2,1)S(1)}, u32[]{:S(2)}, u32[]{:S(2)}) collective-permute-start(bf16[96,896]{1,0:T(8,128)(2,1)S(1)} %fusion.12), channel_id=1, source_target_pairs={{0,8},{1,9},{2,10},{3,11},{4,12},{5,13},{6,14},{7,15},{8,0},{9,1},... | collective-permute-start | bytes 516104 | tf_op jit(solution)/shard_map/ppermute | solution.py:685
  325.1 14.6 %copy-start.54 = (f32[2,192,768]{2,1,0:T(8,128)S(1)}, f32[2,192,768]{2,1,0:T(8,128)}, u32[]{:S(2)}) copy-start(f32[2,192,768]{2,1,0:T(8,128)} %param.25) | copy-start | bytes 3538948
  325.1 10.0 %collective-permute-start.28 = (bf16[2,96,768]{2,1,0:T(8,128)(2,1)S(1)}, bf16[2,96,768]{2,1,0:T(8,128)(2,1)S(1)}, u32[]{:S(2)}, u32[]{:S(2)}) collective-permute-start(bf16[2,96,768]{2,1,0:T(8,128)(2,1)S(1)} %pad_maximum_fusion.5), channel_id=1, source_target_pairs={{0,8},{1,9},{2,10},{3,11},{4,12},{5,13},{6,14},{7,15},{8,0},{9,1},... | collective-permute-start | bytes 884744 | tf_op jit(solution)/shard_map/ppermute | solution.py:685
  327.3 12.3 %collective-permute-start.34 = (f32[1,192,768]{2,1,0:T(8,128)S(1)}, f32[1,192,768]{2,1,0:T(8,128)S(1)}, u32[]{:S(2)}, u32[]{:S(2)}) collective-permute-start(f32[1,192,768]{2,1,0:T(8,128)S(1)} %copy-done.56), channel_id=1, source_target_pairs={{0,1},{1,0},{2,3},{3,2},{4,5},{5,4},{6,7},{7,6},{8,9},{9,8},{10,11... | collective-permute-start | bytes 1769480 | tf_op jit(solution)/shard_map/ppermute | solution.py:678
  327.4 11.4 %collective-permute-start.32 = (bf16[96,896]{1,0:T(8,128)(2,1)S(1)}, bf16[96,896]{1,0:T(8,128)(2,1)S(1)}, u32[]{:S(2)}, u32[]{:S(2)}) collective-permute-start(bf16[96,896]{1,0:T(8,128)(2,1)S(1)} %add_convert_fusion.1), channel_id=1, source_target_pairs={{0,16},{1,17},{2,18},{3,19},{4,20},{5,21},{6,22},{7,23},{8,24},{9,... | collective-permute-start | bytes 516104 | tf_op jit(solution)/shard_map/ppermute | solution.py:685
  335.1 20.3 %collective-permute-start.31 = (bf16[2,192,768]{2,1,0:T(8,128)(2,1)S(1)}, bf16[2,192,768]{2,1,0:T(8,128)(2,1)S(1)}, u32[]{:S(2)}, u32[]{:S(2)}) collective-permute-start(bf16[2,192,768]{2,1,0:T(8,128)(2,1)S(1)} %pad_maximum_fusion.4), channel_id=1, source_target_pairs={{0,4},{1,3},{2,6},{3,1},{4,0},{5,7},{6,2},{7,5},{8,12},{9,11},{10,... | collective-permute-start | bytes 1769480 | tf_op jit(solution)/shard_map/ppermute | solution.py:685
  338.8 8.1 %collective-permute-start.33 = (bf16[96,896]{1,0:T(8,128)(2,1)S(1)}, bf16[96,896]{1,0:T(8,128)(2,1)S(1)}, u32[]{:S(2)}, u32[]{:S(2)}) collective-permute-start(bf16[96,896]{1,0:T(8,128)(2,1)S(1)} %add_convert_fusion), channel_id=1, source_target_pairs={{0,4},{1,3},{2,6},{3,1},{4,0},{5,7},{6,2},{7,5},{8,12},{9,11},{10,... | collective-permute-start | bytes 516104 | tf_op jit(solution)/shard_map/ppermute | solution.py:685
  347.0 7.3 %collective-permute-start.35 = (bf16[2,96,896]{2,1,0:T(8,128)(2,1)S(1)}, bf16[2,96,896]{2,1,0:T(8,128)(2,1)S(1)}, u32[]{:S(2)}, u32[]{:S(2)}) collective-permute-start(bf16[2,96,896]{2,1,0:T(8,128)(2,1)S(1)} %maximum_select_fusion.17), channel_id=1, source_target_pairs={{0,2},{1,5},{2,0},{3,7},{4,6},{5,1},{6,4},{7,3},{8,10},{9,13},{10,... | collective-permute-start | bytes 1032200 | tf_op jit(solution)/shard_map/ppermute | solution.py:685
  347.5 4.5 %collective-permute-start.36 = (f32[1920]{0:T(1024)S(1)}, f32[1920]{0:T(1024)S(1)}, u32[]{:S(2)}, u32[]{:S(2)}) collective-permute-start(f32[1920]{0:T(1024)S(1)} %add.247), channel_id=1, source_target_pairs={{0,16},{1,17},{2,18},{3,19},{4,20},{5,21},{6,22},{7,23},{8,24},{9,... | collective-permute-start | bytes 23048 | tf_op jit(solution)/shard_map/ppermute | solution.py:685
  356.6 16.5 %collective-permute-start.37 = (bf16[2,384,768]{2,1,0:T(8,128)(2,1)}, bf16[2,384,768]{2,1,0:T(8,128)(2,1)}, u32[]{:S(2)}, u32[]{:S(2)}) collective-permute-start(bf16[2,384,768]{2,1,0:T(8,128)(2,1)} %held.1.refs_0_), channel_id=1, source_target_pairs={{0,2},{1,5},{2,0},{3,7},{4,6},{5,1},{6,4},{7,3},{8,10},{9,13},{10,... | collective-permute-start | bytes 3538952 | tf_op jit(solution)/shard_map/ppermute | solution.py:685
  357.6 1.6 collective-permute-start.39
  358.5 1.6 collective-permute-start.38
  (75 other events, 321.2 us)
Sparse Core Ops, SparseCore 0:
  11.5 89.2 all-gather.1

commit v3 on v2

--- a/solution.py
+++ b/solution.py
@@ -702,20 +702,23 @@
         came = yield send, functools.partial(self.swap_dp, turn=0)
         return buf + came.astype(F32)
 
-    def scatter_rest(self, buf):
-        many, _, rows, width = buf.shape
+    def scatter_rest(self, parts, axis):
+        buf = None
         for turn in range(1, self.bits):
             bit = self.turn_bit(turn)
-            view = buf.reshape(many, -1, 2, rows, width)
-            cut = lambda b: lax.dynamic_index_in_dim(view, b, 2, keepdims=False)
+
+            def cut(b):
+                pieces = []
+                for v in parts:
+                    view = v.reshape((v.shape[0], -1, 2) + v.shape[2:])
+                    pieces.append(lax.dynamic_index_in_dim(view, b, 2, keepdims=False))
+                return jnp.concatenate(pieces, axis=axis) if len(pieces) > 1 else pieces[0]
+
             send, buf = cut(1 - bit).astype(BF), cut(bit)
             came = yield send, functools.partial(self.swap_dp, turn=turn)
             buf = buf + came.astype(F32)
+            parts = [buf]
         return buf
-
-    def scatter(self, value, got):
-        buf = yield from self.scatter_first(value, got)
-        return (yield from self.scatter_rest(buf))
 
     def sum_far(self, value):
         for turn in range(2, self.bits):
@@ -749,11 +752,10 @@
         shape = value.shape
         return buf.reshape(shape[:axis] + (shape[axis] * self.size,) + shape[axis + 1 :])
 
-    def gather_rows(self, buf, last):
+    def gather_rows(self, buf):
         for turn in range(self.bits - 1, 0, -1):
             came = yield buf, functools.partial(self.swap_dp, turn=turn)
             buf = jnp.concatenate([buf, came], axis=1)
-        buf = held(buf, last())
         came = yield buf, functools.partial(self.swap_dp, turn=0)
         return buf, came
 
@@ -873,7 +875,8 @@
 def muon_kernel(parts, gathered, scaling, *refs):
     sources, (mom_ref, master_ref, out_ref) = refs[:parts], refs[parts:]
     if gathered:
-        gram = sum(mm(ref[0], ref[0], TN) for ref in sources)
+        whole = jnp.concatenate([ref[0] for ref in sources], axis=0)
+        gram = mm(whole, whole, TN)
     else:
         gram = unpack_gram(sources[0][0].astype(F32))
     width = gram.shape[1]
@@ -1031,8 +1034,7 @@
         return (yield from links.scatter_first(keep.reshape(view), came.reshape(view)))
 
     def ffn_rest(first_part, second_part):
-        buf = jnp.concatenate([first_part, second_part], axis=2)
-        total = yield from links.scatter_rest(buf)
+        total = yield from links.scatter_rest([first_part, second_part], 2)
         return total.reshape(1, 2 * half, width)
 
     y_parts, dn_parts, sums = [], [], []
@@ -1089,11 +1091,10 @@
         return (yield from links.scatter_first(keep.reshape(view), came.reshape(view)))
 
     def attn_rest(first_group, second_group):
-        buf = jnp.concatenate([first_group, second_group], axis=3)
-        total = yield from links.scatter_rest(buf)
+        total = yield from links.scatter_rest([first_group, second_group], 3)
         grad = total.reshape(2, width // size, width)
         mom = muon_beta * moment_attn + grad
-        whole = yield from links.gather_rows(mom.astype(BF), lambda: gram.result)
+        whole = yield from links.gather_rows(mom.astype(BF))
         return grad, mom, whole
 
     two.step()
@@ -1129,6 +1130,7 @@
     hidden_out = links.by_core(out_own, clock.after(out_other), 0)
     clock.done(hidden_out)
     maps_sum.step()
+    units.flight = held(units.flight, maps_sum.flight)
     ffn_grad = units.finish()
     mom_ffn = muon_beta * pick(ffn_moment, 1) + ffn_grad
     gram = Chain(clock, links.sum_blocks(packed_gram(mom_ffn[0])))
@@ -1148,26 +1150,24 @@
     gram.step()
     ffn_mom = muon_beta * ffn_moment + links.by_core(ffn_grad, clock.after(ffn_other), 0)
     clock.done(ffn_mom)
+    maps_sum.step()
     gram.step()
     small.step()
-    gram.finish()
-    maps_sum.step()
     if links.bits > 4:
         maps_sum.step(2 * links.bits - 8)
     gram_ffn, small = gram.finish(), small.finish()
     gain_sum = small[: 2 * width].reshape(2, width)
     table_sum = small[2 * width :].reshape(table_grad.shape)
-    new_ffn = muon(
-        [gram_ffn[None]],
-        False,
-        clock.after(mom_ffn),
-        pick(ffn_master, 1),
-        math.sqrt(max(1.0, FF / D)),
-    )
-    clock.done(new_ffn)
     attn_grad, mom_attn, attn_whole = maps_sum.finish()
     attn_other = links.swap_seq(attn_grad)
     new_attn = muon(attn_whole, True, mom_attn, pick(attn_master, 2), 1.0)
+    new_ffn = muon(
+        [held(gram_ffn, new_attn)[None]],
+        False,
+        mom_ffn,
+        pick(ffn_master, 1),
+        math.sqrt(max(1.0, FF / D)),
+    )
     attn_mom = muon_beta * attn_moment + links.by_core(attn_grad, attn_other, 0)
     new_gains, new_gain_first, new_gain_second = adamw(gains, gain_first, gain_second, gain_sum)
     new_bias, new_bias_first, new_bias_second = adamw(

time: 401 us -> 405 us (level)
  other arithmetic: 46.3 us -> 39.6 us
  local copies, waits for them, and re-layouts: 35.9 us -> 42.1 us
    unnamed x163 -> x161, local copies, waits for them, and re-layouts: 18 us -> 25.9 us
    convert_element_type x6 -> x4, local copies, waits for them, and re-layouts: 6.38 us -> 1.05 us  [scatter_rest(): send, buf = (cut(1 - bit).astype(BF), cut(bit))]
  transfers between devices with their start and end apart: 41 -> 41, of which waited for: 18 -> 17; matrix products, arithmetic and copies ran while one was open for 15% -> 14% of each run, Pallas kernels for 31% -> 29%
where the time goes in v3:
time: 405 us; the launch traced here: 401 us
  Pallas kernels  166 us (41%)
  waiting for transfers between devices  98.8 us (24%)
  local copies, waits for them, and re-layouts  42.1 us (10%)
  other arithmetic  39.6 us (10%)
  starting transfers between devices  35.9 us (9%)
  between operations  15.6 us (4%)
    ppermute x28, waiting for transfers between devices, swap_dp(): return lax.ppermute(value, ('dp', 'seq'), pairs)  94.2 us
    pallas_call x2, Pallas kernels, ffn(): pl.pallas_call(functools.partial(ffn_kernel, len(after)), grid=(units //...  48.6 us
    ppermute x28, starting transfers between devices, swap_dp(): return lax.ppermute(value, ('dp', 'seq'), pairs)  34.4 us
    pallas_call x3, Pallas kernels, attend_back(): pl.pallas_call(functools.partial(attend_back_kernel, rows, length, 2 * TI...  33.3 us
    unnamed x161, local copies, waits for them, and re-layouts  25.9 us
    pallas_call x2, Pallas kernels, muon(): pl.pallas_call(functools.partial(muon_kernel, len(sources), gathered, sca...  19.8 us
    pallas_call x1, Pallas kernels, attend(): pl.pallas_call(functools.partial(attend_kernel, rows, length, 2 * TILE, l...  17.3 us
    pallas_call x1, Pallas kernels, entry_back(): pl.pallas_call(entry_kernel, grid_spec=pltpu.PrefetchScalarGridSpec(num_s...  10.9 us
  transfers between devices with their start and end apart: 41, of which 17 were waited for; matrix products, arithmetic and copies ran while one was open for 14% of the time, Pallas kernels for 29%

profile of v3, /device:TPU:0, one launch (start us, length us, event | category | flops | bytes accessed | tf_op | source)
XLA Modules:
  0.0 400.6 jit_solution(15259476546212810732)
XLA Ops:
  10.2 4.1 %collective-permute-start.1 = (bf16[4,48,384]{2,1,0:T(8,128)(2,1)S(1)}, bf16[4,48,384]{2,1,0:T(8,128)(2,1)S(1)}, u32[]{:S(2)}, u32[]{:S(2)}) collective-permute-start(bf16[4,48,384]{2,1,0:T(8,128)(2,1)S(1)} %dynamic-slice_convert_fusion.4), channel_id=1, source_target_pairs={{0,16},{1,17},{2,18},{3,19},{4,20},{5,21},{6,22},{7,23},{8,24},{9,... | collective-permute-start | bytes 442376 | tf_op jit(solution)/shard_map/ppermute | solution.py:685
  14.3 2.5 dynamic-slice_bitcast_fusion.5
  22.3 2.1 multiply_reduce_fusion.1
  25.6 8.5 %collective-permute-done.2 = bf16[4,2,48,384]{3,2,0,1:T(8,128)(2,1)S(1)} collective-permute-done((bf16[4,2,48,384]{3,2,0,1:T(8,128)(2,1)S(1)}, bf16[4,2,48,384]{3,2,0,1:T(8,128)(2,1)S(1)}, u32[]{:S(2)}, u32[]{:S(2)}) %collective-permute-start.2) | collective-permute-done | bytes 294944 | tf_op jit(solution)/shard_map/ppermute | solution.py:685
  36.0 1.9 maximum_select_fusion.4
  39.4 4.8 %collective-permute-done.3 = bf16[4,2,2,48,384]{4,3,0,2,1:T(8,128)(2,1)S(1)} collective-permute-done((bf16[4,2,2,48,384]{4,3,0,2,1:T(8,128)(2,1)S(1)}, bf16[4,2,2,48,384]{4,3,0,2,1:T(8,128)(2,1)S(1)}, u32[]{:S(2)}, u32[]{:S(2)}) %collective-permute-start.3) | collective-permute-done | bytes 589856 | tf_op jit(solution)/shard_map/ppermute | solution.py:685
  48.9 18.2 %collective-permute-done.5 = bf16[4,2,2,2,48,384]{5,4,0,2,1,3:T(8,128)(2,1)} collective-permute-done((bf16[4,2,2,2,48,384]{5,4,0,2,1,3:T(8,128)(2,1)}, bf16[4,2,2,2,48,384]{5,4,0,2,1,3:T(8,128)(2,1)}, u32[]{:S(2)}, u32[]{:S(2)}) %collective-permute-start.5) | collective-permute-done | bytes 1179680 | tf_op jit(solution)/shard_map/ppermute | solution.py:685
  67.1 3.6 fusion.2
  70.7 2.0 copy.132
  73.1 4.6 %collective-permute-done.6.other_ref.w_other_ref = bf16[4,768,384]{2,1,0:T(8,128)(2,1)} collective-permute-done((bf16[4,768,384]{2,1,0:T(8,128)(2,1)}, bf16[4,768,384]{2,1,0:T(8,128)(2,1)}, u32[]{:S(2)}, u32[]{:S(2)}) %collective-permute-start.6) | collective-permute-done | bytes 2359328 | tf_op jit(solution)/shard_map/ppermute | solution.py:678
  77.8 7.9 %project.1.q_ref.k_ref.v_ref = bf16[3,1024,768]{2,1,0:T(8,128)(2,1)S(1)} custom-call(s32[1]{0:T(128)} %bitcast.core_ref, bf16[1024,768]{1,0:T(8,128)(2,1)S(1)} %fusion.1.normed_ref, bf16[4,768,384]{2,1,0:T(8,128)(2,1)} %bitcast.26.own_ref.w_own_ref, bf16[4,768,384]{2,1,0:T(8,128)(2,1)} %collective-permute-done.6.other_ref.w_other_ref), custom_call_target="tpu_custom_call" | custom-call | flops 1000 | bytes 1000 | tf_op jit(solution)/shard_map/project/pallas_call | solution.py:491
  85.8 17.3 %attend.1 = (bf16[1024,768]{1,0:T(8,128)(2,1)S(1)}, f32[6,2,1024]{2,1,0:T(2,128)S(1)}) custom-call(f32[6,2,512]{2,1,0:T(2,128)S(1)} %reshape.775.trev_ref, s32[2,512,1]{2,1,0:T(8,128)S(1)} %copy.133.segk_ref, s32[2,1,512]{2,1,0:T(1,128)S(1)} %reshape.777.segq_ref, bf16[3,1024,768]{2,1,0:T(8,128)(2,1)S(1)} %project.1.q_ref.k_ref.v_ref, ...), custom_call_target="tpu_custom_call" | custom-call | flops 1000 | bytes 1000 | tf_op jit(solution)/shard_map/attend/pallas_call | solution.py:171
  108.5 24.5 %ffn.2 = (f32[1024,768]{1,0:T(8,128)}, f32[1024,768]{1,0:T(8,128)}, f32[1536,768]{1,0:T(8,128)}, bf16[1536,768]{1,0:T(8,128)(2,1)}) custom-call(s32[1]{0:T(128)} %bitcast.1.first_ref, bf16[1024,768]{1,0:T(8,128)(2,1)S(1)} %multiply_convert_fusion.normed_ref, bf16[1024,768]{1,0:T(8,128)(2,1)} %bitcast_select_fusion.cot_ref, bf16[2,16,2,96,768]{4,3,2,1,0:T(8,128)(2,1)} %bitcast.196), custom_call_target="tpu_custom_call" | custom-call | flops 1000 | bytes 1000 | tf_op jit(solution)/shard_map/ffn/pallas_call | solution.py:378
  135.0 24.1 %ffn.3 = (f32[1024,768]{1,0:T(8,128)}, f32[1024,768]{1,0:T(8,128)}, f32[1536,768]{1,0:T(8,128)}, bf16[1536,768]{1,0:T(8,128)(2,1)}) custom-call(s32[1]{0:T(128)} %bitcast.1.first_ref, bf16[1024,768]{1,0:T(8,128)(2,1)S(1)} %copy-done.10, bf16[1024,768]{1,0:T(8,128)(2,1)} %bitcast_select_fusion.cot_ref, bf16[2,16,2,96,768]{4,3,2,1,0:T(8,128)(2,1)} %bitcast.197), custom_call_target="tpu_custom_call" | custom-call | flops 1000 | bytes 1000 | tf_op jit(solution)/shard_map/ffn/pallas_call | solution.py:378
  159.5 2.3 fold.4
  163.4 10.6 %middle_back.1 = (bf16[2,256,768]{2,1,0:T(8,128)(2,1)S(1)}, bf16[2,256,768]{2,1,0:T(8,128)(2,1)S(1)}, f32[1024,768]{1,0:T(8,128)S(1)}, bf16[1024,768]{1,0:T(8,12...) custom-call(s32[1]{0:T(128)} %bitcast.core_ref, f32[1024,768]{1,0:T(8,128)} %copy-done.43, ...), custom_call_target="tpu_custom_call" | custom-call | flops 1000 | bytes 1000 | tf_op jit(solution)/shard_map/middle_back/pallas_call | solution.py:451
  178.9 1.9 collective-permute-start.10
  180.7 11.3 %attend_back.3 = (bf16[3,1024,512]{2,1,0:T(8,128)(2,1)S(1)}, f32[2,2,512]{2,1,0:T(2,128)S(1)}) custom-call(f32[6,2,512]{2,1,0:T(2,128)S(1)} %copy-done.36, s32[2,512,1]{2,1,0:T(8,128)S(1)} %copy-done.12, s32[2,1,512]{2,1,0:T(1,128)S(1)} %reshape.777.segq_ref, f32[6,2,1024]{2,1,0:T(2,128)S(1)} %copy-done.38, bf16[3,1024,768]{2,1,0:T(8,128)(2,1)} %copy-done.1, ...), custom_call_target="tpu_custom_call" | custom-call | flops 1000 | bytes 1000 | tf_op jit(solution)/shard_map/attend_back/pallas_call | solution.py:288
  192.0 11.0 %attend_back.4 = (bf16[3,1024,512]{2,1,0:T(8,128)(2,1)S(1)}, f32[2,2,512]{2,1,0:T(2,128)S(1)}) custom-call(f32[6,2,512]{2,1,0:T(2,128)S(1)} %copy-done.36, s32[2,512,1]{2,1,0:T(8,128)S(1)} %copy-done.12, s32[2,1,512]{2,1,0:T(1,128)S(1)} %reshape.777.segq_ref, f32[6,2,1024]{2,1,0:T(2,128)S(1)} %copy-done.38, ...), custom_call_target="tpu_custom_call", output_to_operand_aliasing={{0}: (8, {})} | custom-call | flops 1000 | bytes 1000 | tf_op jit(solution)/shard_map/attend_back/pallas_call | solution.py:288
  203.1 2.6 convert_add_fusion.2
  211.4 4.8 %maps_grad.2 = (f32[2,768,512]{2,1,0:T(8,128)S(1)}, bf16[2,768,512]{2,1,0:T(8,128)(2,1)}) custom-call(s32[1]{0:T(128)} %bitcast.1.first_ref, bf16[1024,768]{1,0:T(8,128)(2,1)S(1)} %copy-done.6, bf16[3,1024,512]{2,1,0:T(8,128)(2,1)S(1)} %get-tuple-element.138.grads_ref.refs_0_, f32[768,768]{1,0:T(8,128)S(1)} %copy-done.14), custom_call_target="tpu_custom_call" | custom-call | flops 1000 | bytes 1000 | tf_op jit(solution)/shard_map/maps_grad/pallas_call | solution.py:603
  217.9 2.0 collective-permute-start.11
  219.9 11.0 %attend_back.5 = (bf16[3,1024,256]{2,1,0:T(8,128)(2,1)S(1)}, f32[2,2,512]{2,1,0:T(2,128)S(1)}) custom-call(f32[6,2,512]{2,1,0:T(2,128)S(1)} %copy-done.36, s32[2,512,1]{2,1,0:T(8,128)S(1)} %copy-done.12, s32[2,1,512]{2,1,0:T(1,128)S(1)} %reshape.777.segq_ref, f32[6,2,1024]{2,1,0:T(2,128)S(1)} %copy-done.38, bf16[3,1024,768]{2,1,0:T(8,128)(2,1)} %copy-done.1, ...), custom_call_target="tpu_custom_call" | custom-call | flops 1000 | bytes 1000 | tf_op jit(solution)/shard_map/attend_back/pallas_call | solution.py:288
  232.7 1.9 copy-done.3
  234.6 2.8 fold.6
  238.8 3.1 maps_grad.3
  244.0 1.8 dynamic-slice_bitcast_fusion
  249.8 2.5 fold.7
  253.2 1.8 collective-permute-start.16
  255.0 10.9 %entry_back.1 = (f32[2,256,768]{2,1,0:T(8,128)S(1)}, f32[2,256,768]{2,1,0:T(8,128)}, f32[8,768]{1,0:T(8,128)S(1)}) custom-call(s32[1]{0:T(128)} %bitcast.core_ref, bf16[1024,768]{1,0:T(8,128)(2,1)} %bitcast.198, f32[1024,768]{1,0:T(8,128)} %copy-done.19, f32[1,768]{1,0:T(1,128)S(1)} %get-tuple-element.243.gain_ref, ...), custom_call_target="tpu_custom_call" | custom-call | flops 1000 | bytes 1000 | tf_op jit(solution)/shard_map/entry_back/pallas_call | solution.py:560
  271.8 7.0 %collective-permute-done.18 = bf16[2,4,48,768]{3,2,1,0:T(8,128)(2,1)S(1)} collective-permute-done((bf16[2,4,48,768]{3,2,1,0:T(8,128)(2,1)S(1)}, bf16[2,4,48,768]{3,2,1,0:T(8,128)(2,1)S(1)}, u32[]{:S(2)}, u32[]{:S(2)}) %collective-permute-start.18) | collective-permute-done | bytes 589856 | tf_op jit(solution)/shard_map/ppermute | solution.py:685
  279.7 3.1 collective-permute-start.20
  284.3 8.0 %collective-permute-done.21 = bf16[2,2,48,768]{3,2,0,1:T(8,128)(2,1)S(1)} collective-permute-done((bf16[2,2,48,768]{3,2,0,1:T(8,128)(2,1)S(1)}, bf16[2,2,48,768]{3,2,0,1:T(8,128)(2,1)S(1)}, u32[]{:S(2)}, u32[]{:S(2)}) %collective-permute-start.21) | collective-permute-done | bytes 294944 | tf_op jit(solution)/shard_map/ppermute | solution.py:685
  293.2 1.8 collective-permute-start.19
  295.0 6.8 %collective-permute-done.22 = bf16[2,1,48,768]{3,2,0,1:T(8,128)(2,1)S(1)} collective-permute-done((bf16[2,1,48,768]{3,2,0,1:T(8,128)(2,1)S(1)}, bf16[2,1,48,768]{3,2,0,1:T(8,128)(2,1)S(1)}, u32[]{:S(2)}, u32[]{:S(2)}) %collective-permute-start.22) | collective-permute-done | bytes 147488 | tf_op jit(solution)/shard_map/ppermute | solution.py:685
  302.5 2.0 multiply_add_fusion
  308.0 5.6 %collective-permute-done.24 = bf16[2,96,896]{2,1,0:T(8,128)(2,1)} collective-permute-done((bf16[2,96,896]{2,1,0:T(8,128)(2,1)}, bf16[2,96,896]{2,1,0:T(8,128)(2,1)}, u32[]{:S(2)}, u32[]{:S(2)}) %collective-permute-start.24) | collective-permute-done | bytes 344096 | tf_op jit(solution)/shard_map/ppermute | solution.py:685
  314.8 1.8 collective-permute-start.25
  316.9 3.5 collective-permute-done.26
  320.4 2.1 collective-permute-start.29
  322.5 4.0 maximum_select_fusion
  326.6 2.1 collective-permute-done.29
  330.0 7.2 %collective-permute-done.28 = bf16[2,96,768]{2,1,0:T(8,128)(2,1)S(1)} collective-permute-done((bf16[2,96,768]{2,1,0:T(8,128)(2,1)S(1)}, bf16[2,96,768]{2,1,0:T(8,128)(2,1)S(1)}, u32[]{:S(2)}, u32[]{:S(2)}) %collective-permute-start.28) | collective-permute-done | bytes 294944 | tf_op jit(solution)/shard_map/ppermute | solution.py:685
  337.3 1.8 collective-permute-start.31
  343.2 5.3 %collective-permute-done.31 = bf16[2,192,768]{2,1,0:T(8,128)(2,1)S(1)} collective-permute-done((bf16[2,192,768]{2,1,0:T(8,128)(2,1)S(1)}, bf16[2,192,768]{2,1,0:T(8,128)(2,1)S(1)}, u32[]{:S(2)}, u32[]{:S(2)}) %collective-permute-start.31) | collective-permute-done | bytes 589856 | tf_op jit(solution)/shard_map/ppermute | solution.py:685
  355.8 12.7 %collective-permute-done.38 = bf16[2,96,896]{2,1,0:T(8,128)(2,1)S(1)} collective-permute-done((bf16[2,96,896]{2,1,0:T(8,128)(2,1)S(1)}, bf16[2,96,896]{2,1,0:T(8,128)(2,1)S(1)}, u32[]{:S(2)}, u32[]{:S(2)}) %collective-permute-start.38) | collective-permute-done | bytes 344096 | tf_op jit(solution)/shard_map/ppermute | solution.py:685
  371.4 14.2 %muon.2.refs_1_ = f32[2,48,768]{2,1,0:T(8,128)} custom-call(bf16[2,384,768]{2,1,0:T(8,128)(2,1)S(1)} %pad_maximum_fusion.1.refs_0_, bf16[2,384,768]{2,1,0:T(8,128)(2,1)} %collective-permute-done.34.refs_1_, f32[2,48,768]{2,1,0:T(8,128)S(1)} %get-tuple-element.233.refs_2_, f32[2,48,768]{2,1,0:T(8,128)S(1)} %copy-done.30), custom_call_target="tpu_custom_call" | custom-call | flops 1000 | bytes 1000 | tf_op jit(solution)/shard_map/muon/pallas_call | solution.py:925
  387.9 5.6 %muon.3 = f32[1,192,768]{2,1,0:T(8,128)} custom-call(bf16[1,384,896]{2,1,0:T(8,128)(2,1)S(1)} %bitcast.194, f32[1,192,768]{2,1,0:T(8,128)S(1)} %get-tuple-element.235.refs_1_, f32[1,192,768]{2,1,0:T(8,128)S(1)} %copy-done.20), custom_call_target="tpu_custom_call" | custom-call | flops 1000 | bytes 1000 | tf_op jit(solution)/shard_map/muon/pallas_call | solution.py:925
  (322 shorter events, 81.9 us)
Async XLA Ops:
  7.2 101.3 %all-gather.2.cloned.1.call-start = ((), (), s32[]{:S(2)}) async-start(), calls=%async_computation | async-start | bytes 9732096 | tf_op jit(solution)/shard_map/all_gather | solution.py:970
  10.2 11.1 %collective-permute-start.1 = (bf16[4,48,384]{2,1,0:T(8,128)(2,1)S(1)}, bf16[4,48,384]{2,1,0:T(8,128)(2,1)S(1)}, u32[]{:S(2)}, u32[]{:S(2)}) collective-permute-start(bf16[4,48,384]{2,1,0:T(8,128)(2,1)S(1)} %dynamic-slice_convert_fusion.4), channel_id=1, source_target_pairs={{0,16},{1,17},{2,18},{3,19},{4,20},{5,21},{6,22},{7,23},{8,24},{9,... | collective-permute-start | bytes 442376 | tf_op jit(solution)/shard_map/ppermute | solution.py:685
  16.8 5.5 %collective-permute-start = (bf16[2,256,768]{2,1,0:T(8,128)(2,1)}, bf16[2,256,768]{2,1,0:T(8,128)(2,1)}, u32[]{:S(2)}, u32[]{:S(2)}) collective-permute-start(bf16[2,256,768]{2,1,0:T(8,128)(2,1)} %get-tuple-element.241), channel_id=1, source_target_pairs={{0,1},{1,0},{2,3},{3,2},{4,5},{5,4},{6,7},{7,6},{8,9},{9,8},{10,11... | collective-permute-start | bytes 2359304 | tf_op jit(solution)/shard_map/ppermute | solution.py:678
  18.1 17.8 %collective-permute-start.4 = (bf16[2,256,768]{2,1,0:T(8,128)(2,1)}, bf16[2,256,768]{2,1,0:T(8,128)(2,1)}, u32[]{:S(2)}, u32[]{:S(2)}) collective-permute-start(bf16[2,256,768]{2,1,0:T(8,128)(2,1)} %get-tuple-element.240), channel_id=1, source_target_pairs={{0,1},{1,0},{2,3},{3,2},{4,5},{5,4},{6,7},{7,6},{8,9},{9,8},{10,11... | collective-permute-start | bytes 2359304 | tf_op jit(solution)/shard_map/ppermute | solution.py:678
  19.7 66.1 %copy-start.35 = (f32[6,2,512]{2,1,0:T(2,128)}, f32[6,2,512]{2,1,0:T(2,128)S(1)}, u32[]{:S(2)}) copy-start(f32[6,2,512]{2,1,0:T(2,128)S(1)} %reshape.775.trev_ref) | copy-start | bytes 73732
  21.4 12.8 %collective-permute-start.2 = (bf16[4,2,48,384]{3,2,0,1:T(8,128)(2,1)S(1)}, bf16[4,2,48,384]{3,2,0,1:T(8,128)(2,1)S(1)}, u32[]{:S(2)}, u32[]{:S(2)}) collective-permute-start(bf16[4,2,48,384]{3,2,0,1:T(8,128)(2,1)S(1)} %maximum_select_fusion.18), channel_id=1, source_target_pairs={{0,8},{1,9},{2,10},{3,11},{4,12},{5,13},{6,14},{7,15},{8,0},{9,1},... | collective-permute-start | bytes 884744 | tf_op jit(solution)/shard_map/ppermute | solution.py:685
  25.6 52.1 %copy-start.5 = (bf16[1024,768]{1,0:T(8,128)(2,1)}, bf16[1024,768]{1,0:T(8,128)(2,1)S(1)}, u32[]{:S(2)}) copy-start(bf16[1024,768]{1,0:T(8,128)(2,1)S(1)} %fusion.1.normed_ref) | copy-start | bytes 4718596
  34.3 9.9 %collective-permute-start.3 = (bf16[4,2,2,48,384]{4,3,0,2,1:T(8,128)(2,1)S(1)}, bf16[4,2,2,48,384]{4,3,0,2,1:T(8,128)(2,1)S(1)}, u32[]{:S(2)}, u32[]{:S(2)}) collective-permute-start(bf16[4,2,2,48,384]{4,3,0,2,1:T(8,128)(2,1)S(1)} %maximum_select_fusion.14), channel_id=1, source_target_pairs={{0,4},{1,3},{2,6},{3,1},{4,0},{5,7},{6,2},{7,5},{8,12},{9,11},{10,... | collective-permute-start | bytes 1769480 | tf_op jit(solution)/shard_map/ppermute | solution.py:685
  45.5 21.6 %collective-permute-start.5 = (bf16[4,2,2,2,48,384]{5,4,0,2,1,3:T(8,128)(2,1)}, bf16[4,2,2,2,48,384]{5,4,0,2,1,3:T(8,128)(2,1)}, u32[]{:S(2)}, u32[]{:S(2)}) collective-permute-start(bf16[4,2,2,2,48,384]{5,4,0,2,1,3:T(8,128)(2,1)} %maximum_select_fusion.7), channel_id=1, source_target_pairs={{0,2},{1,5},{2,0},{3,7},{4,6},{5,1},{6,4},{7,3},{8,10},{9,13},{10,... | collective-permute-start | bytes 3538952 | tf_op jit(solution)/shard_map/ppermute | solution.py:685
  72.9 4.9 %collective-permute-start.6 = (bf16[4,768,384]{2,1,0:T(8,128)(2,1)}, bf16[4,768,384]{2,1,0:T(8,128)(2,1)}, u32[]{:S(2)}, u32[]{:S(2)}) collective-permute-start(bf16[4,768,384]{2,1,0:T(8,128)(2,1)} %bitcast.26.own_ref.w_own_ref), channel_id=1, source_target_pairs={{0,1},{1,0},{2,3},{3,2},{4,5},{5,4},{6,7},{7,6},{8,9},{9,8},{10,11... | collective-permute-start | bytes 7077896 | tf_op jit(solution)/shard_map/ppermute | solution.py:678
  85.7 17.4 %copy-start.1 = (bf16[3,1024,768]{2,1,0:T(8,128)(2,1)}, bf16[3,1024,768]{2,1,0:T(8,128)(2,1)S(1)}, u32[]{:S(2)}) copy-start(bf16[3,1024,768]{2,1,0:T(8,128)(2,1)S(1)} %project.1.q_ref.k_ref.v_ref) | copy-start | bytes 14155780
  108.5 24.5 %copy-start.9 = (bf16[1024,768]{1,0:T(8,128)(2,1)}, bf16[1024,768]{1,0:T(8,128)(2,1)S(1)}, u32[]{:S(2)}) copy-start(bf16[1024,768]{1,0:T(8,128)(2,1)S(1)} %multiply_convert_fusion.normed_ref) | copy-start | bytes 4718596
  133.0 26.4 %slice-start.2 = ((s8[4718592]{0:T(1024)(128)(4,1)}), s8[4194304]{0:T(1024)(128)(4,1)S(1)}, s32[]{:S(2)}) async-start(s8[4718592]{0:T(1024)(128)(4,1)} %bitcast.161), calls=%async_computation.3 | async-start | bytes 8388608
  133.0 26.4 %slice-start.3 = ((s8[4718592]{0:T(1024)(128)(4,1)}), s8[524288]{0:T(1024)(128)(4,1)S(1)}, s32[]{:S(2)}) async-start(s8[4718592]{0:T(1024)(128)(4,1)} %bitcast.161), calls=%async_computation.4 | async-start | bytes 1048576
  133.0 26.4 %collective-permute-start.7 = (bf16[1536,768]{1,0:T(8,128)(2,1)}, bf16[1536,768]{1,0:T(8,128)(2,1)S(1)}, u32[]{:S(2)}, u32[]{:S(2)}) collective-permute-start(bf16[1536,768]{1,0:T(8,128)(2,1)} %get-tuple-element.109), channel_id=1, source_target_pairs={{0,1},{1,0},{2,3},{3,2},{4,5},{5,4},{6,7},{7,6},{8,9},{9,8},{10,11... | collective-permute-start | bytes 7077896 | tf_op jit(solution)/shard_map/ppermute | solution.py:678
  159.1 14.9 %collective-permute-start.9 = (bf16[1536,768]{1,0:T(8,128)(2,1)}, bf16[1536,768]{1,0:T(8,128)(2,1)S(1)}, u32[]{:S(2)}, u32[]{:S(2)}) collective-permute-start(bf16[1536,768]{1,0:T(8,128)(2,1)} %get-tuple-element.111), channel_id=1, source_target_pairs={{0,1},{1,0},{2,3},{3,2},{4,5},{5,4},{6,7},{7,6},{8,9},{9,8},{10,11... | collective-permute-start | bytes 7077896 | tf_op jit(solution)/shard_map/ppermute | solution.py:678
  163.2 39.8 %collective-permute-start.8 = (bf16[1,8,96,768]{3,2,1,0:T(8,128)(2,1)}, bf16[1,8,96,768]{3,2,1,0:T(8,128)(2,1)}, u32[]{:S(2)}, u32[]{:S(2)}) collective-permute-start(bf16[1,8,96,768]{3,2,1,0:T(8,128)(2,1)} %get-tuple-element.114), channel_id=1, source_target_pairs={{0,2},{1,5},{2,0},{3,7},{4,6},{5,1},{6,4},{7,3},{8,10},{9,13},{10,... | collective-permute-start | bytes 3538952 | tf_op jit(solution)/shard_map/ppermute | solution.py:685
  178.9 26.8 %collective-permute-start.10 = (bf16[1,8,96,768]{3,2,1,0:T(8,128)(2,1)S(1)}, bf16[1,8,96,768]{3,2,1,0:T(8,128)(2,1)}, u32[]{:S(2)}, u32[]{:S(2)}) collective-permute-start(bf16[1,8,96,768]{3,2,1,0:T(8,128)(2,1)S(1)} %get-tuple-element.126), channel_id=1, source_target_pairs={{0,2},{1,5},{2,0},{3,7},{4,6},{5,1},{6,4},{7,3},{8,10},{9,13},{10,... | collective-permute-start | bytes 3538952 | tf_op jit(solution)/shard_map/ppermute | solution.py:685
  217.9 14.9 %collective-permute-start.12 = (bf16[2,768,512]{2,1,0:T(8,128)(2,1)}, bf16[2,768,512]{2,1,0:T(8,128)(2,1)S(1)}, u32[]{:S(2)}, u32[]{:S(2)}) collective-permute-start(bf16[2,768,512]{2,1,0:T(8,128)(2,1)} %get-tuple-element.140), channel_id=1, source_target_pairs={{0,1},{1,0},{2,3},{3,2},{4,5},{5,4},{6,7},{7,6},{8,9},{9,8},{10,11... | collective-permute-start | bytes 4718600 | tf_op jit(solution)/shard_map/ppermute | solution.py:678
  217.9 28.0 %collective-permute-start.11 = (bf16[1,4,192,768]{3,2,1,0:T(8,128)(2,1)}, bf16[1,4,192,768]{3,2,1,0:T(8,128)(2,1)}, u32[]{:S(2)}, u32[]{:S(2)}) collective-permute-start(bf16[1,4,192,768]{3,2,1,0:T(8,128)(2,1)} %pad_maximum_fusion), channel_id=1, source_target_pairs={{0,4},{1,3},{2,6},{3,1},{4,0},{5,7},{6,2},{7,5},{8,12},{9,11},{10,... | collective-permute-start | bytes 3538952 | tf_op jit(solution)/shard_map/ppermute | solution.py:685
  238.6 28.5 %collective-permute-start.14 = (bf16[2,8,48,512]{3,2,1,0:T(8,128)(2,1)}, bf16[2,8,48,512]{3,2,1,0:T(8,128)(2,1)}, u32[]{:S(2)}, u32[]{:S(2)}) collective-permute-start(bf16[2,8,48,512]{3,2,1,0:T(8,128)(2,1)} %get-tuple-element.145), channel_id=1, source_target_pairs={{0,2},{1,5},{2,0},{3,7},{4,6},{5,1},{6,4},{7,3},{8,10},{9,13},{10,... | collective-permute-start | bytes 2359304 | tf_op jit(solution)/shard_map/ppermute | solution.py:685
  242.0 7.9 %collective-permute-start.15 = (bf16[2,768,256]{2,1,0:T(8,128)(2,1)}, bf16[2,768,256]{2,1,0:T(8,128)(2,1)S(1)}, u32[]{:S(2)}, u32[]{:S(2)}) collective-permute-start(bf16[2,768,256]{2,1,0:T(8,128)(2,1)} %get-tuple-element.148), channel_id=1, source_target_pairs={{0,1},{1,0},{2,3},{3,2},{4,5},{5,4},{6,7},{7,6},{8,9},{9,8},{10,11... | collective-permute-start | bytes 2359304 | tf_op jit(solution)/shard_map/ppermute | solution.py:678
  248.3 21.2 %collective-permute-start.13 = (bf16[1,2,192,768]{3,2,1,0:T(8,128)(2,1)}, bf16[1,2,192,768]{3,2,1,0:T(8,128)(2,1)}, u32[]{:S(2)}, u32[]{:S(2)}) collective-permute-start(bf16[1,2,192,768]{3,2,1,0:T(8,128)(2,1)} %fusion.9), channel_id=1, source_target_pairs={{0,8},{1,9},{2,10},{3,11},{4,12},{5,13},{6,14},{7,15},{8,0},{9,1},... | collective-permute-start | bytes 1769480 | tf_op jit(solution)/shard_map/ppermute | solution.py:685
  253.2 15.5 %collective-permute-start.16 = (bf16[2,8,48,256]{3,2,1,0:T(8,128)(2,1)}, bf16[2,8,48,256]{3,2,1,0:T(8,128)(2,1)S(1)}, u32[]{:S(2)}, u32[]{:S(2)}) collective-permute-start(bf16[2,8,48,256]{3,2,1,0:T(8,128)(2,1)} %get-tuple-element.153), channel_id=1, source_target_pairs={{0,2},{1,5},{2,0},{3,7},{4,6},{5,1},{6,4},{7,3},{8,10},{9,13},{10,... | collective-permute-start | bytes 1179656 | tf_op jit(solution)/shard_map/ppermute | solution.py:685
  268.9 9.9 %collective-permute-start.18 = (bf16[2,4,48,768]{3,2,1,0:T(8,128)(2,1)S(1)}, bf16[2,4,48,768]{3,2,1,0:T(8,128)(2,1)S(1)}, u32[]{:S(2)}, u32[]{:S(2)}) collective-permute-start(bf16[2,4,48,768]{3,2,1,0:T(8,128)(2,1)S(1)} %pad_maximum_fusion.3), channel_id=1, source_target_pairs={{0,4},{1,3},{2,6},{3,1},{4,0},{5,7},{6,2},{7,5},{8,12},{9,11},{10,... | collective-permute-start | bytes 1769480 | tf_op jit(solution)/shard_map/ppermute | solution.py:685
  271.6 11.3 %collective-permute-start.17 = (bf16[2,256,768]{2,1,0:T(8,128)(2,1)S(1)}, bf16[2,256,768]{2,1,0:T(8,128)(2,1)S(1)}, u32[]{:S(2)}, u32[]{:S(2)}) collective-permute-start(bf16[2,256,768]{2,1,0:T(8,128)(2,1)S(1)} %copy-done.40), channel_id=1, source_target_pairs={{0,1},{1,0},{2,3},{3,2},{4,5},{5,4},{6,7},{7,6},{8,9},{9,8},{10,11... | collective-permute-start | bytes 2359304 | tf_op jit(solution)/shard_map/ppermute | solution.py:678
  279.0 13.2 %collective-permute-start.21 = (bf16[2,2,48,768]{3,2,0,1:T(8,128)(2,1)S(1)}, bf16[2,2,48,768]{3,2,0,1:T(8,128)(2,1)S(1)}, u32[]{:S(2)}, u32[]{:S(2)}) collective-permute-start(bf16[2,2,48,768]{3,2,0,1:T(8,128)(2,1)S(1)} %fusion.14), channel_id=1, source_target_pairs={{0,8},{1,9},{2,10},{3,11},{4,12},{5,13},{6,14},{7,15},{8,0},{9,1},... | collective-permute-start | bytes 884744 | tf_op jit(solution)/shard_map/ppermute | solution.py:685
  279.7 15.3 %collective-permute-start.20 = (bf16[1,1,192,768]{3,2,1,0:T(8,128)(2,1)S(1)}, bf16[1,1,192,768]{3,2,1,0:T(8,128)(2,1)S(1)}, u32[]{:S(2)}, u32[]{:S(2)}) collective-permute-start(bf16[1,1,192,768]{3,2,1,0:T(8,128)(2,1)S(1)} %dynamic-slice_convert_fusion), channel_id=1, source_target_pairs={{0,16},{1,17},{2,18},{3,19},{4,20},{5,21},{6,22},{7,23},{8,24},{9,... | collective-permute-start | bytes 884744 | tf_op jit(solution)/shard_map/ppermute | solution.py:685
  293.1 8.7 %collective-permute-start.22 = (bf16[2,1,48,768]{3,2,0,1:T(8,128)(2,1)S(1)}, bf16[2,1,48,768]{3,2,0,1:T(8,128)(2,1)S(1)}, u32[]{:S(2)}, u32[]{:S(2)}) collective-permute-start(bf16[2,1,48,768]{3,2,0,1:T(8,128)(2,1)S(1)} %dynamic-slice_convert_fusion.3), channel_id=1, source_target_pairs={{0,16},{1,17},{2,18},{3,19},{4,20},{5,21},{6,22},{7,23},{8,24},{9,... | collective-permute-start | bytes 442376 | tf_op jit(solution)/shard_map/ppermute | solution.py:685
  293.2 12.7 %collective-permute-start.19 = (f32[1920]{0:T(1024)S(1)}, f32[1920]{0:T(1024)S(1)}, u32[]{:S(2)}, u32[]{:S(2)}) collective-permute-start(f32[1920]{0:T(1024)S(1)} %pad_maximum_fusion.7), channel_id=1, source_target_pairs={{0,2},{1,5},{2,0},{3,7},{4,6},{5,1},{6,4},{7,3},{8,10},{9,13},{10,... | collective-permute-start | bytes 23048 | tf_op jit(solution)/shard_map/ppermute | solution.py:685
  305.9 16.6 %collective-permute-start.23 = (f32[2,256,768]{2,1,0:T(8,128)}, f32[2,256,768]{2,1,0:T(8,128)}, u32[]{:S(2)}, u32[]{:S(2)}) collective-permute-start(f32[2,256,768]{2,1,0:T(8,128)} %get-tuple-element.169), channel_id=1, source_target_pairs={{0,1},{1,0},{2,3},{3,2},{4,5},{5,4},{6,7},{7,6},{8,9},{9,8},{10,11... | collective-permute-start | bytes 4718600 | tf_op jit(solution)/shard_map/ppermute | solution.py:678
  306.0 7.6 %collective-permute-start.24 = (bf16[2,96,896]{2,1,0:T(8,128)(2,1)}, bf16[2,96,896]{2,1,0:T(8,128)(2,1)}, u32[]{:S(2)}, u32[]{:S(2)}) collective-permute-start(bf16[2,96,896]{2,1,0:T(8,128)(2,1)} %fusion.6), channel_id=1, source_target_pairs={{0,2},{1,5},{2,0},{3,7},{4,6},{5,1},{6,4},{7,3},{8,10},{9,13},{10,... | collective-permute-start | bytes 1032200 | tf_op jit(solution)/shard_map/ppermute | solution.py:685
  314.8 5.6 %collective-permute-start.25 = (bf16[96,896]{1,0:T(8,128)(2,1)S(1)}, bf16[96,896]{1,0:T(8,128)(2,1)S(1)}, u32[]{:S(2)}, u32[]{:S(2)}) collective-permute-start(bf16[96,896]{1,0:T(8,128)(2,1)S(1)} %fusion.16), channel_id=1, source_target_pairs={{0,4},{1,3},{2,6},{3,1},{4,0},{5,7},{6,2},{7,5},{8,12},{9,11},{10,... | collective-permute-start | bytes 516104 | tf_op jit(solution)/shard_map/ppermute | solution.py:685
  316.6 3.8 collective-permute-start.26
  316.9 9.6 %collective-permute-start.27 = (bf16[2,48,768]{2,1,0:T(8,128)(2,1)S(1)}, bf16[2,48,768]{2,1,0:T(8,128)(2,1)S(1)}, u32[]{:S(2)}, u32[]{:S(2)}) collective-permute-start(bf16[2,48,768]{2,1,0:T(8,128)(2,1)S(1)} %get-tuple-element.232), channel_id=1, source_target_pairs={{0,16},{1,17},{2,18},{3,19},{4,20},{5,21},{6,22},{7,23},{8,24},{9,... | collective-permute-start | bytes 442376 | tf_op jit(solution)/shard_map/ppermute | solution.py:685
  320.4 6.2 %collective-permute-start.30 = (f32[1920]{0:T(1024)S(1)}, f32[1920]{0:T(1024)S(1)}, u32[]{:S(2)}, u32[]{:S(2)}) collective-permute-start(f32[1920]{0:T(1024)S(1)} %add.250), channel_id=1, source_target_pairs={{0,8},{1,9},{2,10},{3,11},{4,12},{5,13},{6,14},{7,15},{8,0},{9,1},... | collective-permute-start | bytes 23048 | tf_op jit(solution)/shard_map/ppermute | solution.py:685
  320.4 8.3 %collective-permute-start.29 = (bf16[96,896]{1,0:T(8,128)(2,1)S(1)}, bf16[96,896]{1,0:T(8,128)(2,1)S(1)}, u32[]{:S(2)}, u32[]{:S(2)}) collective-permute-start(bf16[96,896]{1,0:T(8,128)(2,1)S(1)} %fusion.13), channel_id=1, source_target_pairs={{0,8},{1,9},{2,10},{3,11},{4,12},{5,13},{6,14},{7,15},{8,0},{9,1},... | collective-permute-start | bytes 516104 | tf_op jit(solution)/shard_map/ppermute | solution.py:685
  326.5 15.4 %copy-start.52 = (f32[2,192,768]{2,1,0:T(8,128)S(1)}, f32[2,192,768]{2,1,0:T(8,128)}, u32[]{:S(2)}) copy-start(f32[2,192,768]{2,1,0:T(8,128)} %param.25) | copy-start | bytes 3538948
  326.5 10.7 %collective-permute-start.28 = (bf16[2,96,768]{2,1,0:T(8,128)(2,1)S(1)}, bf16[2,96,768]{2,1,0:T(8,128)(2,1)S(1)}, u32[]{:S(2)}, u32[]{:S(2)}) collective-permute-start(bf16[2,96,768]{2,1,0:T(8,128)(2,1)S(1)} %pad_maximum_fusion.5), channel_id=1, source_target_pairs={{0,8},{1,9},{2,10},{3,11},{4,12},{5,13},{6,14},{7,15},{8,0},{9,1},... | collective-permute-start | bytes 884744 | tf_op jit(solution)/shard_map/ppermute | solution.py:685
  328.8 13.1 %collective-permute-start.32 = (f32[1,192,768]{2,1,0:T(8,128)S(1)}, f32[1,192,768]{2,1,0:T(8,128)S(1)}, u32[]{:S(2)}, u32[]{:S(2)}) collective-permute-start(f32[1,192,768]{2,1,0:T(8,128)S(1)} %copy-done.54), channel_id=1, source_target_pairs={{0,1},{1,0},{2,3},{3,2},{4,5},{5,4},{6,7},{7,6},{8,9},{9,8},{10,11... | collective-permute-start | bytes 1769480 | tf_op jit(solution)/shard_map/ppermute | solution.py:678
  328.9 11.2 %collective-permute-start.33 = (bf16[96,896]{1,0:T(8,128)(2,1)S(1)}, bf16[96,896]{1,0:T(8,128)(2,1)S(1)}, u32[]{:S(2)}, u32[]{:S(2)}) collective-permute-start(bf16[96,896]{1,0:T(8,128)(2,1)S(1)} %add_convert_fusion.1), channel_id=1, source_target_pairs={{0,16},{1,17},{2,18},{3,19},{4,20},{5,21},{6,22},{7,23},{8,24},{9,... | collective-permute-start | bytes 516104 | tf_op jit(solution)/shard_map/ppermute | solution.py:685
  337.3 11.2 %collective-permute-start.31 = (bf16[2,192,768]{2,1,0:T(8,128)(2,1)S(1)}, bf16[2,192,768]{2,1,0:T(8,128)(2,1)S(1)}, u32[]{:S(2)}, u32[]{:S(2)}) collective-permute-start(bf16[2,192,768]{2,1,0:T(8,128)(2,1)S(1)} %pad_maximum_fusion.4), channel_id=1, source_target_pairs={{0,4},{1,3},{2,6},{3,1},{4,0},{5,7},{6,2},{7,5},{8,12},{9,11},{10,... | collective-permute-start | bytes 1769480 | tf_op jit(solution)/shard_map/ppermute | solution.py:685
  339.0 14.2 %collective-permute-start.39 = (f32[2,48,768]{2,1,0:T(8,128)S(1)}, f32[2,48,768]{2,1,0:T(8,128)S(1)}, u32[]{:S(2)}, u32[]{:S(2)}) collective-permute-start(f32[2,48,768]{2,1,0:T(8,128)S(1)} %get-tuple-element.234), channel_id=1, source_target_pairs={{0,1},{1,0},{2,3},{3,2},{4,5},{5,4},{6,7},{7,6},{8,9},{9,8},{10,11... | collective-permute-start | bytes 884744 | tf_op jit(solution)/shard_map/ppermute | solution.py:678
  340.1 12.0 %collective-permute-start.36 = (bf16[96,896]{1,0:T(8,128)(2,1)S(1)}, bf16[96,896]{1,0:T(8,128)(2,1)S(1)}, u32[]{:S(2)}, u32[]{:S(2)}) collective-permute-start(bf16[96,896]{1,0:T(8,128)(2,1)S(1)} %add_convert_fusion), channel_id=1, source_target_pairs={{0,4},{1,3},{2,6},{3,1},{4,0},{5,7},{6,2},{7,5},{8,12},{9,11},{10,... | collective-permute-start | bytes 516104 | tf_op jit(solution)/shard_map/ppermute | solution.py:685
  348.6 21.9 %collective-permute-start.34 = (bf16[2,384,768]{2,1,0:T(8,128)(2,1)S(1)}, bf16[2,384,768]{2,1,0:T(8,128)(2,1)}, u32[]{:S(2)}, u32[]{:S(2)}) collective-permute-start(bf16[2,384,768]{2,1,0:T(8,128)(2,1)S(1)} %pad_maximum_fusion.1.refs_0_), channel_id=1, source_target_pairs={{0,2},{1,5},{2,0},{3,7},{4,6},{5,1},{6,4},{7,3},{8,10},{9,13},{10,... | collective-permute-start | bytes 3538952 | tf_op jit(solution)/shard_map/ppermute | solution.py:685
  351.1 4.5 %collective-permute-start.35 = (f32[1920]{0:T(1024)S(1)}, f32[1920]{0:T(1024)S(1)}, u32[]{:S(2)}, u32[]{:S(2)}) collective-permute-start(f32[1920]{0:T(1024)S(1)} %add.252), channel_id=1, source_target_pairs={{0,16},{1,17},{2,18},{3,19},{4,20},{5,21},{6,22},{7,23},{8,24},{9,... | collective-permute-start | bytes 23048 | tf_op jit(solution)/shard_map/ppermute | solution.py:685
  352.2 16.3 %collective-permute-start.38 = (bf16[2,96,896]{2,1,0:T(8,128)(2,1)S(1)}, bf16[2,96,896]{2,1,0:T(8,128)(2,1)S(1)}, u32[]{:S(2)}, u32[]{:S(2)}) collective-permute-start(bf16[2,96,896]{2,1,0:T(8,128)(2,1)S(1)} %maximum_select_fusion.16), channel_id=1, source_target_pairs={{0,2},{1,5},{2,0},{3,7},{4,6},{5,1},{6,4},{7,3},{8,10},{9,13},{10,... | collective-permute-start | bytes 1032200 | tf_op jit(solution)/shard_map/ppermute | solution.py:685
  355.6 14.0 %collective-permute-start.37 = (f32[1920]{0:T(1024)S(1)}, f32[1920]{0:T(1024)S(1)}, u32[]{:S(2)}, u32[]{:S(2)}) collective-permute-start(f32[1920]{0:T(1024)S(1)} %add.256), channel_id=1, source_target_pairs={{0,1},{1,0},{2,3},{3,2},{4,5},{5,4},{6,7},{7,6},{8,9},{9,8},{10,11... | collective-permute-start | bytes 23048 | tf_op jit(solution)/shard_map/ppermute | solution.py:678
  (74 other events, 351.1 us)
Sparse Core Ops, SparseCore 0:
  11.5 88.5 all-gather.1
